TPU v7x, 128 devices: a whole 4x4x4 slice. The times are simulated.
128 devices in a mesh: section: 8 (over x, core), tp: 16 (over z, y).
Axes of the slice: x: 4, y: 4, z: 4, core: 2. Of those that a mesh axis runs over, the one named last changes fastest.
Arguments:
- x_in: bfloat16 [256, 6144], P(None, 'tp'), may hold values from -6 to 6
- cotangent: bfloat16 [256, 6144], P(None, 'tp'), may hold values from -6 to 6
- weights: bfloat16 [8, 6144, 6144], P('section', None, 'tp'), may hold values from -0.0390625 to 0.0390625
- down_weight_store: bfloat16 [8, 8, 6144, 128], P('section', None, 'tp'), may hold values from -0.078125 to 0.078125
- lib_b: bfloat16 [8, 8, 128, 6144], P('section', None, None, 'tp'), may hold values from -0.5 to 0.5
- style_ids: int32 [2, 4], replicated, may hold values from 0 to 7
- slot_of: int32 [8], replicated, may hold values from 0 to 7, each once
Outputs:
- grad_a: bfloat16 [8, 8, 6144, 128], P(None, 'section', 'tp')
- grad_b: bfloat16 [8, 8, 128, 6144], P(None, 'section', None, 'tp')
Inputs may be any that keep to these rules, and one draw needn't show every extreme that they name: Each slot once; style k's adapters are stored at slot slot_of[k].
All inputs are finite; a program needn't handle non-finite values.
Results may differ from a plain program's by a relative error of at most 0.035.
Values may be sent and summed in bfloat16 or wider, within the bound.
No kernel may reach another device: no remote copies, remote signals or barrier semaphores. Data moves between devices by JAX's collectives and lax.ppermute only.
A program may use at most 64 MiB of HBM per device.

v0:
```python
import jax
import jax.numpy as jnp
from jax import lax
from jax.sharding import PartitionSpec as P

ADAPTER_SCALE = 0.25


def passed_along(value, axis, steps):
    count = lax.axis_size(axis)
    leading, last = (max(0, -steps), min(count, count - steps))
    return lax.ppermute(value, axis, [(source, source + steps) for source in range(leading, last)])


def storage_position(buffer, value, microbatch_slot, active_mask):
    previous = lax.dynamic_index_in_dim(buffer, microbatch_slot, 0, keepdims=False)
    chosen = jnp.where(active_mask, value, previous)
    return lax.dynamic_update_index_in_dim(buffer, chosen, microbatch_slot, 0)


def body(x_in, cotangent, weights, down_weight_store, lib_b, style_ids, slot_of):
    segment_count = lax.axis_size("section")
    number_groups = lax.axis_size("tp")
    segment_pos = lax.axis_index("section")
    feature_columns = weights.shape[2]
    adapter_rank = down_weight_store.shape[3]
    number_microbatches = style_ids.shape[0]
    number_blocks = style_ids.shape[1]
    token_rows = x_in.shape[0] // number_microbatches
    rows_per_block = token_rows // number_blocks
    style_count = slot_of.shape[0]
    tick_count = number_microbatches + segment_count - 1
    fetched_a, fetched_b = (
        lax.all_to_all(down_weight_store, "section", split_axis=1, concat_axis=0, tiled=True),
        lax.all_to_all(lib_b, "section", split_axis=1, concat_axis=0, tiled=True),
    )
    fetched_a = fetched_a[:, 0]
    fetched_b = fetched_b[:, 0]
    flat_ids = style_ids.reshape(-1)
    style_axis = jnp.arange(style_count, dtype=jnp.int32)
    slot_ids = jnp.sum(
        jnp.where(flat_ids[:, None] == style_axis[None, :], slot_of[None, :], 0), axis=1
    )
    pick_rows = (slot_ids[:, None] == style_axis[None, :]).astype(jnp.bfloat16)
    selected_down_weight = jnp.einsum(
        "ns,sir->nir", pick_rows, fetched_a, preferred_element_type=jnp.float32
    )
    selected_down_weight = selected_down_weight.astype(jnp.bfloat16).reshape(
        number_microbatches, number_blocks, feature_columns, adapter_rank
    )
    selected_up_weight = jnp.einsum(
        "ns,sri->nri", pick_rows, fetched_b, preferred_element_type=jnp.float32
    )
    selected_up_weight = selected_up_weight.astype(jnp.bfloat16).reshape(
        number_microbatches, number_blocks, adapter_rank, feature_columns
    )
    local_weight = weights[0]
    inputs = x_in.reshape(number_microbatches, token_rows, feature_columns)
    targets = cotangent.reshape(number_microbatches, token_rows, feature_columns)

    def forward_tick(tick_idx, state_in):
        incoming, saved_x, saved_y, kept_hidden = state_in
        micro_pos = tick_idx - segment_pos
        active_mask = (micro_pos >= 0) & (micro_pos < number_microbatches)
        microbatch_slot = jnp.clip(micro_pos, 0, number_microbatches - 1)
        first_in = lax.dynamic_index_in_dim(
            inputs, jnp.clip(tick_idx, 0, number_microbatches - 1), 0, keepdims=False
        )
        current = jnp.where(segment_pos == 0, first_in, incoming)
        blk_a = lax.dynamic_index_in_dim(selected_down_weight, microbatch_slot, 0, keepdims=False)
        blk_b = lax.dynamic_index_in_dim(selected_up_weight, microbatch_slot, 0, keepdims=False)
        down_weight_piece = jnp.einsum(
            "nbi,nir->nbr",
            current.reshape(number_blocks, rows_per_block, feature_columns),
            blk_a,
            preferred_element_type=jnp.float32,
        )
        down_weight_piece = down_weight_piece.reshape(token_rows, adapter_rank).astype(jnp.bfloat16)
        feature_rows, down_weight_library = (
            lax.all_gather(current, "tp", axis=1, tiled=True),
            lax.all_gather(down_weight_piece, "tp", axis=1, tiled=True),
        )
        adapter_hidden = jnp.sum(
            down_weight_library.reshape(token_rows, number_groups, adapter_rank).astype(
                jnp.float32
            ),
            axis=1,
        )
        adapter_hidden = adapter_hidden.astype(jnp.bfloat16)
        raised_rows = jnp.einsum(
            "swz,sze->swe",
            adapter_hidden.reshape(number_blocks, rows_per_block, adapter_rank),
            blk_b,
            preferred_element_type=jnp.float32,
        ).reshape(token_rows, feature_columns)
        preactivation = (
            jnp.dot(feature_rows, local_weight, preferred_element_type=jnp.float32)
            + ADAPTER_SCALE * raised_rows
        )
        output = (current.astype(jnp.float32) + jax.nn.gelu(preactivation)).astype(jnp.bfloat16)
        saved_x = storage_position(saved_x, current, microbatch_slot, active_mask)
        saved_y = storage_position(saved_y, preactivation, microbatch_slot, active_mask)
        kept_hidden = storage_position(kept_hidden, adapter_hidden, microbatch_slot, active_mask)
        passed = passed_along(output, "section", 1)
        return (passed, saved_x, saved_y, kept_hidden)

    start_state = (
        jnp.zeros((token_rows, feature_columns), jnp.bfloat16),
        jnp.zeros((number_microbatches, token_rows, feature_columns), jnp.bfloat16),
        jnp.zeros((number_microbatches, token_rows, feature_columns), jnp.float32),
        jnp.zeros((number_microbatches, token_rows, adapter_rank), jnp.bfloat16),
    )
    unused_out, saved_x, saved_y, kept_hidden = lax.fori_loop(
        0, tick_count, forward_tick, start_state
    )

    def backward_tick(tick_idx, state_in):
        incoming, down_gradient_total, up_gradient_total = state_in
        micro_pos = tick_idx - (segment_count - 1 - segment_pos)
        active_mask = (micro_pos >= 0) & (micro_pos < number_microbatches)
        microbatch_slot = jnp.clip(micro_pos, 0, number_microbatches - 1)
        last_in = lax.dynamic_index_in_dim(
            targets, jnp.clip(tick_idx, 0, number_microbatches - 1), 0, keepdims=False
        )
        earlier_neighbour = jnp.where(segment_pos == segment_count - 1, last_in, incoming)
        blk_a = lax.dynamic_index_in_dim(selected_down_weight, microbatch_slot, 0, keepdims=False)
        blk_b = lax.dynamic_index_in_dim(selected_up_weight, microbatch_slot, 0, keepdims=False)
        preactivation = lax.dynamic_index_in_dim(saved_y, microbatch_slot, 0, keepdims=False)
        gelu_out, gelu_pull = jax.vjp(jax.nn.gelu, preactivation)
        grad_pre = gelu_pull(earlier_neighbour.astype(jnp.float32))[0].astype(jnp.bfloat16)
        gradient_rows = grad_pre.reshape(number_blocks, rows_per_block, feature_columns)
        hidden_rows = lax.dynamic_index_in_dim(
            kept_hidden, microbatch_slot, 0, keepdims=False
        ).reshape(number_blocks, rows_per_block, adapter_rank)
        updated_up_weight = ADAPTER_SCALE * jnp.einsum(
            "nbr,nbi->nri", hidden_rows, gradient_rows, preferred_element_type=jnp.float32
        )
        backward_hidden = ADAPTER_SCALE * jnp.einsum(
            "nbi,nri->nbr", gradient_rows, blk_b, preferred_element_type=jnp.float32
        )
        backward_hidden = backward_hidden.reshape(token_rows, adapter_rank)
        backward_input = lax.dot_general(
            grad_pre, local_weight, (((1,), (1,)), ((), ())), preferred_element_type=jnp.float32
        )
        input_total = lax.psum_scatter(
            backward_input.astype(jnp.bfloat16), "tp", scatter_dimension=1, tiled=True
        ).astype(jnp.float32)
        hidden_total = lax.psum(backward_hidden.astype(jnp.bfloat16), "tp")
        hidden_gradient = hidden_total.reshape(number_blocks, rows_per_block, adapter_rank)
        x_rows = lax.dynamic_index_in_dim(saved_x, microbatch_slot, 0, keepdims=False).reshape(
            number_blocks, rows_per_block, feature_columns
        )
        new_a = jnp.einsum(
            "nbi,nbr->nir", x_rows, hidden_gradient, preferred_element_type=jnp.float32
        )
        adapter_input = jnp.einsum(
            "qwa,qla->qwl", hidden_gradient, blk_a, preferred_element_type=jnp.float32
        ).reshape(token_rows, feature_columns)
        later_neighbour = (
            earlier_neighbour.astype(jnp.float32) + input_total + adapter_input
        ).astype(jnp.bfloat16)
        down_gradient_total = storage_position(
            down_gradient_total, new_a, microbatch_slot, active_mask
        )
        up_gradient_total = storage_position(
            up_gradient_total, updated_up_weight, microbatch_slot, active_mask
        )
        passed = passed_along(later_neighbour, "section", -1)
        return (passed, down_gradient_total, up_gradient_total)

    back_state = (
        jnp.zeros((token_rows, feature_columns), jnp.bfloat16),
        jnp.zeros((number_microbatches, number_blocks, feature_columns, adapter_rank), jnp.float32),
        jnp.zeros((number_microbatches, number_blocks, adapter_rank, feature_columns), jnp.float32),
    )
    unused_grad, down_gradient_total, up_gradient_total = lax.fori_loop(
        0, tick_count, backward_tick, back_state
    )
    owners_of = (flat_ids[None, :] == style_axis[:, None]).astype(jnp.float32)
    block_down_weight = down_gradient_total.reshape(
        number_microbatches * number_blocks, feature_columns, adapter_rank
    )
    block_up_weight = up_gradient_total.reshape(
        number_microbatches * number_blocks, adapter_rank, feature_columns
    )
    grad_a = jnp.einsum(
        "kn,nir->kir", owners_of, block_down_weight, precision=lax.Precision.HIGHEST
    ).astype(jnp.bfloat16)
    grad_b = jnp.einsum(
        "kn,nri->kri", owners_of, block_up_weight, precision=lax.Precision.HIGHEST
    ).astype(jnp.bfloat16)
    return (grad_a[:, None], grad_b[:, None])


def solution(mesh):
    in_specs = (
        P(None, "tp"),
        P(None, "tp"),
        P("section", None, "tp"),
        P("section", None, "tp", None),
        P("section", None, None, "tp"),
        P(),
        P(),
    )
    out_specs = (P(None, "section", "tp", None), P(None, "section", None, "tp"))
    return jax.shard_map(body, mesh=mesh, in_specs=in_specs, out_specs=out_specs, check_vma=False)
```

profile of v0, /device:TPU:15, one launch (start us, length us, event | category | flops | bytes accessed | tf_op | source)
XLA Modules:
  0.0 1365.9 jit_solution(3440392727681885792)
XLA Ops:
  7.2 15.6 %all_to_all.8 = bf16[1,8,384,128]{3,2,0,1:T(8,128)(2,1)S(1)} all-to-all(bf16[1,8,384,128]{3,2,0,1:T(8,128)(2,1)} %bitcast.207), channel_id=1, replica_groups=mesh['section'=8,'tp'=16] {'section'}, dimensions={1} | all-to-all | bytes 1572864 | tf_op jit(solution)/shard_map/all_to_all | solution.py:34
  22.8 6.2 all-to-all-start.1
  30.0 9.6 all-to-all-done.1
  41.7 524.8 %while.40 = (s32[]{:T(128)}, bf16[128,384]{1,0:T(8,128)(2,1)S(1)}, bf16[2,128,384]{2,1,0:T(8,128)(2,1)S(1)}, f32[2,128,384]{2,1,0:T(8,128)}, bf16[2,128,128]{2,1...) while((s32[]{:T(128)}, bf16[128,384]{1,0:T(8,128)(2,1)S(1)}, ...), condition=%wide.region_3.4_spmd, body=%wide.region_1.3_spmd.sunk | while | flops 630210560 | bytes 17760612 | solution.py:113
  43.6 21.4 %all_gather.22 = bf16[128,2048]{1,0:T(8,128)(2,1)S(1)} all-gather(bf16[128,128]{1,0:T(8,128)(2,1)S(1)} %bitcast.202), channel_id=1, replica_groups=mesh['section'=8,'tp'=16] {'tp'}, dimensions={1}, use_global_device_ids=true | all-gather | bytes 557056 | tf_op jit(solution)/shard_map/while/body/eval_jaxpr/all_gather | solution.py:81
  67.9 23.9 %all-gather.2.cloned.1.call-done = bf16[128,6144]{1,0:T(8,128)(2,1)} async-done(((bf16[128,384]{1,0:T(8,128)(2,1)}), bf16[128,6144]{1,0:T(8,128)(2,1)}) %all-gather.2.cloned.1.call-update) | async-done | bytes 1572880 | tf_op jit(solution)/shard_map/while/body/eval_jaxpr/all_gather | solution.py:80
  101.8 17.9 %all_gather.22 = bf16[128,2048]{1,0:T(8,128)(2,1)S(1)} all-gather(bf16[128,128]{1,0:T(8,128)(2,1)S(1)} %bitcast.202), channel_id=1, replica_groups=mesh['section'=8,'tp'=16] {'tp'}, dimensions={1}, use_global_device_ids=true | all-gather | bytes 557056 | tf_op jit(solution)/shard_map/while/body/eval_jaxpr/all_gather | solution.py:81
  122.6 27.5 %all-gather.2.cloned.1.call-done = bf16[128,6144]{1,0:T(8,128)(2,1)} async-done(((bf16[128,384]{1,0:T(8,128)(2,1)}), bf16[128,6144]{1,0:T(8,128)(2,1)}) %all-gather.2.cloned.1.call-update) | async-done | bytes 1572880 | tf_op jit(solution)/shard_map/while/body/eval_jaxpr/all_gather | solution.py:80
  160.2 17.9 %all_gather.22 = bf16[128,2048]{1,0:T(8,128)(2,1)S(1)} all-gather(bf16[128,128]{1,0:T(8,128)(2,1)S(1)} %bitcast.202), channel_id=1, replica_groups=mesh['section'=8,'tp'=16] {'tp'}, dimensions={1}, use_global_device_ids=true | all-gather | bytes 557056 | tf_op jit(solution)/shard_map/while/body/eval_jaxpr/all_gather | solution.py:81
  181.0 27.5 %all-gather.2.cloned.1.call-done = bf16[128,6144]{1,0:T(8,128)(2,1)} async-done(((bf16[128,384]{1,0:T(8,128)(2,1)}), bf16[128,6144]{1,0:T(8,128)(2,1)}) %all-gather.2.cloned.1.call-update) | async-done | bytes 1572880 | tf_op jit(solution)/shard_map/while/body/eval_jaxpr/all_gather | solution.py:80
  218.5 17.7 %all_gather.22 = bf16[128,2048]{1,0:T(8,128)(2,1)S(1)} all-gather(bf16[128,128]{1,0:T(8,128)(2,1)S(1)} %bitcast.202), channel_id=1, replica_groups=mesh['section'=8,'tp'=16] {'tp'}, dimensions={1}, use_global_device_ids=true | all-gather | bytes 557056 | tf_op jit(solution)/shard_map/while/body/eval_jaxpr/all_gather | solution.py:81
  239.2 27.6 %all-gather.2.cloned.1.call-done = bf16[128,6144]{1,0:T(8,128)(2,1)} async-done(((bf16[128,384]{1,0:T(8,128)(2,1)}), bf16[128,6144]{1,0:T(8,128)(2,1)}) %all-gather.2.cloned.1.call-update) | async-done | bytes 1572880 | tf_op jit(solution)/shard_map/while/body/eval_jaxpr/all_gather | solution.py:80
  276.8 17.7 %all_gather.22 = bf16[128,2048]{1,0:T(8,128)(2,1)S(1)} all-gather(bf16[128,128]{1,0:T(8,128)(2,1)S(1)} %bitcast.202), channel_id=1, replica_groups=mesh['section'=8,'tp'=16] {'tp'}, dimensions={1}, use_global_device_ids=true | all-gather | bytes 557056 | tf_op jit(solution)/shard_map/while/body/eval_jaxpr/all_gather | solution.py:81
  297.4 27.6 %all-gather.2.cloned.1.call-done = bf16[128,6144]{1,0:T(8,128)(2,1)} async-done(((bf16[128,384]{1,0:T(8,128)(2,1)}), bf16[128,6144]{1,0:T(8,128)(2,1)}) %all-gather.2.cloned.1.call-update) | async-done | bytes 1572880 | tf_op jit(solution)/shard_map/while/body/eval_jaxpr/all_gather | solution.py:80
  335.0 17.7 %all_gather.22 = bf16[128,2048]{1,0:T(8,128)(2,1)S(1)} all-gather(bf16[128,128]{1,0:T(8,128)(2,1)S(1)} %bitcast.202), channel_id=1, replica_groups=mesh['section'=8,'tp'=16] {'tp'}, dimensions={1}, use_global_device_ids=true | all-gather | bytes 557056 | tf_op jit(solution)/shard_map/while/body/eval_jaxpr/all_gather | solution.py:81
  355.7 27.6 %all-gather.2.cloned.1.call-done = bf16[128,6144]{1,0:T(8,128)(2,1)} async-done(((bf16[128,384]{1,0:T(8,128)(2,1)}), bf16[128,6144]{1,0:T(8,128)(2,1)}) %all-gather.2.cloned.1.call-update) | async-done | bytes 1572880 | tf_op jit(solution)/shard_map/while/body/eval_jaxpr/all_gather | solution.py:80
  393.3 17.9 %all_gather.22 = bf16[128,2048]{1,0:T(8,128)(2,1)S(1)} all-gather(bf16[128,128]{1,0:T(8,128)(2,1)S(1)} %bitcast.202), channel_id=1, replica_groups=mesh['section'=8,'tp'=16] {'tp'}, dimensions={1}, use_global_device_ids=true | all-gather | bytes 557056 | tf_op jit(solution)/shard_map/while/body/eval_jaxpr/all_gather | solution.py:81
  414.1 27.5 %all-gather.2.cloned.1.call-done = bf16[128,6144]{1,0:T(8,128)(2,1)} async-done(((bf16[128,384]{1,0:T(8,128)(2,1)}), bf16[128,6144]{1,0:T(8,128)(2,1)}) %all-gather.2.cloned.1.call-update) | async-done | bytes 1572880 | tf_op jit(solution)/shard_map/while/body/eval_jaxpr/all_gather | solution.py:80
  451.6 17.9 %all_gather.22 = bf16[128,2048]{1,0:T(8,128)(2,1)S(1)} all-gather(bf16[128,128]{1,0:T(8,128)(2,1)S(1)} %bitcast.202), channel_id=1, replica_groups=mesh['section'=8,'tp'=16] {'tp'}, dimensions={1}, use_global_device_ids=true | all-gather | bytes 557056 | tf_op jit(solution)/shard_map/while/body/eval_jaxpr/all_gather | solution.py:81
  472.4 27.5 %all-gather.2.cloned.1.call-done = bf16[128,6144]{1,0:T(8,128)(2,1)} async-done(((bf16[128,384]{1,0:T(8,128)(2,1)}), bf16[128,6144]{1,0:T(8,128)(2,1)}) %all-gather.2.cloned.1.call-update) | async-done | bytes 1572880 | tf_op jit(solution)/shard_map/while/body/eval_jaxpr/all_gather | solution.py:80
  510.0 17.9 %all_gather.22 = bf16[128,2048]{1,0:T(8,128)(2,1)S(1)} all-gather(bf16[128,128]{1,0:T(8,128)(2,1)S(1)} %bitcast.202), channel_id=1, replica_groups=mesh['section'=8,'tp'=16] {'tp'}, dimensions={1}, use_global_device_ids=true | all-gather | bytes 557056 | tf_op jit(solution)/shard_map/while/body/eval_jaxpr/all_gather | solution.py:81
  530.8 27.6 %all-gather.2.cloned.1.call-done = bf16[128,6144]{1,0:T(8,128)(2,1)} async-done(((bf16[128,384]{1,0:T(8,128)(2,1)}), bf16[128,6144]{1,0:T(8,128)(2,1)}) %all-gather.2.cloned.1.call-update) | async-done | bytes 1572880 | tf_op jit(solution)/shard_map/while/body/eval_jaxpr/all_gather | solution.py:80
  569.0 783.3 %while.41 = (s32[]{:T(128)}, bf16[128,384]{1,0:T(8,128)(2,1)S(1)}, f32[2,4,384,128]{3,2,1,0:T(8,128)}, f32[2,4,128,384]{3,2,1,0:T(8,128)S(1)}, pred[]{:T(512)}, ...) while((s32[]{:T(128)}, bf16[128,384]{1,0:T(8,128)(2,1)S(1)}, ...), condition=%wide.region_7.8_spmd, body=%wide.region_4.7_spmd.sunk | while | flops 657113088 | bytes 30540184 | solution.py:176
  577.1 53.9 %psum.15 = bf16[4,32,128]{2,1,0:T(8,128)(2,1)S(1)} all-reduce(bf16[4,32,128]{2,1,0:T(8,128)(2,1)S(1)} %fusion.126), channel_id=1, replica_groups=mesh['section'=8,'tp'=16] {'tp'}, use_global_device_ids=true, to_apply=%region_6.6 | all-reduce | flops 16384 | bytes 65536 | tf_op jit(solution)/shard_map/while/body/eval_jaxpr/psum | solution.py:148
  633.7 15.6 %reduce-scatter.6.cloned.1.call-done = bf16[384,128]{1,0:T(8,128)(2,1)} async-done(((bf16[6144,128]{1,0:T(8,128)(2,1)}), bf16[384,128]{1,0:T(8,128)(2,1)}) %reduce-scatter.6.cloned.1.call-update) | async-done | bytes 98320 | tf_op jit(solution)/shard_map/while
  651.3 4.6 collective-permute-start.1
  665.2 56.6 %psum.15 = bf16[4,32,128]{2,1,0:T(8,128)(2,1)S(1)} all-reduce(bf16[4,32,128]{2,1,0:T(8,128)(2,1)S(1)} %fusion.126), channel_id=1, replica_groups=mesh['section'=8,'tp'=16] {'tp'}, use_global_device_ids=true, to_apply=%region_6.6 | all-reduce | flops 16384 | bytes 65536 | tf_op jit(solution)/shard_map/while/body/eval_jaxpr/psum | solution.py:148
  724.5 12.2 reduce-scatter.6.cloned.1.call-done
  738.6 4.4 collective-permute-start.1
  752.3 55.9 %psum.15 = bf16[4,32,128]{2,1,0:T(8,128)(2,1)S(1)} all-reduce(bf16[4,32,128]{2,1,0:T(8,128)(2,1)S(1)} %fusion.126), channel_id=1, replica_groups=mesh['section'=8,'tp'=16] {'tp'}, use_global_device_ids=true, to_apply=%region_6.6 | all-reduce | flops 16384 | bytes 65536 | tf_op jit(solution)/shard_map/while/body/eval_jaxpr/psum | solution.py:148
  811.0 12.6 reduce-scatter.6.cloned.1.call-done
  825.5 4.3 collective-permute-start.1
  839.2 55.9 %psum.15 = bf16[4,32,128]{2,1,0:T(8,128)(2,1)S(1)} all-reduce(bf16[4,32,128]{2,1,0:T(8,128)(2,1)S(1)} %fusion.126), channel_id=1, replica_groups=mesh['section'=8,'tp'=16] {'tp'}, use_global_device_ids=true, to_apply=%region_6.6 | all-reduce | flops 16384 | bytes 65536 | tf_op jit(solution)/shard_map/while/body/eval_jaxpr/psum | solution.py:148
  897.8 12.7 reduce-scatter.6.cloned.1.call-done
  926.0 55.9 %psum.15 = bf16[4,32,128]{2,1,0:T(8,128)(2,1)S(1)} all-reduce(bf16[4,32,128]{2,1,0:T(8,128)(2,1)S(1)} %fusion.126), channel_id=1, replica_groups=mesh['section'=8,'tp'=16] {'tp'}, use_global_device_ids=true, to_apply=%region_6.6 | all-reduce | flops 16384 | bytes 65536 | tf_op jit(solution)/shard_map/while/body/eval_jaxpr/psum | solution.py:148
  984.6 12.6 reduce-scatter.6.cloned.1.call-done
  999.2 4.4 collective-permute-start.1
  1012.9 55.9 %psum.15 = bf16[4,32,128]{2,1,0:T(8,128)(2,1)S(1)} all-reduce(bf16[4,32,128]{2,1,0:T(8,128)(2,1)S(1)} %fusion.126), channel_id=1, replica_groups=mesh['section'=8,'tp'=16] {'tp'}, use_global_device_ids=true, to_apply=%region_6.6 | all-reduce | flops 16384 | bytes 65536 | tf_op jit(solution)/shard_map/while/body/eval_jaxpr/psum | solution.py:148
  1071.5 12.7 reduce-scatter.6.cloned.1.call-done
  1086.1 4.4 collective-permute-start.1
  1099.8 55.8 %psum.15 = bf16[4,32,128]{2,1,0:T(8,128)(2,1)S(1)} all-reduce(bf16[4,32,128]{2,1,0:T(8,128)(2,1)S(1)} %fusion.126), channel_id=1, replica_groups=mesh['section'=8,'tp'=16] {'tp'}, use_global_device_ids=true, to_apply=%region_6.6 | all-reduce | flops 16384 | bytes 65536 | tf_op jit(solution)/shard_map/while/body/eval_jaxpr/psum | solution.py:148
  1158.3 12.7 reduce-scatter.6.cloned.1.call-done
  1186.6 56.0 %psum.15 = bf16[4,32,128]{2,1,0:T(8,128)(2,1)S(1)} all-reduce(bf16[4,32,128]{2,1,0:T(8,128)(2,1)S(1)} %fusion.126), channel_id=1, replica_groups=mesh['section'=8,'tp'=16] {'tp'}, use_global_device_ids=true, to_apply=%region_6.6 | all-reduce | flops 16384 | bytes 65536 | tf_op jit(solution)/shard_map/while/body/eval_jaxpr/psum | solution.py:148
  1245.3 12.6 reduce-scatter.6.cloned.1.call-done
  1259.8 4.3 collective-permute-start.1
  1273.5 55.9 %psum.15 = bf16[4,32,128]{2,1,0:T(8,128)(2,1)S(1)} all-reduce(bf16[4,32,128]{2,1,0:T(8,128)(2,1)S(1)} %fusion.126), channel_id=1, replica_groups=mesh['section'=8,'tp'=16] {'tp'}, use_global_device_ids=true, to_apply=%region_6.6 | all-reduce | flops 16384 | bytes 65536 | tf_op jit(solution)/shard_map/while/body/eval_jaxpr/psum | solution.py:148
  1332.0 12.7 reduce-scatter.6.cloned.1.call-done
  1346.7 4.3 collective-permute-start.1
  (353 shorter events, 262.0 us)
Async XLA Ops:
  7.2 21.9 %copy-start.6 = (s32[2,4]{1,0:T(2,128)S(1)}, s32[2,4]{1,0:T(2,128)}, u32[]{:S(2)}) copy-start(s32[2,4]{1,0:T(2,128)} %param.16) | copy-start | bytes 100
  7.2 21.9 %copy-start.7 = (s32[8]{0:T(128)S(1)}, s32[8]{0:T(128)}, u32[]{:S(2)}) copy-start(s32[8]{0:T(128)} %param.17) | copy-start | bytes 100
  22.8 16.8 %all-to-all-start.1 = ((bf16[1,8,128,384]{3,2,0,1:T(8,128)(2,1)}), bf16[1,8,128,384]{3,2,0,1:T(8,128)(2,1)S(1)}, u32[]{:S(2)}, u32[]{:S(2)}) async-start(bf16[1,8,128,384]{3,2,0,1:T(8,128)(2,1)} %bitcast.32), calls=%async_computation.2 | async-start | bytes 1572864 | tf_op jit(solution)/shard_map/all_to_all | solution.py:35
  41.7 50.1 %all-gather.2.cloned.1.call-start = ((), (), s32[]{:S(2)}) async-start(), calls=%async_computation.3 | async-start | bytes 1671168 | tf_op jit(solution)/shard_map/while/body/eval_jaxpr/all_gather | solution.py:80
  43.6 48.3 %copy-start = (bf16[128,384]{1,0:T(8,128)(2,1)S(1)}, bf16[128,384]{1,0:T(8,128)(2,1)}, u32[]{:S(2)}) copy-start(bf16[128,384]{1,0:T(8,128)(2,1)} %get-tuple-element.818) | copy-start | bytes 294916 | tf_op jit(solution)/shard_map/while
  95.7 4.3 collective-permute-start
  100.0 50.2 %all-gather.2.cloned.1.call-start = ((), (), s32[]{:S(2)}) async-start(), calls=%async_computation.3 | async-start | bytes 1671168 | tf_op jit(solution)/shard_map/while/body/eval_jaxpr/all_gather | solution.py:80
  101.8 48.3 %copy-start = (bf16[128,384]{1,0:T(8,128)(2,1)S(1)}, bf16[128,384]{1,0:T(8,128)(2,1)}, u32[]{:S(2)}) copy-start(bf16[128,384]{1,0:T(8,128)(2,1)} %get-tuple-element.818) | copy-start | bytes 294916 | tf_op jit(solution)/shard_map/while
  154.0 4.3 collective-permute-start
  158.3 50.2 %all-gather.2.cloned.1.call-start = ((), (), s32[]{:S(2)}) async-start(), calls=%async_computation.3 | async-start | bytes 1671168 | tf_op jit(solution)/shard_map/while/body/eval_jaxpr/all_gather | solution.py:80
  160.2 48.3 %copy-start = (bf16[128,384]{1,0:T(8,128)(2,1)S(1)}, bf16[128,384]{1,0:T(8,128)(2,1)}, u32[]{:S(2)}) copy-start(bf16[128,384]{1,0:T(8,128)(2,1)} %get-tuple-element.818) | copy-start | bytes 294916 | tf_op jit(solution)/shard_map/while
  212.4 4.3 collective-permute-start
  216.7 50.1 %all-gather.2.cloned.1.call-start = ((), (), s32[]{:S(2)}) async-start(), calls=%async_computation.3 | async-start | bytes 1671168 | tf_op jit(solution)/shard_map/while/body/eval_jaxpr/all_gather | solution.py:80
  218.5 48.3 %copy-start = (bf16[128,384]{1,0:T(8,128)(2,1)S(1)}, bf16[128,384]{1,0:T(8,128)(2,1)}, u32[]{:S(2)}) copy-start(bf16[128,384]{1,0:T(8,128)(2,1)} %get-tuple-element.818) | copy-start | bytes 294916 | tf_op jit(solution)/shard_map/while
  270.6 4.3 collective-permute-start
  274.9 50.1 %all-gather.2.cloned.1.call-start = ((), (), s32[]{:S(2)}) async-start(), calls=%async_computation.3 | async-start | bytes 1671168 | tf_op jit(solution)/shard_map/while/body/eval_jaxpr/all_gather | solution.py:80
  276.8 48.3 %copy-start = (bf16[128,384]{1,0:T(8,128)(2,1)S(1)}, bf16[128,384]{1,0:T(8,128)(2,1)}, u32[]{:S(2)}) copy-start(bf16[128,384]{1,0:T(8,128)(2,1)} %get-tuple-element.818) | copy-start | bytes 294916 | tf_op jit(solution)/shard_map/while
  328.9 4.3 collective-permute-start
  333.2 50.1 %all-gather.2.cloned.1.call-start = ((), (), s32[]{:S(2)}) async-start(), calls=%async_computation.3 | async-start | bytes 1671168 | tf_op jit(solution)/shard_map/while/body/eval_jaxpr/all_gather | solution.py:80
  335.0 48.3 %copy-start = (bf16[128,384]{1,0:T(8,128)(2,1)S(1)}, bf16[128,384]{1,0:T(8,128)(2,1)}, u32[]{:S(2)}) copy-start(bf16[128,384]{1,0:T(8,128)(2,1)} %get-tuple-element.818) | copy-start | bytes 294916 | tf_op jit(solution)/shard_map/while
  387.1 4.3 collective-permute-start
  391.4 50.2 %all-gather.2.cloned.1.call-start = ((), (), s32[]{:S(2)}) async-start(), calls=%async_computation.3 | async-start | bytes 1671168 | tf_op jit(solution)/shard_map/while/body/eval_jaxpr/all_gather | solution.py:80
  393.3 48.3 %copy-start = (bf16[128,384]{1,0:T(8,128)(2,1)S(1)}, bf16[128,384]{1,0:T(8,128)(2,1)}, u32[]{:S(2)}) copy-start(bf16[128,384]{1,0:T(8,128)(2,1)} %get-tuple-element.818) | copy-start | bytes 294916 | tf_op jit(solution)/shard_map/while
  445.5 4.3 collective-permute-start
  449.8 50.2 %all-gather.2.cloned.1.call-start = ((), (), s32[]{:S(2)}) async-start(), calls=%async_computation.3 | async-start | bytes 1671168 | tf_op jit(solution)/shard_map/while/body/eval_jaxpr/all_gather | solution.py:80
  451.6 48.3 %copy-start = (bf16[128,384]{1,0:T(8,128)(2,1)S(1)}, bf16[128,384]{1,0:T(8,128)(2,1)}, u32[]{:S(2)}) copy-start(bf16[128,384]{1,0:T(8,128)(2,1)} %get-tuple-element.818) | copy-start | bytes 294916 | tf_op jit(solution)/shard_map/while
  503.8 4.3 collective-permute-start
  508.2 50.2 %all-gather.2.cloned.1.call-start = ((), (), s32[]{:S(2)}) async-start(), calls=%async_computation.3 | async-start | bytes 1671168 | tf_op jit(solution)/shard_map/while/body/eval_jaxpr/all_gather | solution.py:80
  510.0 48.3 %copy-start = (bf16[128,384]{1,0:T(8,128)(2,1)S(1)}, bf16[128,384]{1,0:T(8,128)(2,1)}, u32[]{:S(2)}) copy-start(bf16[128,384]{1,0:T(8,128)(2,1)} %get-tuple-element.818) | copy-start | bytes 294916 | tf_op jit(solution)/shard_map/while
  562.2 4.3 collective-permute-start
  569.0 80.3 %reduce-scatter.6.cloned.1.call-start = ((), (), s32[]{:S(2)}) async-start(), calls=%async_computation.4 | async-start | bytes 1671168 | tf_op jit(solution)/shard_map/while
  651.3 5.8 collective-permute-start.1
  657.1 79.5 %reduce-scatter.6.cloned.1.call-start = ((), (), s32[]{:S(2)}) async-start(), calls=%async_computation.4 | async-start | bytes 1671168 | tf_op jit(solution)/shard_map/while
  738.6 5.7 collective-permute-start.1
  744.3 79.2 %reduce-scatter.6.cloned.1.call-start = ((), (), s32[]{:S(2)}) async-start(), calls=%async_computation.4 | async-start | bytes 1671168 | tf_op jit(solution)/shard_map/while
  825.5 5.6 collective-permute-start.1
  831.1 79.3 %reduce-scatter.6.cloned.1.call-start = ((), (), s32[]{:S(2)}) async-start(), calls=%async_computation.4 | async-start | bytes 1671168 | tf_op jit(solution)/shard_map/while
  912.4 5.6 collective-permute-start.1
  918.0 79.3 %reduce-scatter.6.cloned.1.call-start = ((), (), s32[]{:S(2)}) async-start(), calls=%async_computation.4 | async-start | bytes 1671168 | tf_op jit(solution)/shard_map/while
  999.2 5.6 collective-permute-start.1
  1004.8 79.3 %reduce-scatter.6.cloned.1.call-start = ((), (), s32[]{:S(2)}) async-start(), calls=%async_computation.4 | async-start | bytes 1671168 | tf_op jit(solution)/shard_map/while
  1086.1 5.6 collective-permute-start.1
  1091.8 79.3 %reduce-scatter.6.cloned.1.call-start = ((), (), s32[]{:S(2)}) async-start(), calls=%async_computation.4 | async-start | bytes 1671168 | tf_op jit(solution)/shard_map/while
  1173.0 5.6 collective-permute-start.1
  1178.6 79.3 %reduce-scatter.6.cloned.1.call-start = ((), (), s32[]{:S(2)}) async-start(), calls=%async_computation.4 | async-start | bytes 1671168 | tf_op jit(solution)/shard_map/while
  1259.8 5.6 collective-permute-start.1
  1265.4 79.3 %reduce-scatter.6.cloned.1.call-start = ((), (), s32[]{:S(2)}) async-start(), calls=%async_computation.4 | async-start | bytes 1671168 | tf_op jit(solution)/shard_map/while
  1346.7 5.6 collective-permute-start.1
  (21 other events, 36.3 us)
Sparse Core Ops, SparseCore 0:
  45.2 46.5 all-gather.1
  103.5 46.6 all-gather.1
  161.8 46.6 all-gather.1
  219.9 46.8 all-gather.1
  278.1 46.8 all-gather.1
  336.4 46.8 all-gather.1
  395.0 46.6 all-gather.1
  453.3 46.6 all-gather.1
  511.7 46.6 all-gather.1
  575.9 73.4 reduce-scatter.5
  663.9 72.6 reduce-scatter.5
  751.1 72.3 reduce-scatter.5
  837.9 72.4 reduce-scatter.5
  924.8 72.4 reduce-scatter.5
  1011.7 72.4 reduce-scatter.5
  1098.6 72.4 reduce-scatter.5
  1185.4 72.4 reduce-scatter.5
  1272.2 72.4 reduce-scatter.5
where the time goes:
time: 1380 us; the launch traced here: 1370 us
  blocking collectives  681 us (49%)
  waiting for transfers between devices  391 us (28%)
  matrix products  106 us (8%)
  local copies, waits for them, and re-layouts  68.2 us (5%)
  starting transfers between devices  57.3 us (4%)
  other arithmetic  46.8 us (3%)
  between operations  14.1 us (1%)
    psum x9, blocking collectives, backward_tick(): hidden_total = lax.psum(backward_hidden.astype(jnp.bfloat16), 'tp')  502 us
    all_gather x9, waiting for transfers between devices, forward_tick(): lax.all_gather(current, 'tp', axis=1, tiled=True)  244 us
    all_gather x9, blocking collectives, forward_tick(): lax.all_gather(down_weight_piece, 'tp', axis=1, tiled=True)  164 us
    while x27, waiting for transfers between devices  117 us
    ppermute x18, starting transfers between devices, passed_along(): lax.ppermute(value, axis, [(source, source + steps) for source in range(l...  51.1 us
    dot_general x9, matrix products, backward_tick(): lax.dot_general(grad_pre, local_weight, (((1,), (1,)), ((), ())), preferr...  35.3 us
    dot_general x9, matrix products, forward_tick(): jnp.dot(feature_rows, local_weight, preferred_element_type=jnp.float32)  34.7 us
    while x81, local copies, waits for them, and re-layouts  34.5 us
  transfers between devices with their start and end apart: 37, of which 28 were waited for; matrix products, arithmetic and copies ran while one was open for 6% of the time, Pallas kernels for 0%

commit v1 on v0

v1 whole, which is shorter than its diff:
```python
import functools

import jax
import jax.numpy as jnp
from jax import lax
from jax.experimental import pallas as pl
from jax.experimental.pallas import tpu as pltpu
from jax.sharding import PartitionSpec as P

ADAPTER_SCALE = 0.25
SIDE = 4
LAYERS = 8
BLOCKS = 8
ROWS = 32
RANK = 128
CHUNK = 384
WIDE = SIDE * CHUNK
Z_AT = WIDE
OWN_AT = WIDE + RANK
PAY = OWN_AT + CHUNK
PAY_EXTRA = PAY + RANK + CHUNK
BF = jnp.bfloat16
F32 = jnp.float32


def along_a(k):
    return lambda x, c, z, y: (x, c, z, y + k) if c == 0 else (x, c, z + k, y)


def along_b(k):
    return lambda x, c, z, y: (x, c, z + k, y) if c == 0 else (x, c, z, y + k)


def onward(k):
    return lambda x, c, z, y: (x, 1, z, y + k) if c == 0 else (x + 1, 0, z + k, y)


def backward(k):
    return lambda x, c, z, y: (x, 0, z + k, y) if c == 1 else (x - 1, 1, z, y + k)


def send(value, target):
    pairs = []
    for sec in range(2 * SIDE):
        for tp in range(SIDE * SIDE):
            x, c, z, y = target(sec // 2, sec % 2, tp // SIDE, tp % SIDE)
            sec_to = (x % SIDE) * 2 + c
            tp_to = (z % SIDE) * SIDE + y % SIDE
            pairs.append((sec * SIDE * SIDE + tp, sec_to * SIDE * SIDE + tp_to))
    return lax.ppermute(value, ("section", "tp"), pairs)


def chunk_at(index):
    return pl.ds(pl.multiple_of(index * CHUNK, CHUNK), CHUNK)


def dot(left, right):
    return jnp.dot(left, right, preferred_element_type=F32)


def dot_nt(left, right):
    return lax.dot_general(left, right, (((1,), (1,)), ((), ())), preferred_element_type=F32)


def dot_tn(left, right):
    return lax.dot_general(left, right, (((0,), (0,)), ((), ())), preferred_element_type=F32)


def gelu_both(y):
    scale = 0.7978845608028654
    square = y * y
    t = jnp.tanh(scale * y * (1.0 + 0.044715 * square))
    half = 0.5 * (1.0 + t)
    slope = half + 0.5 * y * (1.0 - t * t) * scale * (1.0 + 3.0 * 0.044715 * square)
    return y * half, slope


def forward_kernel(tick, sc, p0, p1, p2, p3, xg, w, a0, a1, a2, a3, b0, b1, b2, b3,
                   _g, _z, _h, pay, g_out, z_out, h_out, h_all):
    at = tick * 8
    first, a, b = sc[at + 3], sc[at + 4], sc[at + 5]
    step = pl.program_id(0)

    @pl.when(step == 0)
    def _():
        z = sum(p[:, Z_AT:OWN_AT].astype(F32) for p in (p0, p1, p2, p3)).astype(BF)
        z_out[0] = z
        z_part = jnp.zeros((ROWS, RANK), F32)
        for k, (p, ak, bk) in enumerate(((p0, a0, b0), (p1, a1, b1), (p2, a2, b2), (p3, a3, b3))):
            here = chunk_at(lax.rem(b - k + SIDE, SIDE))
            y = sum(q[:, here].astype(F32) for q in (p0, p1, p2, p3))
            y = y + ADAPTER_SCALE * dot(z, bk[0])
            value, slope = gelu_both(y)
            h = (p[:, OWN_AT:PAY].astype(F32) + value).astype(BF)
            h = jnp.where(first > 0, xg[:, here], h)
            h_all[:, here] = h
            g_out[0, :, here] = slope
            z_part = z_part + dot(h, ak[0])
            if k == 0:
                h_out[0] = h
                pay[:, OWN_AT:PAY] = h
        pay[:, Z_AT:OWN_AT] = z_part.astype(BF)

    pay[:, chunk_at(lax.rem(a - step + SIDE, SIDE))] = dot(h_all[...], w[0]).astype(BF)


def backward_kernel(tick, sc, q0, q1, q2, q3, cg, w, a0, a1, a2, a3, b0, b1, b2, b3, slope, z_in,
                    _q, _z, _e, pay0, pay, q_out, z_out, e_out, e_all, total):
    at = tick * 8
    first, b = sc[at + 3], sc[at + 5]
    step = pl.program_id(0)

    @pl.when(step == 0)
    def _():
        q = sum(p[:, Z_AT:OWN_AT].astype(F32) for p in (q0, q1, q2, q3)).astype(BF)
        q_out[0] = q
        z_out[0] = q0[:, PAY:PAY + RANK]
        e_out[0] = q0[:, PAY + RANK:]
        q_part = jnp.zeros((ROWS, RANK), F32)
        for k, (p, ak, bk) in enumerate(((q0, a0, b0), (q1, a1, b1), (q2, a2, b2), (q3, a3, b3))):
            here = chunk_at(lax.rem(b - k + SIDE, SIDE))
            n = sum(r[:, here].astype(F32) for r in (q0, q1, q2, q3))
            g = (p[:, OWN_AT:PAY].astype(F32) + n + dot_nt(q, ak[0])).astype(BF)
            g = jnp.where(first > 0, cg[:, here], g)
            e = (slope[0, :, here] * g.astype(F32)).astype(BF)
            e_all[k] = e
            q_part = q_part + dot_nt(e, bk[0])
            if k == 0:
                pay[:, OWN_AT:PAY] = g
                pay0[:, OWN_AT:PAY] = g
                pay0[:, PAY + RANK:] = e
        q_part = (ADAPTER_SCALE * q_part).astype(BF)
        pay[:, Z_AT:OWN_AT] = q_part
        pay0[:, Z_AT:OWN_AT] = q_part
        pay0[:, PAY:PAY + RANK] = z_in[0]
        total[...] = jnp.zeros_like(total)

    total[...] += dot_nt(e_all[step], w[0])

    @pl.when(step == SIDE - 1)
    def _():
        n = total[...].astype(BF)
        pay[:, :WIDE] = n
        pay0[:, :WIDE] = n


def gradient_kernel(sc, x, h, q, z, e, ga, gb):
    style = pl.program_id(0)
    block = lax.broadcasted_iota(jnp.int32, (BLOCKS * ROWS, 1), 0) // ROWS
    mine = jnp.zeros((BLOCKS * ROWS, 1), F32)
    for n in range(BLOCKS):
        mine = jnp.where((block == n) & (sc[n] == style), 1.0, mine)
    rows = jnp.where(sc[BLOCKS] == 0, x[...], h[...])
    q_mine = (q[...].astype(F32) * mine).astype(BF)
    z_mine = (z[...].astype(F32) * mine).astype(BF)
    ga[0, 0] = dot_tn(rows, q_mine).astype(BF)
    gb[0, 0] = (ADAPTER_SCALE * dot_tn(z_mine, e[...])).astype(BF)


def whole(shape):
    return pl.BlockSpec(shape, lambda i, sc: (0,) * len(shape))


def adapter_specs(at, shape):
    return [pl.BlockSpec((1,) + shape, lambda i, sc: (sc[at], 0, 0)) for _ in range(SIDE)]


def slot_spec(at, columns):
    return pl.BlockSpec((1, ROWS, columns), lambda i, sc: (sc[at], 0, 0))


PARAMS = pltpu.CompilerParams(vmem_limit_bytes=24 << 20)


def forward_tick(tick, table, payloads, xg, w, a_lib, b_lib, g_buf, z_buf, h_buf):
    at = tick * 8
    keep = pl.BlockSpec(memory_space=pl.ANY)
    grid_spec = pltpu.PrefetchScalarGridSpec(
        num_scalar_prefetch=1,
        grid=(SIDE,),
        in_specs=[whole((ROWS, PAY))] * SIDE
        + [pl.BlockSpec((ROWS, WIDE), lambda i, sc: (sc[at + 1], 0))]
        + [pl.BlockSpec((1, WIDE, CHUNK), lambda i, sc: (i, 0, 0))]
        + adapter_specs(at, (CHUNK, RANK))
        + adapter_specs(at, (RANK, CHUNK))
        + [keep] * 3,
        out_specs=[whole((ROWS, PAY)), slot_spec(at + 2, WIDE), slot_spec(at + 2, RANK), slot_spec(at + 2, CHUNK)],
        scratch_shapes=[pltpu.VMEM((ROWS, WIDE), BF)],
    )
    like = lambda v: jax.ShapeDtypeStruct(v.shape, v.dtype)
    return pl.pallas_call(
        functools.partial(forward_kernel, tick),
        grid_spec=grid_spec,
        out_shape=[jax.ShapeDtypeStruct((ROWS, PAY), BF), like(g_buf), like(z_buf), like(h_buf)],
        input_output_aliases={15: 1, 16: 2, 17: 3},
        compiler_params=PARAMS,
        name="forward_stage",
    )(table, *payloads, xg, w, *a_lib, *b_lib, g_buf, z_buf, h_buf)


def backward_tick(tick, table, payloads, cg, w, a_lib, b_lib, g_buf, z_buf, q_buf, zr_buf, e_buf):
    at = tick * 8
    keep = pl.BlockSpec(memory_space=pl.ANY)
    grid_spec = pltpu.PrefetchScalarGridSpec(
        num_scalar_prefetch=1,
        grid=(SIDE,),
        in_specs=[whole((ROWS, PAY_EXTRA))] + [whole((ROWS, PAY))] * (SIDE - 1)
        + [pl.BlockSpec((ROWS, WIDE), lambda i, sc: (sc[at + 1] + BLOCKS, 0))]
        + [pl.BlockSpec((1, WIDE, CHUNK), lambda i, sc: (i, 0, 0))]
        + adapter_specs(at, (CHUNK, RANK))
        + adapter_specs(at, (RANK, CHUNK))
        + [slot_spec(at + 1, WIDE), slot_spec(at + 1, RANK)]
        + [keep] * 3,
        out_specs=[whole((ROWS, PAY_EXTRA)), whole((ROWS, PAY)),
                   slot_spec(at + 2, RANK), slot_spec(at + 2, RANK), slot_spec(at + 2, CHUNK)],
        scratch_shapes=[pltpu.VMEM((SIDE, ROWS, CHUNK), BF), pltpu.VMEM((ROWS, WIDE), F32)],
    )
    like = lambda v: jax.ShapeDtypeStruct(v.shape, v.dtype)
    return pl.pallas_call(
        functools.partial(backward_kernel, tick),
        grid_spec=grid_spec,
        out_shape=[jax.ShapeDtypeStruct((ROWS, PAY_EXTRA), BF), jax.ShapeDtypeStruct((ROWS, PAY), BF),
                   like(q_buf), like(zr_buf), like(e_buf)],
        input_output_aliases={17: 2, 18: 3, 19: 4},
        compiler_params=PARAMS,
        name="backward_stage",
    )(table, *payloads, cg, w, *a_lib, *b_lib, g_buf, z_buf, q_buf, zr_buf, e_buf)


def gradients(info, x_in, h_buf, q_buf, zr_buf, e_buf):
    flat = lambda v: v.reshape(-1, v.shape[-1])
    total = BLOCKS * ROWS
    grid_spec = pltpu.PrefetchScalarGridSpec(
        num_scalar_prefetch=1,
        grid=(LAYERS,),
        in_specs=[whole((total, CHUNK)), whole((total, CHUNK)), whole((total, RANK)), whole((total, RANK)),
                  whole((total, CHUNK))],
        out_specs=[pl.BlockSpec((1, 1, CHUNK, RANK), lambda i, sc: (i, 0, 0, 0)),
                   pl.BlockSpec((1, 1, RANK, CHUNK), lambda i, sc: (i, 0, 0, 0))],
    )
    return pl.pallas_call(
        gradient_kernel,
        grid_spec=grid_spec,
        out_shape=[jax.ShapeDtypeStruct((LAYERS, 1, CHUNK, RANK), BF),
                   jax.ShapeDtypeStruct((LAYERS, 1, RANK, CHUNK), BF)],
        compiler_params=PARAMS,
        name="style_gradients",
    )(info, x_in, flat(h_buf), flat(q_buf), flat(zr_buf), flat(e_buf))


def tick_tables(section, slots, a, b):
    def table(ticks, mb, save, first):
        cols = [slots[jnp.clip(mb, 0, BLOCKS - 1)], jnp.clip(mb, 0, BLOCKS - 1),
                jnp.where((save >= 0) & (save < BLOCKS), save, BLOCKS), first.astype(jnp.int32),
                jnp.broadcast_to(a, ticks.shape), jnp.broadcast_to(b, ticks.shape),
                jnp.zeros_like(ticks), jnp.zeros_like(ticks)]
        return jnp.stack(cols, axis=1).astype(jnp.int32).reshape(-1)

    ticks = jnp.arange(2 * LAYERS + BLOCKS, dtype=jnp.int32)
    start = section == 0
    boundary = jnp.where(start, LAYERS, section)
    fwd_mb = ticks - jnp.where(start & (ticks >= LAYERS), LAYERS, section)
    fwd = table(ticks, fwd_mb, ticks - boundary, start & (ticks < LAYERS))
    bwd = table(ticks, ticks - 2 * LAYERS + boundary, ticks - 2 * LAYERS + section,
                jnp.broadcast_to(start, ticks.shape))
    return fwd, bwd


def body(x_in, cotangent, weights, down_weight_store, lib_b, style_ids, slot_of):
    section = lax.axis_index("section")
    tp = lax.axis_index("tp")
    core, z_pos, y_pos = section % 2, tp // SIDE, tp % SIDE
    a = jnp.where(core == 0, y_pos, z_pos)
    b = jnp.where(core == 0, z_pos, y_pos)
    flat_ids = style_ids.reshape(-1)
    styles = jnp.arange(slot_of.shape[0], dtype=jnp.int32)
    slots = jnp.sum(jnp.where(flat_ids[:, None] == styles[None, :], slot_of[None, :], 0), axis=1)
    fwd_table, bwd_table = tick_tables(section, slots, a, b)

    with jax.named_scope("weight_blocks"):
        grid4 = weights[0].reshape(SIDE, SIDE, CHUNK, CHUNK)
        pieces = []
        for k in range(SIDE):
            to = lax.rem(a + k, SIDE)
            for_core0 = lax.dynamic_slice_in_dim(grid4, to, 1, 1).reshape(WIDE, CHUNK)
            for_core1 = lax.dynamic_slice_in_dim(grid4, to, 1, 0).reshape(WIDE, CHUNK)
            pieces.append(jnp.where(core == 0, for_core0, for_core1))
        w_own = jnp.stack([pieces[0]] + [send(pieces[k], along_a(k)) for k in range(1, SIDE)])
        w_prev = send(w_own, onward(0))
    with jax.named_scope("ends"):
        ends = jnp.concatenate([x_in, cotangent], axis=0)
        ends_all = jnp.zeros((ends.shape[0], WIDE), BF)
        for k in range(SIDE):
            piece = ends if k == 0 else send(ends, along_b(k))
            ends_all = lax.dynamic_update_slice(ends_all, piece, (0, lax.rem(b - k + SIDE, SIDE) * CHUNK))
    with jax.named_scope("adapters"):
        a_own = lax.all_to_all(down_weight_store, "section", split_axis=1, concat_axis=0, tiled=True)[:, 0]
        b_own = lax.all_to_all(lib_b, "section", split_axis=1, concat_axis=0, tiled=True)[:, 0]
        a_lib = [a_own] + [send(a_own, along_b(k)) for k in range(1, SIDE)]
        b_lib = [send(b_own, onward(k)) for k in range(SIDE)]

    fwd_in = [jnp.zeros((ROWS, PAY), BF)] * SIDE
    bwd_in = [jnp.zeros((ROWS, PAY_EXTRA), BF)] + [jnp.zeros((ROWS, PAY), BF)] * (SIDE - 1)
    buffer = lambda columns, dtype: jnp.zeros((BLOCKS + 1, ROWS, columns), dtype)
    g_buf, z_buf, h_buf = buffer(WIDE, F32), buffer(RANK, BF), buffer(CHUNK, BF)
    q_buf, zr_buf, e_buf = buffer(RANK, BF), buffer(RANK, BF), buffer(CHUNK, BF)
    for tick in range(2 * LAYERS + BLOCKS):
        if tick < LAYERS + BLOCKS:
            with jax.named_scope("forward"):
                pay, g_buf, z_buf, h_buf = forward_tick(
                    tick, fwd_table, fwd_in, ends_all, w_own, a_lib, b_lib, g_buf, z_buf, h_buf)
                if tick < LAYERS + BLOCKS - 1:
                    fwd_in = [send(pay, onward(k)) for k in range(SIDE)]
        if tick >= LAYERS:
            with jax.named_scope("backward"):
                pay0, pay, q_buf, zr_buf, e_buf = backward_tick(
                    tick, bwd_table, bwd_in, ends_all, w_prev, a_lib, b_lib, g_buf, z_buf, q_buf, zr_buf, e_buf)
                if tick < 2 * LAYERS + BLOCKS - 1:
                    bwd_in = [send(pay0, backward(0))] + [send(pay, backward(k)) for k in range(1, SIDE)]
    info = jnp.concatenate([flat_ids, section[None]]).astype(jnp.int32)
    with jax.named_scope("gradients"):
        grad_a, grad_b = gradients(info, x_in, h_buf, q_buf, zr_buf, e_buf)
    return grad_a, grad_b


def solution(mesh):
    in_specs = (
        P(None, "tp"),
        P(None, "tp"),
        P("section", None, "tp"),
        P("section", None, "tp", None),
        P("section", None, None, "tp"),
        P(),
        P(),
    )
    out_specs = (P(None, "section", "tp", None), P(None, "section", None, "tp"))
    return jax.shard_map(body, mesh=mesh, in_specs=in_specs, out_specs=out_specs, check_vma=False)
```

time: 1380 us -> 635 us (0.46)
  the two profiles are of different devices: /device:TPU:15 before, /device:TPU:1 now
where the time goes in v1:
time: 635 us; the launch traced here: 624 us
  waiting for transfers between devices  208 us (33%)
  starting transfers between devices  204 us (32%)
  Pallas kernels  173 us (27%)
  local copies, waits for them, and re-layouts  28.8 us (5%)
  other arithmetic  8.25 us (1%)
    ppermute x134, starting transfers between devices, send(): return lax.ppermute(value, ('section', 'tp'), pairs)  193 us
    ppermute x134, waiting for transfers between devices, send(): return lax.ppermute(value, ('section', 'tp'), pairs)  146 us
    pallas_call x16, Pallas kernels, backward_tick(): pl.pallas_call(functools.partial(backward_kernel, tick), grid_spec=grid_s...  87.5 us
    pallas_call x16, Pallas kernels, forward_tick(): pl.pallas_call(functools.partial(forward_kernel, tick), grid_spec=grid_sp...  80.8 us
    all_to_all x1, waiting for transfers between devices, body(): lax.all_to_all(lib_b, 'section', split_axis=1, concat_axis=0, tiled=True)  56.9 us
    unnamed x79, local copies, waits for them, and re-layouts  16 us
  transfers between devices with their start and end apart: 136, of which 52 were waited for; matrix products, arithmetic and copies ran while one was open for 2% of the time, Pallas kernels for 19%

profile of v1, /device:TPU:1, one launch (start us, length us, event | category | flops | bytes accessed | tf_op | source)
XLA Modules:
  0.0 624.1 jit_solution(624687908675483927)
XLA Ops:
  5.4 4.7 collective-permute-start.5
  11.9 23.9 %collective-permute-done.5 = bf16[1536,384]{1,0:T(8,128)(2,1)S(1)} collective-permute-done((bf16[1536,384]{1,0:T(8,128)(2,1)S(1)}, bf16[1536,384]{1,0:T(8,128)(2,1)S(1)}, u32[]{:S(2)}, u32[]{:S(2)}) %collective-permute-start.5) | collective-permute-done | bytes 1179680 | tf_op jit(solution)/shard_map/weight_blocks/ppermute | solution.py:50
  50.3 56.9 %all-to-all-done.1 = bf16[1,8,128,384]{3,2,0,1:T(8,128)(2,1)} async-done(((bf16[1,8,128,384]{3,2,0,1:T(8,128)(2,1)}), bf16[1,8,128,384]{3,2,0,1:T(8,128)(2,1)}, u32[]{:S(2)}, u32[]{:S(2)}) %all-to-all-start.1) | async-done | bytes 786464 | tf_op jit(solution)/shard_map/adapters/all_to_all | solution.py:298
  109.9 6.9 %all-to-all-start = ((bf16[1,8,384,128]{3,2,0,1:T(8,128)(2,1)}), bf16[1,8,384,128]{3,2,0,1:T(8,128)(2,1)S(1)}, u32[]{:S(2)}, u32[]{:S(2)}) async-start(bf16[1,8,384,128]{3,2,0,1:T(8,128)(2,1)} %bitcast.81), calls=%async_computation | async-start | bytes 1572864 | tf_op jit(solution)/shard_map/adapters/all_to_all | solution.py:297
  119.4 11.8 %collective-permute-done = bf16[512,384]{1,0:T(8,128)(2,1)} collective-permute-done((bf16[512,384]{1,0:T(8,128)(2,1)S(1)}, bf16[512,384]{1,0:T(8,128)(2,1)}, u32[]{:S(2)}, u32[]{:S(2)}) %collective-permute-start) | collective-permute-done | bytes 393248 | tf_op jit(solution)/shard_map/ends/ppermute | solution.py:50
  131.2 13.2 %collective-permute-start.9 = (bf16[8,128,384]{2,1,0:T(8,128)(2,1)}, bf16[8,128,384]{2,1,0:T(8,128)(2,1)}, u32[]{:S(2)}, u32[]{:S(2)}) collective-permute-start(bf16[8,128,384]{2,1,0:T(8,128)(2,1)} %bitcast.18), channel_id=1, source_target_pairs={{0,16},{1,17},{2,18},{3,19},{4,20},{5,21},{6,22},{7,23},{8,24},{9,... | collective-permute-start | bytes 2359304 | tf_op jit(solution)/shard_map/adapters/ppermute | solution.py:50
  144.4 5.8 all-to-all-done
  163.9 8.3 %collective-permute-done.6.a1 = bf16[8,384,128]{2,1,0:T(8,128)(2,1)} collective-permute-done((bf16[8,384,128]{2,1,0:T(8,128)(2,1)S(1)}, bf16[8,384,128]{2,1,0:T(8,128)(2,1)}, u32[]{:S(2)}, u32[]{:S(2)}) %collective-permute-start.6) | collective-permute-done | bytes 786464 | tf_op jit(solution)/shard_map/adapters/ppermute | solution.py:50
  172.5 4.9 forward_stage.16
  185.0 4.9 forward_stage.17
  200.0 4.9 forward_stage.18
  216.0 4.9 forward_stage.19
  231.0 4.9 forward_stage.20
  236.0 5.2 collective-permute-start.32
  248.4 4.9 forward_stage.21
  263.4 4.9 forward_stage.22
  279.4 5.6 forward_stage.23
  301.5 5.7 forward_stage.24
  307.9 5.5 collective-permute-start.48
  323.3 5.7 backward_stage.16
  336.8 5.1 forward_stage.25
  346.1 5.4 backward_stage.17
  352.8 4.6 collective-permute-start.80
  358.6 4.9 forward_stage.26
  367.9 5.4 backward_stage.18
  381.0 4.9 forward_stage.27
  389.3 5.4 backward_stage.19
  402.6 4.9 forward_stage.28
  412.4 5.4 backward_stage.20
  425.4 4.9 forward_stage.29
  435.3 5.4 backward_stage.21
  442.3 4.5 collective-permute-start.96
  448.8 4.9 forward_stage.30
  456.8 5.4 backward_stage.22
  472.0 5.6 forward_stage.31
  478.0 5.4 backward_stage.23
  489.7 4.7 collective-permute-done.104.q2
  495.4 5.4 backward_stage.24
  506.2 4.9 collective-permute-done.108.q2
  512.2 5.4 backward_stage.25
  528.7 5.4 backward_stage.26
  541.0 4.4 collective-permute-done.116.q2
  545.8 5.4 backward_stage.27
  562.4 5.4 backward_stage.28
  579.3 5.4 backward_stage.29
  596.1 5.4 backward_stage.30
  612.9 6.1 backward_stage.31
  619.0 4.7 style_gradients.1
  (380 shorter events, 283.8 us)
Async XLA Ops:
  5.4 30.4 %collective-permute-start.5 = (bf16[1536,384]{1,0:T(8,128)(2,1)S(1)}, bf16[1536,384]{1,0:T(8,128)(2,1)S(1)}, u32[]{:S(2)}, u32[]{:S(2)}) collective-permute-start(bf16[1536,384]{1,0:T(8,128)(2,1)S(1)} %bitcast_select_fusion), channel_id=1, source_target_pairs={{0,3},{1,0},{2,1},{3,2},{4,7},{5,4},{6,5},{7,6},{8,11},{9,8},{10,9... | collective-permute-start | bytes 3538952 | tf_op jit(solution)/shard_map/weight_blocks/ppermute | solution.py:50
  10.4 25.4 %collective-permute-start.4 = (bf16[1536,384]{1,0:T(8,128)(2,1)S(1)}, bf16[1536,384]{1,0:T(8,128)(2,1)S(1)}, u32[]{:S(2)}, u32[]{:S(2)}) collective-permute-start(bf16[1536,384]{1,0:T(8,128)(2,1)S(1)} %bitcast_select_fusion.1), channel_id=1, source_target_pairs={{0,2},{1,3},{2,0},{3,1},{4,6},{5,7},{6,4},{7,5},{8,10},{9,11},{10,... | collective-permute-start | bytes 3538952 | tf_op jit(solution)/shard_map/weight_blocks/ppermute | solution.py:50
  10.9 29.1 %collective-permute-start.3 = (bf16[1536,384]{1,0:T(8,128)(2,1)S(1)}, bf16[1536,384]{1,0:T(8,128)(2,1)S(1)}, u32[]{:S(2)}, u32[]{:S(2)}) collective-permute-start(bf16[1536,384]{1,0:T(8,128)(2,1)S(1)} %bitcast_select_fusion.2), channel_id=1, source_target_pairs={{0,1},{1,2},{2,3},{3,0},{4,5},{5,6},{6,7},{7,4},{8,9},{9,10},{10,1... | collective-permute-start | bytes 3538952 | tf_op jit(solution)/shard_map/weight_blocks/ppermute | solution.py:50
  42.5 276.1 %collective-permute-start.73 = (bf16[4,1536,384]{2,1,0:T(8,128)(2,1)}, bf16[4,1536,384]{2,1,0:T(8,128)(2,1)}, u32[]{:S(2)}, u32[]{:S(2)}) collective-permute-start(bf16[4,1536,384]{2,1,0:T(8,128)(2,1)} %pad_maximum_fusion.w), channel_id=1, source_target_pairs={{0,16},{1,17},{2,18},{3,19},{4,20},{5,21},{6,22},{7,23},{8,24},{9,... | collective-permute-start | bytes 14155784 | tf_op jit(solution)/shard_map/weight_blocks/ppermute | solution.py:50
  44.4 62.7 %all-to-all-start.1 = ((bf16[1,8,128,384]{3,2,0,1:T(8,128)(2,1)}), bf16[1,8,128,384]{3,2,0,1:T(8,128)(2,1)}, u32[]{:S(2)}, u32[]{:S(2)}) async-start(bf16[1,8,128,384]{3,2,0,1:T(8,128)(2,1)} %bitcast.17), calls=%async_computation.1 | async-start | bytes 1572864 | tf_op jit(solution)/shard_map/adapters/all_to_all | solution.py:298
  48.7 60.5 %collective-permute-start.2 = (bf16[512,384]{1,0:T(8,128)(2,1)S(1)}, bf16[512,384]{1,0:T(8,128)(2,1)S(1)}, u32[]{:S(2)}, u32[]{:S(2)}) collective-permute-start(bf16[512,384]{1,0:T(8,128)(2,1)S(1)} %constant_dynamic-update-slice_fusion), channel_id=1, source_target_pairs={{0,12},{1,13},{2,14},{3,15},{4,0},{5,1},{6,2},{7,3},{8,4},{9,5},{1... | collective-permute-start | bytes 1179656 | tf_op jit(solution)/shard_map/ends/ppermute | solution.py:50
  49.9 66.9 %collective-permute-start.1 = (bf16[512,384]{1,0:T(8,128)(2,1)S(1)}, bf16[512,384]{1,0:T(8,128)(2,1)}, u32[]{:S(2)}, u32[]{:S(2)}) collective-permute-start(bf16[512,384]{1,0:T(8,128)(2,1)S(1)} %constant_dynamic-update-slice_fusion), channel_id=1, source_target_pairs={{0,8},{1,9},{2,10},{3,11},{4,12},{5,13},{6,14},{7,15},{8,0},{9,1},... | collective-permute-start | bytes 1179656 | tf_op jit(solution)/shard_map/ends/ppermute | solution.py:50
  107.1 43.1 %collective-permute-start.12 = (bf16[8,128,384]{2,1,0:T(8,128)(2,1)}, bf16[8,128,384]{2,1,0:T(8,128)(2,1)S(1)}, u32[]{:S(2)}, u32[]{:S(2)}) collective-permute-start(bf16[8,128,384]{2,1,0:T(8,128)(2,1)} %bitcast.18), channel_id=1, source_target_pairs={{0,19},{1,16},{2,17},{3,18},{4,23},{5,20},{6,21},{7,22},{8,27},{9,... | collective-permute-start | bytes 2359304 | tf_op jit(solution)/shard_map/adapters/ppermute | solution.py:50
  109.1 41.2 %collective-permute-start.11 = (bf16[8,128,384]{2,1,0:T(8,128)(2,1)}, bf16[8,128,384]{2,1,0:T(8,128)(2,1)S(1)}, u32[]{:S(2)}, u32[]{:S(2)}) collective-permute-start(bf16[8,128,384]{2,1,0:T(8,128)(2,1)} %bitcast.18), channel_id=1, source_target_pairs={{0,18},{1,19},{2,16},{3,17},{4,22},{5,23},{6,20},{7,21},{8,26},{9,... | collective-permute-start | bytes 2359304 | tf_op jit(solution)/shard_map/adapters/ppermute | solution.py:50
  109.1 42.2 %collective-permute-start.10 = (bf16[8,128,384]{2,1,0:T(8,128)(2,1)}, bf16[8,128,384]{2,1,0:T(8,128)(2,1)S(1)}, u32[]{:S(2)}, u32[]{:S(2)}) collective-permute-start(bf16[8,128,384]{2,1,0:T(8,128)(2,1)} %bitcast.18), channel_id=1, source_target_pairs={{0,17},{1,18},{2,19},{3,16},{4,21},{5,22},{6,23},{7,20},{8,25},{9,... | collective-permute-start | bytes 2359304 | tf_op jit(solution)/shard_map/adapters/ppermute | solution.py:50
  109.9 40.3 %all-to-all-start = ((bf16[1,8,384,128]{3,2,0,1:T(8,128)(2,1)}), bf16[1,8,384,128]{3,2,0,1:T(8,128)(2,1)S(1)}, u32[]{:S(2)}, u32[]{:S(2)}) async-start(bf16[1,8,384,128]{3,2,0,1:T(8,128)(2,1)} %bitcast.81), calls=%async_computation | async-start | bytes 1572864 | tf_op jit(solution)/shard_map/adapters/all_to_all | solution.py:297
  116.8 14.4 %collective-permute-start = (bf16[512,384]{1,0:T(8,128)(2,1)S(1)}, bf16[512,384]{1,0:T(8,128)(2,1)}, u32[]{:S(2)}, u32[]{:S(2)}) collective-permute-start(bf16[512,384]{1,0:T(8,128)(2,1)S(1)} %constant_dynamic-update-slice_fusion), channel_id=1, source_target_pairs={{0,4},{1,5},{2,6},{3,7},{4,8},{5,9},{6,10},{7,11},{8,12},{9,13},{1... | collective-permute-start | bytes 1179656 | tf_op jit(solution)/shard_map/ends/ppermute | solution.py:50
  131.2 28.5 %collective-permute-start.9 = (bf16[8,128,384]{2,1,0:T(8,128)(2,1)}, bf16[8,128,384]{2,1,0:T(8,128)(2,1)}, u32[]{:S(2)}, u32[]{:S(2)}) collective-permute-start(bf16[8,128,384]{2,1,0:T(8,128)(2,1)} %bitcast.18), channel_id=1, source_target_pairs={{0,16},{1,17},{2,18},{3,19},{4,20},{5,21},{6,22},{7,23},{8,24},{9,... | collective-permute-start | bytes 2359304 | tf_op jit(solution)/shard_map/adapters/ppermute | solution.py:50
  151.3 12.6 %collective-permute-start.7 = (bf16[8,384,128]{2,1,0:T(8,128)(2,1)S(1)}, bf16[8,384,128]{2,1,0:T(8,128)(2,1)}, u32[]{:S(2)}, u32[]{:S(2)}) collective-permute-start(bf16[8,384,128]{2,1,0:T(8,128)(2,1)S(1)} %bitcast.35), channel_id=1, source_target_pairs={{0,8},{1,9},{2,10},{3,11},{4,12},{5,13},{6,14},{7,15},{8,0},{9,1},... | collective-permute-start | bytes 2359304 | tf_op jit(solution)/shard_map/adapters/ppermute | solution.py:50
  152.2 20.0 %collective-permute-start.6 = (bf16[8,384,128]{2,1,0:T(8,128)(2,1)S(1)}, bf16[8,384,128]{2,1,0:T(8,128)(2,1)}, u32[]{:S(2)}, u32[]{:S(2)}) collective-permute-start(bf16[8,384,128]{2,1,0:T(8,128)(2,1)S(1)} %bitcast.36), channel_id=1, source_target_pairs={{0,4},{1,5},{2,6},{3,7},{4,8},{5,9},{6,10},{7,11},{8,12},{9,13},{1... | collective-permute-start | bytes 2359304 | tf_op jit(solution)/shard_map/adapters/ppermute | solution.py:50
  307.9 23.8 %collective-permute-start.48 = (bf16[32,2048]{1,0:T(8,128)(2,1)}, bf16[32,2048]{1,0:T(8,128)(2,1)}, u32[]{:S(2)}, u32[]{:S(2)}) collective-permute-start(bf16[32,2048]{1,0:T(8,128)(2,1)} %get-tuple-element.175), channel_id=1, source_target_pairs={{0,19},{1,16},{2,17},{3,18},{4,23},{5,20},{6,21},{7,22},{8,27},{9,... | collective-permute-start | bytes 393224 | tf_op jit(solution)/shard_map/forward/ppermute | solution.py:50
  313.4 20.7 %collective-permute-start.47 = (bf16[32,2048]{1,0:T(8,128)(2,1)}, bf16[32,2048]{1,0:T(8,128)(2,1)}, u32[]{:S(2)}, u32[]{:S(2)}) collective-permute-start(bf16[32,2048]{1,0:T(8,128)(2,1)} %get-tuple-element.175), channel_id=1, source_target_pairs={{0,18},{1,19},{2,16},{3,17},{4,22},{5,23},{6,20},{7,21},{8,26},{9,... | collective-permute-start | bytes 393224 | tf_op jit(solution)/shard_map/forward/ppermute | solution.py:50
  313.4 22.6 %collective-permute-start.46 = (bf16[32,2048]{1,0:T(8,128)(2,1)}, bf16[32,2048]{1,0:T(8,128)(2,1)}, u32[]{:S(2)}, u32[]{:S(2)}) collective-permute-start(bf16[32,2048]{1,0:T(8,128)(2,1)} %get-tuple-element.175), channel_id=1, source_target_pairs={{0,17},{1,18},{2,19},{3,16},{4,21},{5,22},{6,23},{7,20},{8,25},{9,... | collective-permute-start | bytes 393224 | tf_op jit(solution)/shard_map/forward/ppermute | solution.py:50
  318.6 18.2 %collective-permute-start.45 = (bf16[32,2048]{1,0:T(8,128)(2,1)}, bf16[32,2048]{1,0:T(8,128)(2,1)S(1)}, u32[]{:S(2)}, u32[]{:S(2)}) collective-permute-start(bf16[32,2048]{1,0:T(8,128)(2,1)} %get-tuple-element.175), channel_id=1, source_target_pairs={{0,16},{1,17},{2,18},{3,19},{4,20},{5,21},{6,22},{7,23},{8,24},{9,... | collective-permute-start | bytes 393224 | tf_op jit(solution)/shard_map/forward/ppermute | solution.py:50
  329.0 13.5 %collective-permute-start.77 = (bf16[32,2048]{1,0:T(8,128)(2,1)S(1)}, bf16[32,2048]{1,0:T(8,128)(2,1)S(1)}, u32[]{:S(2)}, u32[]{:S(2)}) collective-permute-start(bf16[32,2048]{1,0:T(8,128)(2,1)S(1)} %get-tuple-element.205), channel_id=1, source_target_pairs={{0,115},{1,112},{2,113},{3,114},{4,119},{5,116},{6,117},{7,118},{8... | collective-permute-start | bytes 393224 | tf_op jit(solution)/shard_map/backward/ppermute | solution.py:50
  331.7 12.5 %collective-permute-start.76 = (bf16[32,2048]{1,0:T(8,128)(2,1)S(1)}, bf16[32,2048]{1,0:T(8,128)(2,1)S(1)}, u32[]{:S(2)}, u32[]{:S(2)}) collective-permute-start(bf16[32,2048]{1,0:T(8,128)(2,1)S(1)} %get-tuple-element.205), channel_id=1, source_target_pairs={{0,114},{1,115},{2,112},{3,113},{4,118},{5,119},{6,116},{7,117},{8... | collective-permute-start | bytes 393224 | tf_op jit(solution)/shard_map/backward/ppermute | solution.py:50
  342.5 14.9 %collective-permute-start.51 = (bf16[32,2048]{1,0:T(8,128)(2,1)S(1)}, bf16[32,2048]{1,0:T(8,128)(2,1)S(1)}, u32[]{:S(2)}, u32[]{:S(2)}) collective-permute-start(bf16[32,2048]{1,0:T(8,128)(2,1)S(1)} %get-tuple-element.179), channel_id=1, source_target_pairs={{0,18},{1,19},{2,16},{3,17},{4,22},{5,23},{6,20},{7,21},{8,26},{9,... | collective-permute-start | bytes 393224 | tf_op jit(solution)/shard_map/forward/ppermute | solution.py:50
  344.2 13.2 %collective-permute-start.50 = (bf16[32,2048]{1,0:T(8,128)(2,1)S(1)}, bf16[32,2048]{1,0:T(8,128)(2,1)S(1)}, u32[]{:S(2)}, u32[]{:S(2)}) collective-permute-start(bf16[32,2048]{1,0:T(8,128)(2,1)S(1)} %get-tuple-element.179), channel_id=1, source_target_pairs={{0,17},{1,18},{2,19},{3,16},{4,21},{5,22},{6,23},{7,20},{8,25},{9,... | collective-permute-start | bytes 393224 | tf_op jit(solution)/shard_map/forward/ppermute | solution.py:50
  346.0 12.6 %collective-permute-start.49 = (bf16[32,2048]{1,0:T(8,128)(2,1)S(1)}, bf16[32,2048]{1,0:T(8,128)(2,1)S(1)}, u32[]{:S(2)}, u32[]{:S(2)}) collective-permute-start(bf16[32,2048]{1,0:T(8,128)(2,1)S(1)} %get-tuple-element.179), channel_id=1, source_target_pairs={{0,16},{1,17},{2,18},{3,19},{4,20},{5,21},{6,22},{7,23},{8,24},{9,... | collective-permute-start | bytes 393224 | tf_op jit(solution)/shard_map/forward/ppermute | solution.py:50
  351.5 13.8 %collective-permute-start.81 = (bf16[32,2048]{1,0:T(8,128)(2,1)S(1)}, bf16[32,2048]{1,0:T(8,128)(2,1)S(1)}, u32[]{:S(2)}, u32[]{:S(2)}) collective-permute-start(bf16[32,2048]{1,0:T(8,128)(2,1)S(1)} %get-tuple-element.210), channel_id=1, source_target_pairs={{0,115},{1,112},{2,113},{3,114},{4,119},{5,116},{6,117},{7,118},{8... | collective-permute-start | bytes 393224 | tf_op jit(solution)/shard_map/backward/ppermute | solution.py:50
  352.8 14.0 %collective-permute-start.80 = (bf16[32,2048]{1,0:T(8,128)(2,1)S(1)}, bf16[32,2048]{1,0:T(8,128)(2,1)S(1)}, u32[]{:S(2)}, u32[]{:S(2)}) collective-permute-start(bf16[32,2048]{1,0:T(8,128)(2,1)S(1)} %get-tuple-element.210), channel_id=1, source_target_pairs={{0,114},{1,115},{2,112},{3,113},{4,118},{5,119},{6,116},{7,117},{8... | collective-permute-start | bytes 393224 | tf_op jit(solution)/shard_map/backward/ppermute | solution.py:50
  365.3 13.3 %collective-permute-start.55 = (bf16[32,2048]{1,0:T(8,128)(2,1)S(1)}, bf16[32,2048]{1,0:T(8,128)(2,1)S(1)}, u32[]{:S(2)}, u32[]{:S(2)}) collective-permute-start(bf16[32,2048]{1,0:T(8,128)(2,1)S(1)} %get-tuple-element.183), channel_id=1, source_target_pairs={{0,18},{1,19},{2,16},{3,17},{4,22},{5,23},{6,20},{7,21},{8,26},{9,... | collective-permute-start | bytes 393224 | tf_op jit(solution)/shard_map/forward/ppermute | solution.py:50
  366.8 12.9 %collective-permute-start.54 = (bf16[32,2048]{1,0:T(8,128)(2,1)S(1)}, bf16[32,2048]{1,0:T(8,128)(2,1)S(1)}, u32[]{:S(2)}, u32[]{:S(2)}) collective-permute-start(bf16[32,2048]{1,0:T(8,128)(2,1)S(1)} %get-tuple-element.183), channel_id=1, source_target_pairs={{0,17},{1,18},{2,19},{3,16},{4,21},{5,22},{6,23},{7,20},{8,25},{9,... | collective-permute-start | bytes 393224 | tf_op jit(solution)/shard_map/forward/ppermute | solution.py:50
  367.3 13.8 %collective-permute-start.53 = (bf16[32,2048]{1,0:T(8,128)(2,1)S(1)}, bf16[32,2048]{1,0:T(8,128)(2,1)S(1)}, u32[]{:S(2)}, u32[]{:S(2)}) collective-permute-start(bf16[32,2048]{1,0:T(8,128)(2,1)S(1)} %get-tuple-element.183), channel_id=1, source_target_pairs={{0,16},{1,17},{2,18},{3,19},{4,20},{5,21},{6,22},{7,23},{8,24},{9,... | collective-permute-start | bytes 393224 | tf_op jit(solution)/shard_map/forward/ppermute | solution.py:50
  373.4 14.6 %collective-permute-start.85 = (bf16[32,2048]{1,0:T(8,128)(2,1)S(1)}, bf16[32,2048]{1,0:T(8,128)(2,1)S(1)}, u32[]{:S(2)}, u32[]{:S(2)}) collective-permute-start(bf16[32,2048]{1,0:T(8,128)(2,1)S(1)} %get-tuple-element.215), channel_id=1, source_target_pairs={{0,115},{1,112},{2,113},{3,114},{4,119},{5,116},{6,117},{7,118},{8... | collective-permute-start | bytes 393224 | tf_op jit(solution)/shard_map/backward/ppermute | solution.py:50
  374.4 14.4 %collective-permute-start.84 = (bf16[32,2048]{1,0:T(8,128)(2,1)S(1)}, bf16[32,2048]{1,0:T(8,128)(2,1)S(1)}, u32[]{:S(2)}, u32[]{:S(2)}) collective-permute-start(bf16[32,2048]{1,0:T(8,128)(2,1)S(1)} %get-tuple-element.215), channel_id=1, source_target_pairs={{0,114},{1,115},{2,112},{3,113},{4,118},{5,119},{6,116},{7,117},{8... | collective-permute-start | bytes 393224 | tf_op jit(solution)/shard_map/backward/ppermute | solution.py:50
  388.0 13.0 %collective-permute-start.59 = (bf16[32,2048]{1,0:T(8,128)(2,1)S(1)}, bf16[32,2048]{1,0:T(8,128)(2,1)S(1)}, u32[]{:S(2)}, u32[]{:S(2)}) collective-permute-start(bf16[32,2048]{1,0:T(8,128)(2,1)S(1)} %get-tuple-element.187), channel_id=1, source_target_pairs={{0,18},{1,19},{2,16},{3,17},{4,22},{5,23},{6,20},{7,21},{8,26},{9,... | collective-permute-start | bytes 393224 | tf_op jit(solution)/shard_map/forward/ppermute | solution.py:50
  388.8 12.8 %collective-permute-start.58 = (bf16[32,2048]{1,0:T(8,128)(2,1)S(1)}, bf16[32,2048]{1,0:T(8,128)(2,1)S(1)}, u32[]{:S(2)}, u32[]{:S(2)}) collective-permute-start(bf16[32,2048]{1,0:T(8,128)(2,1)S(1)} %get-tuple-element.187), channel_id=1, source_target_pairs={{0,17},{1,18},{2,19},{3,16},{4,21},{5,22},{6,23},{7,20},{8,25},{9,... | collective-permute-start | bytes 393224 | tf_op jit(solution)/shard_map/forward/ppermute | solution.py:50
  389.3 13.3 %collective-permute-start.57 = (bf16[32,2048]{1,0:T(8,128)(2,1)S(1)}, bf16[32,2048]{1,0:T(8,128)(2,1)S(1)}, u32[]{:S(2)}, u32[]{:S(2)}) collective-permute-start(bf16[32,2048]{1,0:T(8,128)(2,1)S(1)} %get-tuple-element.187), channel_id=1, source_target_pairs={{0,16},{1,17},{2,18},{3,19},{4,20},{5,21},{6,22},{7,23},{8,24},{9,... | collective-permute-start | bytes 393224 | tf_op jit(solution)/shard_map/forward/ppermute | solution.py:50
  394.7 16.8 %collective-permute-start.89 = (bf16[32,2048]{1,0:T(8,128)(2,1)S(1)}, bf16[32,2048]{1,0:T(8,128)(2,1)S(1)}, u32[]{:S(2)}, u32[]{:S(2)}) collective-permute-start(bf16[32,2048]{1,0:T(8,128)(2,1)S(1)} %get-tuple-element.220), channel_id=1, source_target_pairs={{0,115},{1,112},{2,113},{3,114},{4,119},{5,116},{6,117},{7,118},{8... | collective-permute-start | bytes 393224 | tf_op jit(solution)/shard_map/backward/ppermute | solution.py:50
  397.1 15.2 %collective-permute-start.88 = (bf16[32,2048]{1,0:T(8,128)(2,1)S(1)}, bf16[32,2048]{1,0:T(8,128)(2,1)S(1)}, u32[]{:S(2)}, u32[]{:S(2)}) collective-permute-start(bf16[32,2048]{1,0:T(8,128)(2,1)S(1)} %get-tuple-element.220), channel_id=1, source_target_pairs={{0,114},{1,115},{2,112},{3,113},{4,118},{5,119},{6,116},{7,117},{8... | collective-permute-start | bytes 393224 | tf_op jit(solution)/shard_map/backward/ppermute | solution.py:50
  412.3 13.0 %collective-permute-start.61 = (bf16[32,2048]{1,0:T(8,128)(2,1)S(1)}, bf16[32,2048]{1,0:T(8,128)(2,1)S(1)}, u32[]{:S(2)}, u32[]{:S(2)}) collective-permute-start(bf16[32,2048]{1,0:T(8,128)(2,1)S(1)} %get-tuple-element.191), channel_id=1, source_target_pairs={{0,16},{1,17},{2,18},{3,19},{4,20},{5,21},{6,22},{7,23},{8,24},{9,... | collective-permute-start | bytes 393224 | tf_op jit(solution)/shard_map/forward/ppermute | solution.py:50
  417.8 15.6 %collective-permute-start.93 = (bf16[32,2048]{1,0:T(8,128)(2,1)S(1)}, bf16[32,2048]{1,0:T(8,128)(2,1)S(1)}, u32[]{:S(2)}, u32[]{:S(2)}) collective-permute-start(bf16[32,2048]{1,0:T(8,128)(2,1)S(1)} %get-tuple-element.225), channel_id=1, source_target_pairs={{0,115},{1,112},{2,113},{3,114},{4,119},{5,116},{6,117},{7,118},{8... | collective-permute-start | bytes 393224 | tf_op jit(solution)/shard_map/backward/ppermute | solution.py:50
  419.3 16.0 %collective-permute-start.90 = (bf16[32,2560]{1,0:T(8,128)(2,1)S(1)}, bf16[32,2560]{1,0:T(8,128)(2,1)S(1)}, u32[]{:S(2)}, u32[]{:S(2)}) collective-permute-start(bf16[32,2560]{1,0:T(8,128)(2,1)S(1)} %get-tuple-element.224), channel_id=1, source_target_pairs={{0,112},{1,113},{2,114},{3,115},{4,116},{5,117},{6,118},{7,119},{8... | collective-permute-start | bytes 491528 | tf_op jit(solution)/shard_map/backward/ppermute | solution.py:50
  433.5 13.4 %collective-permute-start.67 = (bf16[32,2048]{1,0:T(8,128)(2,1)S(1)}, bf16[32,2048]{1,0:T(8,128)(2,1)S(1)}, u32[]{:S(2)}, u32[]{:S(2)}) collective-permute-start(bf16[32,2048]{1,0:T(8,128)(2,1)S(1)} %get-tuple-element.195), channel_id=1, source_target_pairs={{0,18},{1,19},{2,16},{3,17},{4,22},{5,23},{6,20},{7,21},{8,26},{9,... | collective-permute-start | bytes 393224 | tf_op jit(solution)/shard_map/forward/ppermute | solution.py:50
  435.3 12.5 %collective-permute-start.66 = (bf16[32,2048]{1,0:T(8,128)(2,1)S(1)}, bf16[32,2048]{1,0:T(8,128)(2,1)S(1)}, u32[]{:S(2)}, u32[]{:S(2)}) collective-permute-start(bf16[32,2048]{1,0:T(8,128)(2,1)S(1)} %get-tuple-element.195), channel_id=1, source_target_pairs={{0,17},{1,18},{2,19},{3,16},{4,21},{5,22},{6,23},{7,20},{8,25},{9,... | collective-permute-start | bytes 393224 | tf_op jit(solution)/shard_map/forward/ppermute | solution.py:50
  435.3 13.5 %collective-permute-start.65 = (bf16[32,2048]{1,0:T(8,128)(2,1)S(1)}, bf16[32,2048]{1,0:T(8,128)(2,1)S(1)}, u32[]{:S(2)}, u32[]{:S(2)}) collective-permute-start(bf16[32,2048]{1,0:T(8,128)(2,1)S(1)} %get-tuple-element.195), channel_id=1, source_target_pairs={{0,16},{1,17},{2,18},{3,19},{4,20},{5,21},{6,22},{7,23},{8,24},{9,... | collective-permute-start | bytes 393224 | tf_op jit(solution)/shard_map/forward/ppermute | solution.py:50
  440.7 14.1 %collective-permute-start.97 = (bf16[32,2048]{1,0:T(8,128)(2,1)S(1)}, bf16[32,2048]{1,0:T(8,128)(2,1)S(1)}, u32[]{:S(2)}, u32[]{:S(2)}) collective-permute-start(bf16[32,2048]{1,0:T(8,128)(2,1)S(1)} %get-tuple-element.230), channel_id=1, source_target_pairs={{0,115},{1,112},{2,113},{3,114},{4,119},{5,116},{6,117},{7,118},{8... | collective-permute-start | bytes 393224 | tf_op jit(solution)/shard_map/backward/ppermute | solution.py:50
  442.3 14.4 %collective-permute-start.96 = (bf16[32,2048]{1,0:T(8,128)(2,1)S(1)}, bf16[32,2048]{1,0:T(8,128)(2,1)S(1)}, u32[]{:S(2)}, u32[]{:S(2)}) collective-permute-start(bf16[32,2048]{1,0:T(8,128)(2,1)S(1)} %get-tuple-element.230), channel_id=1, source_target_pairs={{0,114},{1,115},{2,112},{3,113},{4,118},{5,119},{6,116},{7,117},{8... | collective-permute-start | bytes 393224 | tf_op jit(solution)/shard_map/backward/ppermute | solution.py:50
  454.8 13.1 %collective-permute-start.71 = (bf16[32,2048]{1,0:T(8,128)(2,1)S(1)}, bf16[32,2048]{1,0:T(8,128)(2,1)S(1)}, u32[]{:S(2)}, u32[]{:S(2)}) collective-permute-start(bf16[32,2048]{1,0:T(8,128)(2,1)S(1)} %get-tuple-element.199), channel_id=1, source_target_pairs={{0,18},{1,19},{2,16},{3,17},{4,22},{5,23},{6,20},{7,21},{8,26},{9,... | collective-permute-start | bytes 393224 | tf_op jit(solution)/shard_map/forward/ppermute | solution.py:50
  456.8 14.6 %collective-permute-start.70 = (bf16[32,2048]{1,0:T(8,128)(2,1)S(1)}, bf16[32,2048]{1,0:T(8,128)(2,1)S(1)}, u32[]{:S(2)}, u32[]{:S(2)}) collective-permute-start(bf16[32,2048]{1,0:T(8,128)(2,1)S(1)} %get-tuple-element.199), channel_id=1, source_target_pairs={{0,17},{1,18},{2,19},{3,16},{4,21},{5,22},{6,23},{7,20},{8,25},{9,... | collective-permute-start | bytes 393224 | tf_op jit(solution)/shard_map/forward/ppermute | solution.py:50
  462.2 15.8 %collective-permute-start.98 = (bf16[32,2560]{1,0:T(8,128)(2,1)S(1)}, bf16[32,2560]{1,0:T(8,128)(2,1)S(1)}, u32[]{:S(2)}, u32[]{:S(2)}) collective-permute-start(bf16[32,2560]{1,0:T(8,128)(2,1)S(1)} %get-tuple-element.234), channel_id=1, source_target_pairs={{0,112},{1,113},{2,114},{3,115},{4,116},{5,117},{6,118},{7,119},{8... | collective-permute-start | bytes 491528 | tf_op jit(solution)/shard_map/backward/ppermute | solution.py:50
  464.0 13.6 %collective-permute-start.101 = (bf16[32,2048]{1,0:T(8,128)(2,1)S(1)}, bf16[32,2048]{1,0:T(8,128)(2,1)S(1)}, u32[]{:S(2)}, u32[]{:S(2)}) collective-permute-start(bf16[32,2048]{1,0:T(8,128)(2,1)S(1)} %get-tuple-element.235), channel_id=1, source_target_pairs={{0,115},{1,112},{2,113},{3,114},{4,119},{5,116},{6,117},{7,118},{8... | collective-permute-start | bytes 393224 | tf_op jit(solution)/shard_map/backward/ppermute | solution.py:50
  (127 other events, 1170.6 us)

commit v2 on v1

v2 whole, which is shorter than its diff:
```python
import functools

import jax
import jax.numpy as jnp
from jax import lax
from jax.experimental import pallas as pl
from jax.experimental.pallas import tpu as pltpu
from jax.sharding import PartitionSpec as P

ADAPTER_SCALE = 0.25
SIDE = 4
LAYERS = 8
BLOCKS = 8
ROWS = 32
TOKENS = BLOCKS * ROWS
RANK = 128
CHUNK = 384
WIDE = SIDE * CHUNK
PAIR = 2 * RANK
Z_AT = WIDE
OWN_AT = WIDE + RANK
PAY = OWN_AT + CHUNK
PAY_EXTRA = PAY + RANK + CHUNK
BF = jnp.bfloat16
F32 = jnp.float32


def along_a(k):
    return lambda x, c, z, y: (x, c, z, y + k) if c == 0 else (x, c, z + k, y)


def along_b(k):
    return lambda x, c, z, y: (x, c, z + k, y) if c == 0 else (x, c, z, y + k)


def onward(k):
    return lambda x, c, z, y: (x, 1, z, y + k) if c == 0 else (x + 1, 0, z + k, y)


def backward(k):
    return lambda x, c, z, y: (x, 0, z + k, y) if c == 1 else (x - 1, 1, z, y + k)


def send(value, target):
    pairs = []
    for sec in range(2 * SIDE):
        for tp in range(SIDE * SIDE):
            x, c, z, y = target(sec // 2, sec % 2, tp // SIDE, tp % SIDE)
            sec_to = (x % SIDE) * 2 + c
            tp_to = (z % SIDE) * SIDE + y % SIDE
            pairs.append((sec * SIDE * SIDE + tp, sec_to * SIDE * SIDE + tp_to))
    return lax.ppermute(value, ("section", "tp"), pairs)


IN_VMEM = pl.BlockSpec(memory_space=pltpu.VMEM)
IN_SMEM = pl.BlockSpec(memory_space=pltpu.SMEM)
ANYWHERE = pl.BlockSpec(memory_space=pl.ANY)
PARAMS = pltpu.CompilerParams(vmem_limit_bytes=24 << 20)


def shaped(*shape, dtype=BF):
    return jax.ShapeDtypeStruct(shape, dtype)


def chunk_at(index):
    return pl.ds(pl.multiple_of(index * CHUNK, CHUNK), CHUNK)


def dot(left, right):
    return jnp.dot(left, right, preferred_element_type=F32)


def dot_nt(left, right):
    return lax.dot_general(left, right, (((1,), (1,)), ((), ())), preferred_element_type=F32)


def dot_tn(left, right):
    return lax.dot_general(left, right, (((0,), (0,)), ((), ())), preferred_element_type=F32)


def gelu_both(y):
    scale = 0.7978845608028654
    square = y * y
    t = jnp.tanh(scale * y * (1.0 + 0.044715 * square))
    half = 0.5 * (1.0 + t)
    slope = half + 0.5 * y * (1.0 - t * t) * scale * (1.0 + 3.0 * 0.044715 * square)
    return y * half, slope


def run_copies(moves, sems):
    copies = [pltpu.make_async_copy(source, target, sems.at[i]) for i, (source, target) in enumerate(moves)]
    for copy in copies:
        copy.start()
    for copy in copies:
        copy.wait()


def copy_kernel(name, kernel, count, out_shape, out_spec, scalars, *operands):
    many = isinstance(out_shape, list)
    return pl.pallas_call(
        kernel,
        in_specs=[IN_SMEM] + [ANYWHERE] * len(operands),
        out_specs=[out_spec] * len(out_shape) if many else out_spec,
        out_shape=out_shape,
        scratch_shapes=[pltpu.SemaphoreType.DMA((count,))],
        compiler_params=PARAMS,
        name=name,
    )(scalars, *operands)


def pack_layers_kernel(a, b, out):
    out[0, :RANK] = a[0, 0].T
    out[0, RANK:] = b[0, 0]


def pack_layers(a, b):
    return pl.pallas_call(
        pack_layers_kernel,
        grid=(LAYERS,),
        in_specs=[pl.BlockSpec((1, 1, CHUNK, RANK), lambda i: (0, i, 0, 0)),
                  pl.BlockSpec((1, 1, RANK, CHUNK), lambda i: (0, lax.rem(i + LAYERS - 1, LAYERS), 0, 0))],
        out_specs=pl.BlockSpec((1, PAIR, CHUNK), lambda i: (i, 0, 0)),
        out_shape=shaped(LAYERS, PAIR, CHUNK),
        compiler_params=PARAMS,
        name="pack_layers",
    )(a, b)


def cut_weights_kernel(sc, w, o0, o1, o2, o3, sems):
    core, a = sc[0], sc[2]
    moves = []
    for k, out in enumerate((o0, o1, o2, o3)):
        to = lax.rem(a + k, SIDE)
        for j in range(SIDE):
            source = jnp.where(core == 0, j * SIDE + to, to * SIDE + j)
            moves.append((w.at[source], out.at[j]))
    run_copies(moves, sems)


def pack_blocks_kernel(sc, x, cot, ab, out, sems):
    moves = [(x, out.at[pl.ds(0, TOKENS)]), (cot, out.at[pl.ds(TOKENS, TOKENS)])]
    for n in range(BLOCKS):
        moves.append((ab.at[sc[8 + n]], out.at[pl.ds(2 * TOKENS + n * PAIR, PAIR)]))
    run_copies(moves, sems)


def settle_weights_kernel(sc, own, w1, w2, w3, out, sems):
    copies = [pltpu.make_async_copy(w, out.at[k + 1], sems.at[k]) for k, w in enumerate((w1, w2, w3))]
    for copy in copies:
        copy.start()
    out[0] = own[...]
    for copy in copies:
        copy.wait()


def settle_weights(scalars, pieces):
    return pl.pallas_call(
        settle_weights_kernel,
        in_specs=[IN_SMEM, IN_VMEM] + [ANYWHERE] * (SIDE - 1),
        out_specs=IN_VMEM,
        out_shape=shaped(SIDE, WIDE, CHUNK),
        scratch_shapes=[pltpu.SemaphoreType.DMA((SIDE - 1,))],
        compiler_params=PARAMS,
        name="settle_weights",
    )(scalars, *pieces)


def settle_blocks_kernel(sc, own, p1, p2, p3, x, cot, ab, sems):
    parts = [(0, x), (TOKENS, cot)]
    copies = []
    for k, piece in enumerate((p1, p2, p3)):
        for i, (start, out) in enumerate(parts):
            copies.append(pltpu.make_async_copy(piece.at[pl.ds(start, TOKENS)], out.at[k + 1], sems.at[k, i]))
        copies.append(pltpu.make_async_copy(piece.at[pl.ds(2 * TOKENS, BLOCKS * PAIR)], ab.at[k + 1], sems.at[k, 2]))
    for copy in copies:
        copy.start()
    for start, out in parts:
        out[0] = own[pl.ds(start, TOKENS)]
    ab[0] = own[pl.ds(2 * TOKENS, BLOCKS * PAIR)]
    for copy in copies:
        copy.wait()


def settle_blocks(scalars, pieces):
    return pl.pallas_call(
        settle_blocks_kernel,
        in_specs=[IN_SMEM, IN_VMEM] + [ANYWHERE] * (SIDE - 1),
        out_specs=[IN_VMEM] * 3,
        out_shape=[shaped(SIDE, TOKENS, CHUNK), shaped(SIDE, TOKENS, CHUNK), shaped(SIDE, BLOCKS * PAIR, CHUNK)],
        scratch_shapes=[pltpu.SemaphoreType.DMA((SIDE - 1, 3))],
        compiler_params=PARAMS,
        name="settle_blocks",
    )(scalars, *pieces)


def settle_previous_kernel(sc, w, out, sems):
    run_copies([(w.at[k], out.at[k]) for k in range(SIDE)], sems)


def transpose_kernel(w, out):
    out[0] = w[0].T


def transposed(w):
    return pl.pallas_call(
        transpose_kernel,
        grid=(SIDE,),
        in_specs=[pl.BlockSpec((1, WIDE, CHUNK), lambda i: (i, 0, 0))],
        out_specs=pl.BlockSpec((1, CHUNK, WIDE), lambda i: (i, 0, 0)),
        out_shape=shaped(SIDE, CHUNK, WIDE),
        compiler_params=PARAMS,
        name="transpose_weights",
    )(w)


def within(index):
    return jnp.clip(index, 0, BLOCKS - 1)


def slot_or_spare(index):
    return jnp.where((index >= 0) & (index < BLOCKS), index, BLOCKS)


def forward_block(tick, section):
    return within(tick - jnp.where((section == 0) & (tick >= LAYERS), LAYERS, section))


def boundary(section):
    return jnp.where(section == 0, LAYERS, section)


def forward_save(tick, section):
    return slot_or_spare(tick - boundary(section))


def backward_block(tick, section):
    return within(tick - 2 * LAYERS + boundary(section))


def backward_save(tick, section):
    return slot_or_spare(tick - 2 * LAYERS + section)


def forward_kernel(tick, sc, p0, p1, p2, p3, rows, w, ab, _g, _z, _h, pay, g_out, z_out, h_out, h_all):
    section, a, b = sc[1], sc[2], sc[3]
    block = forward_block(tick, section)
    own_rows = pl.ds(pl.multiple_of(block * ROWS, ROWS), ROWS)
    down = pl.ds(pl.multiple_of(block * PAIR, PAIR), RANK)
    up = pl.ds(pl.multiple_of(block * PAIR + RANK, RANK), RANK)
    z = sum(p[:, Z_AT:OWN_AT].astype(F32) for p in (p0, p1, p2, p3)).astype(BF)
    z_out[0] = z
    z_part = jnp.zeros((ROWS, RANK), F32)
    for k, p in enumerate((p0, p1, p2, p3)):
        here = chunk_at(lax.rem(b - k + SIDE, SIDE))
        y = sum(q[:, here].astype(F32) for q in (p0, p1, p2, p3))
        value, slope = gelu_both(y + ADAPTER_SCALE * dot(z, ab[k, up]))
        h = (p[:, OWN_AT:PAY].astype(F32) + value).astype(BF)
        if tick < LAYERS:
            h = jnp.where(section == 0, rows[k, own_rows], h)
        h_all[:, here] = h
        g_out[0, :, here] = slope
        z_part = z_part + dot_nt(h, ab[k, down])
        if k == 0:
            h_out[0] = h
            pay[:, OWN_AT:PAY] = h
    pay[:, Z_AT:OWN_AT] = z_part.astype(BF)
    h = h_all[...]
    for k in range(SIDE):
        pay[:, chunk_at(lax.rem(a - k + SIDE, SIDE))] = dot(h, w[k]).astype(BF)


def backward_kernel(tick, sc, q0, q1, q2, q3, rows, wt, ab, slope, z_in,
                    _q, _z, _e, pay0, pay, q_out, z_out, e_out):
    section, b = sc[1], sc[3]
    block = backward_block(tick, section)
    q = sum(p[:, Z_AT:OWN_AT].astype(F32) for p in (q0, q1, q2, q3)).astype(BF)
    q_out[0] = q
    z_out[0] = q0[:, PAY:PAY + RANK]
    e_out[0] = q0[:, PAY + RANK:]
    q_part = jnp.zeros((ROWS, RANK), F32)
    total = jnp.zeros((ROWS, WIDE), F32)
    own_rows = pl.ds(pl.multiple_of(block * ROWS, ROWS), ROWS)
    down = pl.ds(pl.multiple_of(block * PAIR, PAIR), RANK)
    up = pl.ds(pl.multiple_of(block * PAIR + RANK, RANK), RANK)
    for k, p in enumerate((q0, q1, q2, q3)):
        here = chunk_at(lax.rem(b - k + SIDE, SIDE))
        n = sum(r[:, here].astype(F32) for r in (q0, q1, q2, q3))
        g = (p[:, OWN_AT:PAY].astype(F32) + n + dot(q, ab[k, down])).astype(BF)
        g = jnp.where(section == 0, rows[k, own_rows], g)
        e = (slope[0, :, here] * g.astype(F32)).astype(BF)
        q_part = q_part + dot_nt(e, ab[k, up])
        total = total + dot(e, wt[k])
        if k == 0:
            pay[:, OWN_AT:PAY] = g
            pay0[:, OWN_AT:PAY] = g
            pay0[:, PAY + RANK:] = e
    q_part = (ADAPTER_SCALE * q_part).astype(BF)
    pay[:, Z_AT:OWN_AT] = q_part
    pay0[:, Z_AT:OWN_AT] = q_part
    pay0[:, PAY:PAY + RANK] = z_in[0]
    n = total.astype(BF)
    pay[:, :WIDE] = n
    pay0[:, :WIDE] = n


def gradient_kernel(sc, x, h, q, z, e, ga, gb):
    style = pl.program_id(0)
    block = lax.broadcasted_iota(jnp.int32, (TOKENS, 1), 0) // ROWS
    mine = jnp.zeros((TOKENS, 1), F32)
    for n in range(BLOCKS):
        mine = jnp.where((block == n) & (sc[16 + n] == style), 1.0, mine)
    rows = jnp.where(sc[1] == 0, x[...], h[...])
    q_mine = (q[...].astype(F32) * mine).astype(BF)
    z_mine = (z[...].astype(F32) * mine).astype(BF)
    ga[0, 0] = dot_tn(rows, q_mine).astype(BF)
    gb[0, 0] = (ADAPTER_SCALE * dot_tn(z_mine, e[...])).astype(BF)


def slot_spec(slot, tick, columns):
    return pl.BlockSpec((1, ROWS, columns), lambda i, sc: (slot(tick, sc[1]), 0, 0))


def forward_tick(tick, scalars, payloads, rows, w, ab, g_buf, z_buf, h_buf):
    grid_spec = pltpu.PrefetchScalarGridSpec(
        num_scalar_prefetch=1,
        grid=(1,),
        in_specs=[IN_VMEM] * 7 + [ANYWHERE] * 3,
        out_specs=[IN_VMEM] + [slot_spec(forward_save, tick, columns) for columns in (WIDE, RANK, CHUNK)],
        scratch_shapes=[pltpu.VMEM((ROWS, WIDE), BF)],
    )
    return pl.pallas_call(
        functools.partial(forward_kernel, tick),
        grid_spec=grid_spec,
        out_shape=[shaped(ROWS, PAY)] + [shaped(*v.shape, dtype=v.dtype) for v in (g_buf, z_buf, h_buf)],
        input_output_aliases={8: 1, 9: 2, 10: 3},
        compiler_params=PARAMS,
        name="forward_stage",
    )(scalars, *payloads, rows, w, ab, g_buf, z_buf, h_buf)


def backward_tick(tick, scalars, payloads, rows, wt, ab, g_buf, z_buf, q_buf, zr_buf, e_buf):
    grid_spec = pltpu.PrefetchScalarGridSpec(
        num_scalar_prefetch=1,
        grid=(1,),
        in_specs=[IN_VMEM] * 7 + [slot_spec(backward_block, tick, columns) for columns in (WIDE, RANK)]
        + [ANYWHERE] * 3,
        out_specs=[IN_VMEM] * 2 + [slot_spec(backward_save, tick, columns) for columns in (RANK, RANK, CHUNK)],
    )
    return pl.pallas_call(
        functools.partial(backward_kernel, tick),
        grid_spec=grid_spec,
        out_shape=[shaped(ROWS, PAY_EXTRA), shaped(ROWS, PAY)]
        + [shaped(*v.shape, dtype=v.dtype) for v in (q_buf, zr_buf, e_buf)],
        input_output_aliases={10: 2, 11: 3, 12: 4},
        compiler_params=PARAMS,
        name="backward_stage",
    )(scalars, *payloads, rows, wt, ab, g_buf, z_buf, q_buf, zr_buf, e_buf)


def gradients(scalars, x_in, h_buf, q_buf, zr_buf, e_buf):
    flat = lambda v: v.reshape(-1, v.shape[-1])
    whole = lambda columns: pl.BlockSpec((TOKENS, columns), lambda i, sc: (0, 0))
    grid_spec = pltpu.PrefetchScalarGridSpec(
        num_scalar_prefetch=1,
        grid=(LAYERS,),
        in_specs=[whole(CHUNK), whole(CHUNK), whole(RANK), whole(RANK), whole(CHUNK)],
        out_specs=[pl.BlockSpec((1, 1, CHUNK, RANK), lambda i, sc: (i, 0, 0, 0)),
                   pl.BlockSpec((1, 1, RANK, CHUNK), lambda i, sc: (i, 0, 0, 0))],
    )
    return pl.pallas_call(
        gradient_kernel,
        grid_spec=grid_spec,
        out_shape=[shaped(LAYERS, 1, CHUNK, RANK), shaped(LAYERS, 1, RANK, CHUNK)],
        compiler_params=PARAMS,
        name="style_gradients",
    )(scalars, x_in, flat(h_buf), flat(q_buf), flat(zr_buf), flat(e_buf))


def body(x_in, cotangent, weights, down_weight_store, lib_b, style_ids, slot_of):
    section = lax.axis_index("section")
    tp = lax.axis_index("tp")
    core, z_pos, y_pos = section % 2, tp // SIDE, tp % SIDE
    a = jnp.where(core == 0, y_pos, z_pos)
    b = jnp.where(core == 0, z_pos, y_pos)
    flat_ids = style_ids.reshape(-1)
    styles = jnp.arange(slot_of.shape[0], dtype=jnp.int32)
    slots = jnp.sum(jnp.where(flat_ids[:, None] == styles[None, :], slot_of[None, :], 0), axis=1)
    place = jnp.stack([core, section, a, b, 0, 0, 0, 0]).astype(jnp.int32)
    scalars = jnp.concatenate([place, slots, flat_ids])

    with jax.named_scope("adapters"):
        ab_out = pack_layers(down_weight_store, lib_b)
        ab_in = lax.all_to_all(ab_out, "section", split_axis=0, concat_axis=0, tiled=True)
    with jax.named_scope("weight_blocks"):
        cut = copy_kernel("cut_weights", cut_weights_kernel, SIDE * SIDE, [shaped(SIDE, CHUNK, CHUNK)] * SIDE, ANYWHERE,
                          place, weights[0].reshape(SIDE * SIDE, CHUNK, CHUNK))
        cut = [piece.reshape(WIDE, CHUNK) for piece in cut]
        w_pieces = [cut[0]] + [send(cut[k], along_a(k)) for k in range(1, SIDE)]
    with jax.named_scope("blocks"):
        packed = copy_kernel("pack_blocks", pack_blocks_kernel, 2 + BLOCKS, shaped(2 * TOKENS + BLOCKS * PAIR, CHUNK),
                             ANYWHERE, scalars, x_in, cotangent, ab_in)
        block_pieces = [packed] + [send(packed, along_b(k)) for k in range(1, SIDE)]
    with jax.named_scope("weight_blocks"):
        w_pieces[0], _ = lax.optimization_barrier((w_pieces[0], packed))
        w_own = settle_weights(place, w_pieces)
        w_turned = transposed(w_own)
    with jax.named_scope("previous_weights"):
        w_prev = send(w_turned, onward(0))
    with jax.named_scope("blocks"):
        block_pieces[0], _ = lax.optimization_barrier((block_pieces[0], w_turned))
        x_rows, cot_rows, ab = settle_blocks(place, block_pieces)

    first_in = jnp.zeros((ROWS, PAY), BF)
    fwd_in = [first_in] * SIDE
    bwd_in = [jnp.zeros((ROWS, PAY_EXTRA), BF)] + [jnp.zeros((ROWS, PAY), BF)] * (SIDE - 1)
    buffer = lambda columns, dtype: jnp.zeros((BLOCKS + 1, ROWS, columns), dtype)
    g_buf, z_buf, h_buf = buffer(WIDE, F32), buffer(RANK, BF), buffer(CHUNK, BF)
    q_buf, zr_buf, e_buf = buffer(RANK, BF), buffer(RANK, BF), buffer(CHUNK, BF)
    for tick in range(2 * LAYERS + BLOCKS):
        if tick == 4:
            with jax.named_scope("previous_weights"):
                w_prev, fwd_in[0] = lax.optimization_barrier((w_prev, fwd_in[0]))
                w_prev = copy_kernel("settle_previous", settle_previous_kernel, SIDE, shaped(SIDE, CHUNK, WIDE),
                                     IN_VMEM, place, w_prev)
        if tick < LAYERS + BLOCKS:
            with jax.named_scope("forward"):
                pay, g_buf, z_buf, h_buf = forward_tick(
                    tick, place, fwd_in, x_rows, w_own, ab, g_buf, z_buf, h_buf)
                if tick < LAYERS + BLOCKS - 1:
                    fwd_in = [send(pay, onward(k)) for k in range(SIDE)]
        if tick >= LAYERS:
            with jax.named_scope("backward"):
                pay0, pay, q_buf, zr_buf, e_buf = backward_tick(
                    tick, place, bwd_in, cot_rows, w_prev, ab, g_buf, z_buf, q_buf, zr_buf, e_buf)
                if tick < 2 * LAYERS + BLOCKS - 1:
                    bwd_in = [send(pay0, backward(0))] + [send(pay, backward(k)) for k in range(1, SIDE)]
    with jax.named_scope("gradients"):
        grad_a, grad_b = gradients(scalars, x_in, h_buf, q_buf, zr_buf, e_buf)
    return grad_a, grad_b


def solution(mesh):
    in_specs = (
        P(None, "tp"),
        P(None, "tp"),
        P("section", None, "tp"),
        P("section", None, "tp", None),
        P("section", None, None, "tp"),
        P(),
        P(),
    )
    out_specs = (P(None, "section", "tp", None), P(None, "section", None, "tp"))
    return jax.shard_map(body, mesh=mesh, in_specs=in_specs, out_specs=out_specs, check_vma=False)
```

time: 635 us -> 451 us (0.71)
  the two profiles are of different devices: /device:TPU:1 before, /device:TPU:15 now
where the time goes in v2:
time: 451 us; the launch traced here: 442 us
  starting transfers between devices  181 us (40%)
  waiting for transfers between devices  170 us (38%)
  Pallas kernels  84.6 us (19%)
  local copies, waits for them, and re-layouts  5.16 us (1%)
    ppermute x127, starting transfers between devices, send(): return lax.ppermute(value, ('section', 'tp'), pairs)  175 us
    ppermute x127, waiting for transfers between devices, send(): return lax.ppermute(value, ('section', 'tp'), pairs)  162 us
    pallas_call x16, Pallas kernels, backward_tick(): pl.pallas_call(functools.partial(backward_kernel, tick), grid_spec=grid_s...  31.8 us
    pallas_call x16, Pallas kernels, forward_tick(): pl.pallas_call(functools.partial(forward_kernel, tick), grid_spec=grid_sp...  30.9 us
  transfers between devices with their start and end apart: 128, of which 55 were waited for; matrix products, arithmetic and copies ran while one was open for 0% of the time, Pallas kernels for 10%

profile of v2, /device:TPU:15, one launch (start us, length us, event | category | flops | bytes accessed | tf_op | source)
XLA Modules:
  0.0 442.3 jit_solution(3787235953011943730)
XLA Ops:
  2.9 3.2 pack_layers.1
  6.0 5.1 %all-to-all-start = ((bf16[8,256,384]{2,1,0:T(8,128)(2,1)}), bf16[8,256,384]{2,1,0:T(8,128)(2,1)S(1)}, u32[]{:S(2)}, u32[]{:S(2)}) async-start(bf16[8,256,384]{2,1,0:T(8,128)(2,1)} %pack_layers.1), calls=%async_computation | async-start | bytes 3145728 | tf_op jit(solution)/shard_map/adapters/all_to_all | solution.py:393
  18.0 3.3 collective-permute-start.1
  22.4 7.7 %all-to-all-done.ab = bf16[8,256,384]{2,1,0:T(8,128)(2,1)S(1)} async-done(((bf16[8,256,384]{2,1,0:T(8,128)(2,1)}), bf16[8,256,384]{2,1,0:T(8,128)(2,1)S(1)}, u32[]{:S(2)}, u32[]{:S(2)}) %all-to-all-start) | async-done | bytes 1572896 | tf_op jit(solution)/shard_map/adapters/all_to_all | solution.py:393
  30.2 3.2 pack_blocks.1.own
  34.2 13.7 %collective-permute-done.1.w2 = bf16[1536,384]{1,0:T(8,128)(2,1)} collective-permute-done((bf16[1536,384]{1,0:T(8,128)(2,1)}, bf16[1536,384]{1,0:T(8,128)(2,1)}, u32[]{:S(2)}, u32[]{:S(2)}) %collective-permute-start.1) | collective-permute-done | bytes 1179680 | tf_op jit(solution)/shard_map/weight_blocks/ppermute | solution.py:52
  56.1 19.8 %collective-permute-done.4.p1 = bf16[2560,384]{1,0:T(8,128)(2,1)S(1)} collective-permute-done((bf16[2560,384]{1,0:T(8,128)(2,1)S(1)}, bf16[2560,384]{1,0:T(8,128)(2,1)S(1)}, u32[]{:S(2)}, u32[]{:S(2)}) %collective-permute-start.4) | collective-permute-done | bytes 1966112 | tf_op jit(solution)/shard_map/blocks/ppermute | solution.py:52
  78.6 20.3 %collective-permute-done.6.p3 = bf16[2560,384]{1,0:T(8,128)(2,1)S(1)} collective-permute-done((bf16[2560,384]{1,0:T(8,128)(2,1)S(1)}, bf16[2560,384]{1,0:T(8,128)(2,1)S(1)}, u32[]{:S(2)}, u32[]{:S(2)}) %collective-permute-start.6) | collective-permute-done | bytes 1966112 | tf_op jit(solution)/shard_map/blocks/ppermute | solution.py:52
  103.8 4.0 collective-permute-start.10
  117.3 3.7 collective-permute-start.11
  142.9 2.9 collective-permute-start.19
  150.2 3.4 collective-permute-done.21.p2
  168.7 3.0 collective-permute-start.27
  176.0 3.3 collective-permute-done.29.p2
  201.9 3.3 collective-permute-done.37.p2
  207.9 3.0 collective-permute-start.39
  222.4 3.0 collective-permute-start.70
  234.0 3.9 collective-permute-start.73
  250.2 3.5 collective-permute-start.77
  265.7 3.2 collective-permute-start.81
  272.9 3.0 collective-permute-start.55
  288.3 4.1 collective-permute-start.59
  298.6 3.6 collective-permute-start.89
  312.2 5.9 %collective-permute-start.66 = (bf16[32,2048]{1,0:T(8,128)(2,1)S(1)}, bf16[32,2048]{1,0:T(8,128)(2,1)S(1)}, u32[]{:S(2)}, u32[]{:S(2)}) collective-permute-start(bf16[32,2048]{1,0:T(8,128)(2,1)S(1)} %get-tuple-element.219), channel_id=1, source_target_pairs={{0,19},{1,16},{2,17},{3,18},{4,23},{5,20},{6,21},{7,22},{8,27},{9,... | collective-permute-start | bytes 393224 | tf_op jit(solution)/shard_map/forward/ppermute | solution.py:52
  332.0 5.4 %collective-permute-done.96.q1 = bf16[32,2048]{1,0:T(8,128)(2,1)S(1)} collective-permute-done((bf16[32,2048]{1,0:T(8,128)(2,1)S(1)}, bf16[32,2048]{1,0:T(8,128)(2,1)S(1)}, u32[]{:S(2)}, u32[]{:S(2)}) %collective-permute-start.96) | collective-permute-done | bytes 131104 | tf_op jit(solution)/shard_map/backward/ppermute | solution.py:52
  337.3 3.4 collective-permute-done.97.q2
  343.3 3.5 collective-permute-start.102
  346.8 3.5 collective-permute-done.100.q1
  350.3 4.3 collective-permute-done.101.q2
  356.7 3.1 collective-permute-start.106
  359.9 3.6 collective-permute-done.104.q1
  363.5 3.6 collective-permute-done.105.q2
  369.9 3.3 collective-permute-start.110
  373.2 4.0 collective-permute-done.108.q1
  377.2 4.0 collective-permute-done.109.q2
  383.4 3.1 collective-permute-start.114
  386.4 3.7 collective-permute-done.112.q1
  390.1 3.6 collective-permute-done.113.q2
  396.6 3.0 collective-permute-start.118
  399.6 4.4 collective-permute-done.116.q1
  403.9 4.0 collective-permute-done.117.q2
  410.0 3.1 collective-permute-start.122
  413.1 3.7 collective-permute-done.120.q1
  416.8 3.6 collective-permute-done.121.q2
  423.2 3.0 collective-permute-start.126
  426.2 4.4 collective-permute-done.124.q1
  430.6 4.0 collective-permute-done.125.q2
  437.2 4.7 %style_gradients.1 = (bf16[8,1,384,128]{3,2,1,0:T(8,128)(2,1)}, bf16[8,1,128,384]{3,2,1,0:T(8,128)(2,1)}) custom-call(s32[24]{0:T(128)S(1)} %concatenate.4.sc, bf16[256,384]{1,0:T(8,128)(2,1)S(1)} %copy-done.1, bf16[288,384]{1,0:T(8,128)(2,1)S(1)} %bitcast.14, bf16[288,128]{1,0:T(8,128)(2,1)S(1)} %bitcast.15, bf16[288,128]{1,0:T(8,128)(2,1)S(1)} %bitcast.16, ...), custom_call_target="tpu_custom_call" | custom-call | tf_op jit(solution)/shard_map/gradients/style_gradients/pallas_call | solution.py:370
  (275 shorter events, 218.0 us)
Async XLA Ops:
  6.0 24.1 %all-to-all-start = ((bf16[8,256,384]{2,1,0:T(8,128)(2,1)}), bf16[8,256,384]{2,1,0:T(8,128)(2,1)S(1)}, u32[]{:S(2)}, u32[]{:S(2)}) async-start(bf16[8,256,384]{2,1,0:T(8,128)(2,1)} %pack_layers.1), calls=%async_computation | async-start | bytes 3145728 | tf_op jit(solution)/shard_map/adapters/all_to_all | solution.py:393
  16.3 17.9 %collective-permute-start = (bf16[1536,384]{1,0:T(8,128)(2,1)}, bf16[1536,384]{1,0:T(8,128)(2,1)}, u32[]{:S(2)}, u32[]{:S(2)}) collective-permute-start(bf16[1536,384]{1,0:T(8,128)(2,1)} %bitcast.6), channel_id=1, source_target_pairs={{0,1},{1,2},{2,3},{3,0},{4,5},{5,6},{6,7},{7,4},{8,9},{9,10},{10,1... | collective-permute-start | bytes 3538952 | tf_op jit(solution)/shard_map/weight_blocks/ppermute | solution.py:52
  18.0 29.8 %collective-permute-start.1 = (bf16[1536,384]{1,0:T(8,128)(2,1)}, bf16[1536,384]{1,0:T(8,128)(2,1)}, u32[]{:S(2)}, u32[]{:S(2)}) collective-permute-start(bf16[1536,384]{1,0:T(8,128)(2,1)} %bitcast.7), channel_id=1, source_target_pairs={{0,2},{1,3},{2,0},{3,1},{4,6},{5,7},{6,4},{7,5},{8,10},{9,11},{10,... | collective-permute-start | bytes 3538952 | tf_op jit(solution)/shard_map/weight_blocks/ppermute | solution.py:52
  21.3 26.5 %collective-permute-start.2 = (bf16[1536,384]{1,0:T(8,128)(2,1)}, bf16[1536,384]{1,0:T(8,128)(2,1)}, u32[]{:S(2)}, u32[]{:S(2)}) collective-permute-start(bf16[1536,384]{1,0:T(8,128)(2,1)} %bitcast.8), channel_id=1, source_target_pairs={{0,3},{1,0},{2,1},{3,2},{4,7},{5,4},{6,5},{7,6},{8,11},{9,8},{10,9... | collective-permute-start | bytes 3538952 | tf_op jit(solution)/shard_map/weight_blocks/ppermute | solution.py:52
  51.9 98.0 %collective-permute-start.3 = (bf16[4,384,1536]{2,1,0:T(8,128)(2,1)S(1)}, bf16[4,384,1536]{2,1,0:T(8,128)(2,1)S(1)}, u32[]{:S(2)}, u32[]{:S(2)}) collective-permute-start(bf16[4,384,1536]{2,1,0:T(8,128)(2,1)S(1)} %transpose_weights.1), channel_id=1, source_target_pairs={{0,16},{1,17},{2,18},{3,19},{4,20},{5,21},{6,22},{7,23},{8,24},{9,... | collective-permute-start | bytes 14155784 | tf_op jit(solution)/shard_map/previous_weights/ppermute | solution.py:52
  52.1 23.8 %collective-permute-start.4 = (bf16[2560,384]{1,0:T(8,128)(2,1)S(1)}, bf16[2560,384]{1,0:T(8,128)(2,1)S(1)}, u32[]{:S(2)}, u32[]{:S(2)}) collective-permute-start(bf16[2560,384]{1,0:T(8,128)(2,1)S(1)} %pack_blocks.1.own), channel_id=1, source_target_pairs={{0,4},{1,5},{2,6},{3,7},{4,8},{5,9},{6,10},{7,11},{8,12},{9,13},{1... | collective-permute-start | bytes 5898248 | tf_op jit(solution)/shard_map/blocks/ppermute | solution.py:52
  53.3 25.3 %collective-permute-start.5 = (bf16[2560,384]{1,0:T(8,128)(2,1)S(1)}, bf16[2560,384]{1,0:T(8,128)(2,1)S(1)}, u32[]{:S(2)}, u32[]{:S(2)}) collective-permute-start(bf16[2560,384]{1,0:T(8,128)(2,1)S(1)} %pack_blocks.1.own), channel_id=1, source_target_pairs={{0,8},{1,9},{2,10},{3,11},{4,12},{5,13},{6,14},{7,15},{8,0},{9,1},... | collective-permute-start | bytes 5898248 | tf_op jit(solution)/shard_map/blocks/ppermute | solution.py:52
  54.1 44.8 %collective-permute-start.6 = (bf16[2560,384]{1,0:T(8,128)(2,1)S(1)}, bf16[2560,384]{1,0:T(8,128)(2,1)S(1)}, u32[]{:S(2)}, u32[]{:S(2)}) collective-permute-start(bf16[2560,384]{1,0:T(8,128)(2,1)S(1)} %pack_blocks.1.own), channel_id=1, source_target_pairs={{0,12},{1,13},{2,14},{3,15},{4,0},{5,1},{6,2},{7,3},{8,4},{9,5},{1... | collective-permute-start | bytes 5898248 | tf_op jit(solution)/shard_map/blocks/ppermute | solution.py:52
  207.9 11.2 %collective-permute-start.39 = (bf16[32,2048]{1,0:T(8,128)(2,1)S(1)}, bf16[32,2048]{1,0:T(8,128)(2,1)S(1)}, u32[]{:S(2)}, u32[]{:S(2)}) collective-permute-start(bf16[32,2048]{1,0:T(8,128)(2,1)S(1)} %get-tuple-element.195), channel_id=1, source_target_pairs={{0,16},{1,17},{2,18},{3,19},{4,20},{5,21},{6,22},{7,23},{8,24},{9,... | collective-permute-start | bytes 393224 | tf_op jit(solution)/shard_map/forward/ppermute | solution.py:52
  210.9 11.1 %collective-permute-start.40 = (bf16[32,2048]{1,0:T(8,128)(2,1)S(1)}, bf16[32,2048]{1,0:T(8,128)(2,1)S(1)}, u32[]{:S(2)}, u32[]{:S(2)}) collective-permute-start(bf16[32,2048]{1,0:T(8,128)(2,1)S(1)} %get-tuple-element.195), channel_id=1, source_target_pairs={{0,17},{1,18},{2,19},{3,16},{4,21},{5,22},{6,23},{7,20},{8,25},{9,... | collective-permute-start | bytes 393224 | tf_op jit(solution)/shard_map/forward/ppermute | solution.py:52
  211.7 10.7 %collective-permute-start.41 = (bf16[32,2048]{1,0:T(8,128)(2,1)S(1)}, bf16[32,2048]{1,0:T(8,128)(2,1)S(1)}, u32[]{:S(2)}, u32[]{:S(2)}) collective-permute-start(bf16[32,2048]{1,0:T(8,128)(2,1)S(1)} %get-tuple-element.195), channel_id=1, source_target_pairs={{0,18},{1,19},{2,16},{3,17},{4,22},{5,23},{6,20},{7,21},{8,26},{9,... | collective-permute-start | bytes 393224 | tf_op jit(solution)/shard_map/forward/ppermute | solution.py:52
  214.0 11.4 %collective-permute-start.42 = (bf16[32,2048]{1,0:T(8,128)(2,1)S(1)}, bf16[32,2048]{1,0:T(8,128)(2,1)S(1)}, u32[]{:S(2)}, u32[]{:S(2)}) collective-permute-start(bf16[32,2048]{1,0:T(8,128)(2,1)S(1)} %get-tuple-element.195), channel_id=1, source_target_pairs={{0,19},{1,16},{2,17},{3,18},{4,23},{5,20},{6,21},{7,22},{8,27},{9,... | collective-permute-start | bytes 393224 | tf_op jit(solution)/shard_map/forward/ppermute | solution.py:52
  234.0 10.3 %collective-permute-start.73 = (bf16[32,2048]{1,0:T(8,128)(2,1)S(1)}, bf16[32,2048]{1,0:T(8,128)(2,1)S(1)}, u32[]{:S(2)}, u32[]{:S(2)}) collective-permute-start(bf16[32,2048]{1,0:T(8,128)(2,1)S(1)} %get-tuple-element.232), channel_id=1, source_target_pairs={{0,114},{1,115},{2,112},{3,113},{4,118},{5,119},{6,116},{7,117},{8... | collective-permute-start | bytes 393224 | tf_op jit(solution)/shard_map/backward/ppermute | solution.py:52
  237.9 10.3 %collective-permute-start.71 = (bf16[32,2560]{1,0:T(8,128)(2,1)S(1)}, bf16[32,2560]{1,0:T(8,128)(2,1)S(1)}, u32[]{:S(2)}, u32[]{:S(2)}) collective-permute-start(bf16[32,2560]{1,0:T(8,128)(2,1)S(1)} %get-tuple-element.231), channel_id=1, source_target_pairs={{0,112},{1,113},{2,114},{3,115},{4,116},{5,117},{6,118},{7,119},{8... | collective-permute-start | bytes 491528 | tf_op jit(solution)/shard_map/backward/ppermute | solution.py:52
  260.2 10.8 %collective-permute-start.53 = (bf16[32,2048]{1,0:T(8,128)(2,1)S(1)}, bf16[32,2048]{1,0:T(8,128)(2,1)S(1)}, u32[]{:S(2)}, u32[]{:S(2)}) collective-permute-start(bf16[32,2048]{1,0:T(8,128)(2,1)S(1)} %get-tuple-element.207), channel_id=1, source_target_pairs={{0,18},{1,19},{2,16},{3,17},{4,22},{5,23},{6,20},{7,21},{8,26},{9,... | collective-permute-start | bytes 393224 | tf_op jit(solution)/shard_map/forward/ppermute | solution.py:52
  265.7 10.3 %collective-permute-start.81 = (bf16[32,2048]{1,0:T(8,128)(2,1)S(1)}, bf16[32,2048]{1,0:T(8,128)(2,1)S(1)}, u32[]{:S(2)}, u32[]{:S(2)}) collective-permute-start(bf16[32,2048]{1,0:T(8,128)(2,1)S(1)} %get-tuple-element.242), channel_id=1, source_target_pairs={{0,114},{1,115},{2,112},{3,113},{4,118},{5,119},{6,116},{7,117},{8... | collective-permute-start | bytes 393224 | tf_op jit(solution)/shard_map/backward/ppermute | solution.py:52
  281.6 10.8 %collective-permute-start.84 = (bf16[32,2048]{1,0:T(8,128)(2,1)S(1)}, bf16[32,2048]{1,0:T(8,128)(2,1)S(1)}, u32[]{:S(2)}, u32[]{:S(2)}) collective-permute-start(bf16[32,2048]{1,0:T(8,128)(2,1)S(1)} %get-tuple-element.247), channel_id=1, source_target_pairs={{0,113},{1,114},{2,115},{3,112},{4,117},{5,118},{6,119},{7,116},{8... | collective-permute-start | bytes 393224 | tf_op jit(solution)/shard_map/backward/ppermute | solution.py:52
  281.7 13.0 %collective-permute-start.83 = (bf16[32,2560]{1,0:T(8,128)(2,1)S(1)}, bf16[32,2560]{1,0:T(8,128)(2,1)S(1)}, u32[]{:S(2)}, u32[]{:S(2)}) collective-permute-start(bf16[32,2560]{1,0:T(8,128)(2,1)S(1)} %get-tuple-element.246), channel_id=1, source_target_pairs={{0,112},{1,113},{2,114},{3,115},{4,116},{5,117},{6,118},{7,119},{8... | collective-permute-start | bytes 491528 | tf_op jit(solution)/shard_map/backward/ppermute | solution.py:52
  283.6 11.0 %collective-permute-start.85 = (bf16[32,2048]{1,0:T(8,128)(2,1)S(1)}, bf16[32,2048]{1,0:T(8,128)(2,1)S(1)}, u32[]{:S(2)}, u32[]{:S(2)}) collective-permute-start(bf16[32,2048]{1,0:T(8,128)(2,1)S(1)} %get-tuple-element.247), channel_id=1, source_target_pairs={{0,114},{1,115},{2,112},{3,113},{4,118},{5,119},{6,116},{7,117},{8... | collective-permute-start | bytes 393224 | tf_op jit(solution)/shard_map/backward/ppermute | solution.py:52
  296.7 11.0 %collective-permute-start.88 = (bf16[32,2048]{1,0:T(8,128)(2,1)S(1)}, bf16[32,2048]{1,0:T(8,128)(2,1)S(1)}, u32[]{:S(2)}, u32[]{:S(2)}) collective-permute-start(bf16[32,2048]{1,0:T(8,128)(2,1)S(1)} %get-tuple-element.252), channel_id=1, source_target_pairs={{0,113},{1,114},{2,115},{3,112},{4,117},{5,118},{6,119},{7,116},{8... | collective-permute-start | bytes 393224 | tf_op jit(solution)/shard_map/backward/ppermute | solution.py:52
  304.9 13.2 %collective-permute-start.63 = (bf16[32,2048]{1,0:T(8,128)(2,1)S(1)}, bf16[32,2048]{1,0:T(8,128)(2,1)S(1)}, u32[]{:S(2)}, u32[]{:S(2)}) collective-permute-start(bf16[32,2048]{1,0:T(8,128)(2,1)S(1)} %get-tuple-element.219), channel_id=1, source_target_pairs={{0,16},{1,17},{2,18},{3,19},{4,20},{5,21},{6,22},{7,23},{8,24},{9,... | collective-permute-start | bytes 393224 | tf_op jit(solution)/shard_map/forward/ppermute | solution.py:52
  307.7 10.4 %collective-permute-start.64 = (bf16[32,2048]{1,0:T(8,128)(2,1)S(1)}, bf16[32,2048]{1,0:T(8,128)(2,1)S(1)}, u32[]{:S(2)}, u32[]{:S(2)}) collective-permute-start(bf16[32,2048]{1,0:T(8,128)(2,1)S(1)} %get-tuple-element.219), channel_id=1, source_target_pairs={{0,17},{1,18},{2,19},{3,16},{4,21},{5,22},{6,23},{7,20},{8,25},{9,... | collective-permute-start | bytes 393224 | tf_op jit(solution)/shard_map/forward/ppermute | solution.py:52
  308.8 11.4 %collective-permute-start.65 = (bf16[32,2048]{1,0:T(8,128)(2,1)S(1)}, bf16[32,2048]{1,0:T(8,128)(2,1)S(1)}, u32[]{:S(2)}, u32[]{:S(2)}) collective-permute-start(bf16[32,2048]{1,0:T(8,128)(2,1)S(1)} %get-tuple-element.219), channel_id=1, source_target_pairs={{0,18},{1,19},{2,16},{3,17},{4,22},{5,23},{6,20},{7,21},{8,26},{9,... | collective-permute-start | bytes 393224 | tf_op jit(solution)/shard_map/forward/ppermute | solution.py:52
  312.2 15.8 %collective-permute-start.91 = (bf16[32,2560]{1,0:T(8,128)(2,1)S(1)}, bf16[32,2560]{1,0:T(8,128)(2,1)S(1)}, u32[]{:S(2)}, u32[]{:S(2)}) collective-permute-start(bf16[32,2560]{1,0:T(8,128)(2,1)S(1)} %get-tuple-element.256), channel_id=1, source_target_pairs={{0,112},{1,113},{2,114},{3,115},{4,116},{5,117},{6,118},{7,119},{8... | collective-permute-start | bytes 491528 | tf_op jit(solution)/shard_map/backward/ppermute | solution.py:52
  329.9 11.2 %collective-permute-start.95 = (bf16[32,2560]{1,0:T(8,128)(2,1)S(1)}, bf16[32,2560]{1,0:T(8,128)(2,1)S(1)}, u32[]{:S(2)}, u32[]{:S(2)}) collective-permute-start(bf16[32,2560]{1,0:T(8,128)(2,1)S(1)} %get-tuple-element.263), channel_id=1, source_target_pairs={{0,112},{1,113},{2,114},{3,115},{4,116},{5,117},{6,118},{7,119},{8... | collective-permute-start | bytes 491528 | tf_op jit(solution)/shard_map/backward/ppermute | solution.py:52
  330.0 10.8 %collective-permute-start.97 = (bf16[32,2048]{1,0:T(8,128)(2,1)S(1)}, bf16[32,2048]{1,0:T(8,128)(2,1)S(1)}, u32[]{:S(2)}, u32[]{:S(2)}) collective-permute-start(bf16[32,2048]{1,0:T(8,128)(2,1)S(1)} %get-tuple-element.264), channel_id=1, source_target_pairs={{0,114},{1,115},{2,112},{3,113},{4,118},{5,119},{6,116},{7,117},{8... | collective-permute-start | bytes 393224 | tf_op jit(solution)/shard_map/backward/ppermute | solution.py:52
  330.1 11.0 %collective-permute-start.98 = (bf16[32,2048]{1,0:T(8,128)(2,1)S(1)}, bf16[32,2048]{1,0:T(8,128)(2,1)S(1)}, u32[]{:S(2)}, u32[]{:S(2)}) collective-permute-start(bf16[32,2048]{1,0:T(8,128)(2,1)S(1)} %get-tuple-element.264), channel_id=1, source_target_pairs={{0,115},{1,112},{2,113},{3,114},{4,119},{5,116},{6,117},{7,118},{8... | collective-permute-start | bytes 393224 | tf_op jit(solution)/shard_map/backward/ppermute | solution.py:52
  343.1 11.5 %collective-permute-start.99 = (bf16[32,2560]{1,0:T(8,128)(2,1)S(1)}, bf16[32,2560]{1,0:T(8,128)(2,1)S(1)}, u32[]{:S(2)}, u32[]{:S(2)}) collective-permute-start(bf16[32,2560]{1,0:T(8,128)(2,1)S(1)} %get-tuple-element.268), channel_id=1, source_target_pairs={{0,112},{1,113},{2,114},{3,115},{4,116},{5,117},{6,118},{7,119},{8... | collective-permute-start | bytes 491528 | tf_op jit(solution)/shard_map/backward/ppermute | solution.py:52
  343.2 11.4 %collective-permute-start.101 = (bf16[32,2048]{1,0:T(8,128)(2,1)S(1)}, bf16[32,2048]{1,0:T(8,128)(2,1)S(1)}, u32[]{:S(2)}, u32[]{:S(2)}) collective-permute-start(bf16[32,2048]{1,0:T(8,128)(2,1)S(1)} %get-tuple-element.269), channel_id=1, source_target_pairs={{0,114},{1,115},{2,112},{3,113},{4,118},{5,119},{6,116},{7,117},{8... | collective-permute-start | bytes 393224 | tf_op jit(solution)/shard_map/backward/ppermute | solution.py:52
  343.3 11.3 %collective-permute-start.102 = (bf16[32,2048]{1,0:T(8,128)(2,1)S(1)}, bf16[32,2048]{1,0:T(8,128)(2,1)S(1)}, u32[]{:S(2)}, u32[]{:S(2)}) collective-permute-start(bf16[32,2048]{1,0:T(8,128)(2,1)S(1)} %get-tuple-element.269), channel_id=1, source_target_pairs={{0,115},{1,112},{2,113},{3,114},{4,119},{5,116},{6,117},{7,118},{8... | collective-permute-start | bytes 393224 | tf_op jit(solution)/shard_map/backward/ppermute | solution.py:52
  356.6 11.2 %collective-permute-start.103 = (bf16[32,2560]{1,0:T(8,128)(2,1)S(1)}, bf16[32,2560]{1,0:T(8,128)(2,1)S(1)}, u32[]{:S(2)}, u32[]{:S(2)}) collective-permute-start(bf16[32,2560]{1,0:T(8,128)(2,1)S(1)} %get-tuple-element.273), channel_id=1, source_target_pairs={{0,112},{1,113},{2,114},{3,115},{4,116},{5,117},{6,118},{7,119},{8... | collective-permute-start | bytes 491528 | tf_op jit(solution)/shard_map/backward/ppermute | solution.py:52
  356.7 10.4 %collective-permute-start.105 = (bf16[32,2048]{1,0:T(8,128)(2,1)S(1)}, bf16[32,2048]{1,0:T(8,128)(2,1)S(1)}, u32[]{:S(2)}, u32[]{:S(2)}) collective-permute-start(bf16[32,2048]{1,0:T(8,128)(2,1)S(1)} %get-tuple-element.274), channel_id=1, source_target_pairs={{0,114},{1,115},{2,112},{3,113},{4,118},{5,119},{6,116},{7,117},{8... | collective-permute-start | bytes 393224 | tf_op jit(solution)/shard_map/backward/ppermute | solution.py:52
  356.7 11.0 %collective-permute-start.106 = (bf16[32,2048]{1,0:T(8,128)(2,1)S(1)}, bf16[32,2048]{1,0:T(8,128)(2,1)S(1)}, u32[]{:S(2)}, u32[]{:S(2)}) collective-permute-start(bf16[32,2048]{1,0:T(8,128)(2,1)S(1)} %get-tuple-element.274), channel_id=1, source_target_pairs={{0,115},{1,112},{2,113},{3,114},{4,119},{5,116},{6,117},{7,118},{8... | collective-permute-start | bytes 393224 | tf_op jit(solution)/shard_map/backward/ppermute | solution.py:52
  369.7 11.5 %collective-permute-start.107 = (bf16[32,2560]{1,0:T(8,128)(2,1)S(1)}, bf16[32,2560]{1,0:T(8,128)(2,1)S(1)}, u32[]{:S(2)}, u32[]{:S(2)}) collective-permute-start(bf16[32,2560]{1,0:T(8,128)(2,1)S(1)} %get-tuple-element.278), channel_id=1, source_target_pairs={{0,112},{1,113},{2,114},{3,115},{4,116},{5,117},{6,118},{7,119},{8... | collective-permute-start | bytes 491528 | tf_op jit(solution)/shard_map/backward/ppermute | solution.py:52
  369.8 11.4 %collective-permute-start.109 = (bf16[32,2048]{1,0:T(8,128)(2,1)S(1)}, bf16[32,2048]{1,0:T(8,128)(2,1)S(1)}, u32[]{:S(2)}, u32[]{:S(2)}) collective-permute-start(bf16[32,2048]{1,0:T(8,128)(2,1)S(1)} %get-tuple-element.279), channel_id=1, source_target_pairs={{0,114},{1,115},{2,112},{3,113},{4,118},{5,119},{6,116},{7,117},{8... | collective-permute-start | bytes 393224 | tf_op jit(solution)/shard_map/backward/ppermute | solution.py:52
  369.9 11.3 %collective-permute-start.110 = (bf16[32,2048]{1,0:T(8,128)(2,1)S(1)}, bf16[32,2048]{1,0:T(8,128)(2,1)S(1)}, u32[]{:S(2)}, u32[]{:S(2)}) collective-permute-start(bf16[32,2048]{1,0:T(8,128)(2,1)S(1)} %get-tuple-element.279), channel_id=1, source_target_pairs={{0,115},{1,112},{2,113},{3,114},{4,119},{5,116},{6,117},{7,118},{8... | collective-permute-start | bytes 393224 | tf_op jit(solution)/shard_map/backward/ppermute | solution.py:52
  383.2 11.2 %collective-permute-start.111 = (bf16[32,2560]{1,0:T(8,128)(2,1)S(1)}, bf16[32,2560]{1,0:T(8,128)(2,1)S(1)}, u32[]{:S(2)}, u32[]{:S(2)}) collective-permute-start(bf16[32,2560]{1,0:T(8,128)(2,1)S(1)} %get-tuple-element.283), channel_id=1, source_target_pairs={{0,112},{1,113},{2,114},{3,115},{4,116},{5,117},{6,118},{7,119},{8... | collective-permute-start | bytes 491528 | tf_op jit(solution)/shard_map/backward/ppermute | solution.py:52
  383.3 10.4 %collective-permute-start.113 = (bf16[32,2048]{1,0:T(8,128)(2,1)S(1)}, bf16[32,2048]{1,0:T(8,128)(2,1)S(1)}, u32[]{:S(2)}, u32[]{:S(2)}) collective-permute-start(bf16[32,2048]{1,0:T(8,128)(2,1)S(1)} %get-tuple-element.284), channel_id=1, source_target_pairs={{0,114},{1,115},{2,112},{3,113},{4,118},{5,119},{6,116},{7,117},{8... | collective-permute-start | bytes 393224 | tf_op jit(solution)/shard_map/backward/ppermute | solution.py:52
  383.4 11.0 %collective-permute-start.114 = (bf16[32,2048]{1,0:T(8,128)(2,1)S(1)}, bf16[32,2048]{1,0:T(8,128)(2,1)S(1)}, u32[]{:S(2)}, u32[]{:S(2)}) collective-permute-start(bf16[32,2048]{1,0:T(8,128)(2,1)S(1)} %get-tuple-element.284), channel_id=1, source_target_pairs={{0,115},{1,112},{2,113},{3,114},{4,119},{5,116},{6,117},{7,118},{8... | collective-permute-start | bytes 393224 | tf_op jit(solution)/shard_map/backward/ppermute | solution.py:52
  396.4 11.5 %collective-permute-start.115 = (bf16[32,2560]{1,0:T(8,128)(2,1)S(1)}, bf16[32,2560]{1,0:T(8,128)(2,1)S(1)}, u32[]{:S(2)}, u32[]{:S(2)}) collective-permute-start(bf16[32,2560]{1,0:T(8,128)(2,1)S(1)} %get-tuple-element.288), channel_id=1, source_target_pairs={{0,112},{1,113},{2,114},{3,115},{4,116},{5,117},{6,118},{7,119},{8... | collective-permute-start | bytes 491528 | tf_op jit(solution)/shard_map/backward/ppermute | solution.py:52
  396.5 11.4 %collective-permute-start.117 = (bf16[32,2048]{1,0:T(8,128)(2,1)S(1)}, bf16[32,2048]{1,0:T(8,128)(2,1)S(1)}, u32[]{:S(2)}, u32[]{:S(2)}) collective-permute-start(bf16[32,2048]{1,0:T(8,128)(2,1)S(1)} %get-tuple-element.289), channel_id=1, source_target_pairs={{0,114},{1,115},{2,112},{3,113},{4,118},{5,119},{6,116},{7,117},{8... | collective-permute-start | bytes 393224 | tf_op jit(solution)/shard_map/backward/ppermute | solution.py:52
  396.6 11.3 %collective-permute-start.118 = (bf16[32,2048]{1,0:T(8,128)(2,1)S(1)}, bf16[32,2048]{1,0:T(8,128)(2,1)S(1)}, u32[]{:S(2)}, u32[]{:S(2)}) collective-permute-start(bf16[32,2048]{1,0:T(8,128)(2,1)S(1)} %get-tuple-element.289), channel_id=1, source_target_pairs={{0,115},{1,112},{2,113},{3,114},{4,119},{5,116},{6,117},{7,118},{8... | collective-permute-start | bytes 393224 | tf_op jit(solution)/shard_map/backward/ppermute | solution.py:52
  409.9 11.2 %collective-permute-start.119 = (bf16[32,2560]{1,0:T(8,128)(2,1)S(1)}, bf16[32,2560]{1,0:T(8,128)(2,1)S(1)}, u32[]{:S(2)}, u32[]{:S(2)}) collective-permute-start(bf16[32,2560]{1,0:T(8,128)(2,1)S(1)} %get-tuple-element.293), channel_id=1, source_target_pairs={{0,112},{1,113},{2,114},{3,115},{4,116},{5,117},{6,118},{7,119},{8... | collective-permute-start | bytes 491528 | tf_op jit(solution)/shard_map/backward/ppermute | solution.py:52
  410.0 10.4 %collective-permute-start.121 = (bf16[32,2048]{1,0:T(8,128)(2,1)S(1)}, bf16[32,2048]{1,0:T(8,128)(2,1)S(1)}, u32[]{:S(2)}, u32[]{:S(2)}) collective-permute-start(bf16[32,2048]{1,0:T(8,128)(2,1)S(1)} %get-tuple-element.294), channel_id=1, source_target_pairs={{0,114},{1,115},{2,112},{3,113},{4,118},{5,119},{6,116},{7,117},{8... | collective-permute-start | bytes 393224 | tf_op jit(solution)/shard_map/backward/ppermute | solution.py:52
  410.0 11.0 %collective-permute-start.122 = (bf16[32,2048]{1,0:T(8,128)(2,1)S(1)}, bf16[32,2048]{1,0:T(8,128)(2,1)S(1)}, u32[]{:S(2)}, u32[]{:S(2)}) collective-permute-start(bf16[32,2048]{1,0:T(8,128)(2,1)S(1)} %get-tuple-element.294), channel_id=1, source_target_pairs={{0,115},{1,112},{2,113},{3,114},{4,119},{5,116},{6,117},{7,118},{8... | collective-permute-start | bytes 393224 | tf_op jit(solution)/shard_map/backward/ppermute | solution.py:52
  423.0 11.5 %collective-permute-start.123 = (bf16[32,2560]{1,0:T(8,128)(2,1)S(1)}, bf16[32,2560]{1,0:T(8,128)(2,1)S(1)}, u32[]{:S(2)}, u32[]{:S(2)}) collective-permute-start(bf16[32,2560]{1,0:T(8,128)(2,1)S(1)} %get-tuple-element.298), channel_id=1, source_target_pairs={{0,112},{1,113},{2,114},{3,115},{4,116},{5,117},{6,118},{7,119},{8... | collective-permute-start | bytes 491528 | tf_op jit(solution)/shard_map/backward/ppermute | solution.py:52
  423.1 11.4 %collective-permute-start.125 = (bf16[32,2048]{1,0:T(8,128)(2,1)S(1)}, bf16[32,2048]{1,0:T(8,128)(2,1)S(1)}, u32[]{:S(2)}, u32[]{:S(2)}) collective-permute-start(bf16[32,2048]{1,0:T(8,128)(2,1)S(1)} %get-tuple-element.299), channel_id=1, source_target_pairs={{0,114},{1,115},{2,112},{3,113},{4,118},{5,119},{6,116},{7,117},{8... | collective-permute-start | bytes 393224 | tf_op jit(solution)/shard_map/backward/ppermute | solution.py:52
  423.2 11.3 %collective-permute-start.126 = (bf16[32,2048]{1,0:T(8,128)(2,1)S(1)}, bf16[32,2048]{1,0:T(8,128)(2,1)S(1)}, u32[]{:S(2)}, u32[]{:S(2)}) collective-permute-start(bf16[32,2048]{1,0:T(8,128)(2,1)S(1)} %get-tuple-element.299), channel_id=1, source_target_pairs={{0,115},{1,112},{2,113},{3,114},{4,119},{5,116},{6,117},{7,118},{8... | collective-permute-start | bytes 393224 | tf_op jit(solution)/shard_map/backward/ppermute | solution.py:52
  (87 other events, 658.0 us)

commit v3 on v2

--- a/solution.py
+++ b/solution.py
@@ -16,11 +16,16 @@
 RANK = 128
 CHUNK = 384
 WIDE = SIDE * CHUNK
+PARTS = CHUNK // RANK
 PAIR = 2 * RANK
+PACKED = 2 * TOKENS + BLOCKS * PAIR
+LAST_FORWARD = LAYERS + BLOCKS - 1
+LAST_BACKWARD = 2 * LAYERS + BLOCKS - 1
 Z_AT = WIDE
 OWN_AT = WIDE + RANK
 PAY = OWN_AT + CHUNK
 PAY_EXTRA = PAY + RANK + CHUNK
+STYLES_AT_ONCE = 4
 BF = jnp.bfloat16
 F32 = jnp.float32
 
@@ -55,7 +60,8 @@
 IN_VMEM = pl.BlockSpec(memory_space=pltpu.VMEM)
 IN_SMEM = pl.BlockSpec(memory_space=pltpu.SMEM)
 ANYWHERE = pl.BlockSpec(memory_space=pl.ANY)
-PARAMS = pltpu.CompilerParams(vmem_limit_bytes=24 << 20)
+SMALL = pl.CostEstimate(flops=0, bytes_accessed=1024, transcendentals=0)
+PARAMS = pltpu.CompilerParams(vmem_limit_bytes=16 << 20)
 
 
 def shaped(*shape, dtype=BF):
@@ -76,6 +82,10 @@
 
 def dot_tn(left, right):
     return lax.dot_general(left, right, (((0,), (0,)), ((), ())), preferred_element_type=F32)
+
+
+def parts(value):
+    return [value[:, part * RANK:(part + 1) * RANK] for part in range(PARTS)]
 
 
 def gelu_both(y):
@@ -104,22 +114,23 @@
         out_shape=out_shape,
         scratch_shapes=[pltpu.SemaphoreType.DMA((count,))],
         compiler_params=PARAMS,
+        cost_estimate=SMALL,
         name=name,
     )(scalars, *operands)
 
 
 def pack_layers_kernel(a, b, out):
-    out[0, :RANK] = a[0, 0].T
-    out[0, RANK:] = b[0, 0]
+    for layer in range(LAYERS):
+        for part in range(PARTS):
+            out[layer, :RANK, part * RANK:(part + 1) * RANK] = a[0, layer, part * RANK:(part + 1) * RANK]
+        out[layer, RANK:] = b[0, (layer - 1) % LAYERS]
 
 
 def pack_layers(a, b):
     return pl.pallas_call(
         pack_layers_kernel,
-        grid=(LAYERS,),
-        in_specs=[pl.BlockSpec((1, 1, CHUNK, RANK), lambda i: (0, i, 0, 0)),
-                  pl.BlockSpec((1, 1, RANK, CHUNK), lambda i: (0, lax.rem(i + LAYERS - 1, LAYERS), 0, 0))],
-        out_specs=pl.BlockSpec((1, PAIR, CHUNK), lambda i: (i, 0, 0)),
+        in_specs=[IN_VMEM] * 2,
+        out_specs=IN_VMEM,
         out_shape=shaped(LAYERS, PAIR, CHUNK),
         compiler_params=PARAMS,
         name="pack_layers",
@@ -161,22 +172,27 @@
         out_shape=shaped(SIDE, WIDE, CHUNK),
         scratch_shapes=[pltpu.SemaphoreType.DMA((SIDE - 1,))],
         compiler_params=PARAMS,
+        cost_estimate=SMALL,
         name="settle_weights",
     )(scalars, *pieces)
 
 
-def settle_blocks_kernel(sc, own, p1, p2, p3, x, cot, ab, sems):
-    parts = [(0, x), (TOKENS, cot)]
-    copies = []
-    for k, piece in enumerate((p1, p2, p3)):
-        for i, (start, out) in enumerate(parts):
-            copies.append(pltpu.make_async_copy(piece.at[pl.ds(start, TOKENS)], out.at[k + 1], sems.at[k, i]))
-        copies.append(pltpu.make_async_copy(piece.at[pl.ds(2 * TOKENS, BLOCKS * PAIR)], ab.at[k + 1], sems.at[k, 2]))
+def settle_blocks_kernel(sc, own, p1, p2_first, p2_second, p3, x, cot, ab, sems):
+    head = 2 * TOKENS
+    split = PACKED // 2 - head
+    moves = []
+    for k, piece in ((1, p1), (2, p2_first), (3, p3)):
+        count = split if k == 2 else BLOCKS * PAIR
+        moves.append((piece.at[pl.ds(0, TOKENS)], x.at[k]))
+        moves.append((piece.at[pl.ds(TOKENS, TOKENS)], cot.at[k]))
+        moves.append((piece.at[pl.ds(head, count)], ab.at[k, pl.ds(0, count)]))
+    moves.append((p2_second, ab.at[2, pl.ds(split, PACKED // 2)]))
+    copies = [pltpu.make_async_copy(source, target, sems.at[i]) for i, (source, target) in enumerate(moves)]
     for copy in copies:
         copy.start()
-    for start, out in parts:
-        out[0] = own[pl.ds(start, TOKENS)]
-    ab[0] = own[pl.ds(2 * TOKENS, BLOCKS * PAIR)]
+    x[0] = own[pl.ds(0, TOKENS)]
+    cot[0] = own[pl.ds(TOKENS, TOKENS)]
+    ab[0] = own[pl.ds(head, BLOCKS * PAIR)]
     for copy in copies:
         copy.wait()
 
@@ -184,11 +200,12 @@
 def settle_blocks(scalars, pieces):
     return pl.pallas_call(
         settle_blocks_kernel,
-        in_specs=[IN_SMEM, IN_VMEM] + [ANYWHERE] * (SIDE - 1),
+        in_specs=[IN_SMEM, IN_VMEM] + [ANYWHERE] * SIDE,
         out_specs=[IN_VMEM] * 3,
         out_shape=[shaped(SIDE, TOKENS, CHUNK), shaped(SIDE, TOKENS, CHUNK), shaped(SIDE, BLOCKS * PAIR, CHUNK)],
-        scratch_shapes=[pltpu.SemaphoreType.DMA((SIDE - 1, 3))],
-        compiler_params=PARAMS,
+        scratch_shapes=[pltpu.SemaphoreType.DMA((10,))],
+        compiler_params=PARAMS,
+        cost_estimate=SMALL,
         name="settle_blocks",
     )(scalars, *pieces)
 
@@ -209,6 +226,7 @@
         out_specs=pl.BlockSpec((1, CHUNK, WIDE), lambda i: (i, 0, 0)),
         out_shape=shaped(SIDE, CHUNK, WIDE),
         compiler_params=PARAMS,
+        cost_estimate=SMALL,
         name="transpose_weights",
     )(w)
 
@@ -259,11 +277,15 @@
             h = jnp.where(section == 0, rows[k, own_rows], h)
         h_all[:, here] = h
         g_out[0, :, here] = slope
-        z_part = z_part + dot_nt(h, ab[k, down])
+        if tick < LAST_FORWARD:
+            for piece, weight in zip(parts(h), parts(ab[k, down])):
+                z_part = z_part + dot(piece, weight)
         if k == 0:
             h_out[0] = h
             pay[:, OWN_AT:PAY] = h
     pay[:, Z_AT:OWN_AT] = z_part.astype(BF)
+    if tick == LAST_FORWARD:
+        return
     h = h_all[...]
     for k in range(SIDE):
         pay[:, chunk_at(lax.rem(a - k + SIDE, SIDE))] = dot(h, w[k]).astype(BF)
@@ -277,6 +299,8 @@
     q_out[0] = q
     z_out[0] = q0[:, PAY:PAY + RANK]
     e_out[0] = q0[:, PAY + RANK:]
+    if tick == LAST_BACKWARD:
+        return
     q_part = jnp.zeros((ROWS, RANK), F32)
     total = jnp.zeros((ROWS, WIDE), F32)
     own_rows = pl.ds(pl.multiple_of(block * ROWS, ROWS), ROWS)
@@ -285,7 +309,8 @@
     for k, p in enumerate((q0, q1, q2, q3)):
         here = chunk_at(lax.rem(b - k + SIDE, SIDE))
         n = sum(r[:, here].astype(F32) for r in (q0, q1, q2, q3))
-        g = (p[:, OWN_AT:PAY].astype(F32) + n + dot(q, ab[k, down])).astype(BF)
+        back = jnp.concatenate([dot_nt(q, weight) for weight in parts(ab[k, down])], axis=1)
+        g = (p[:, OWN_AT:PAY].astype(F32) + n + back).astype(BF)
         g = jnp.where(section == 0, rows[k, own_rows], g)
         e = (slope[0, :, here] * g.astype(F32)).astype(BF)
         q_part = q_part + dot_nt(e, ab[k, up])
@@ -303,17 +328,21 @@
     pay0[:, :WIDE] = n
 
 
-def gradient_kernel(sc, x, h, q, z, e, ga, gb):
-    style = pl.program_id(0)
-    block = lax.broadcasted_iota(jnp.int32, (TOKENS, 1), 0) // ROWS
-    mine = jnp.zeros((TOKENS, 1), F32)
-    for n in range(BLOCKS):
-        mine = jnp.where((block == n) & (sc[16 + n] == style), 1.0, mine)
-    rows = jnp.where(sc[1] == 0, x[...], h[...])
-    q_mine = (q[...].astype(F32) * mine).astype(BF)
-    z_mine = (z[...].astype(F32) * mine).astype(BF)
-    ga[0, 0] = dot_tn(rows, q_mine).astype(BF)
-    gb[0, 0] = (ADAPTER_SCALE * dot_tn(z_mine, e[...])).astype(BF)
+def gradient_kernel(sc, x, h, q, z, e, ga, gb, h_turned, z_turned):
+    @pl.when(pl.program_id(0) == 0)
+    def _():
+        h_turned[...] = jnp.where(sc[1] == 0, x[...], h[...]).T
+        z_turned[...] = z[...].T
+
+    block = lax.broadcasted_iota(jnp.int32, (1, TOKENS), 1) // ROWS
+    for i in range(STYLES_AT_ONCE):
+        style = pl.program_id(0) * STYLES_AT_ONCE + i
+        keep = jnp.zeros((1, TOKENS), F32)
+        for n in range(BLOCKS):
+            keep = jnp.where((block == n) & (sc[16 + n] == style), 1.0, keep)
+        keep = keep.astype(BF)
+        ga[i, 0] = dot(h_turned[...] * keep, q[...]).astype(BF)
+        gb[i, 0] = (ADAPTER_SCALE * dot(z_turned[...] * keep, e[...])).astype(BF)
 
 
 def slot_spec(slot, tick, columns):
@@ -362,10 +391,11 @@
     whole = lambda columns: pl.BlockSpec((TOKENS, columns), lambda i, sc: (0, 0))
     grid_spec = pltpu.PrefetchScalarGridSpec(
         num_scalar_prefetch=1,
-        grid=(LAYERS,),
+        grid=(LAYERS // STYLES_AT_ONCE,),
         in_specs=[whole(CHUNK), whole(CHUNK), whole(RANK), whole(RANK), whole(CHUNK)],
-        out_specs=[pl.BlockSpec((1, 1, CHUNK, RANK), lambda i, sc: (i, 0, 0, 0)),
-                   pl.BlockSpec((1, 1, RANK, CHUNK), lambda i, sc: (i, 0, 0, 0))],
+        out_specs=[pl.BlockSpec((STYLES_AT_ONCE, 1, CHUNK, RANK), lambda i, sc: (i, 0, 0, 0)),
+                   pl.BlockSpec((STYLES_AT_ONCE, 1, RANK, CHUNK), lambda i, sc: (i, 0, 0, 0))],
+        scratch_shapes=[pltpu.VMEM((CHUNK, TOKENS), BF), pltpu.VMEM((RANK, TOKENS), BF)],
     )
     return pl.pallas_call(
         gradient_kernel,
@@ -390,16 +420,20 @@
 
     with jax.named_scope("adapters"):
         ab_out = pack_layers(down_weight_store, lib_b)
+        raw, ab_out = lax.optimization_barrier((weights, ab_out))
         ab_in = lax.all_to_all(ab_out, "section", split_axis=0, concat_axis=0, tiled=True)
     with jax.named_scope("weight_blocks"):
         cut = copy_kernel("cut_weights", cut_weights_kernel, SIDE * SIDE, [shaped(SIDE, CHUNK, CHUNK)] * SIDE, ANYWHERE,
-                          place, weights[0].reshape(SIDE * SIDE, CHUNK, CHUNK))
+                          place, raw[0].reshape(SIDE * SIDE, CHUNK, CHUNK))
         cut = [piece.reshape(WIDE, CHUNK) for piece in cut]
         w_pieces = [cut[0]] + [send(cut[k], along_a(k)) for k in range(1, SIDE)]
     with jax.named_scope("blocks"):
-        packed = copy_kernel("pack_blocks", pack_blocks_kernel, 2 + BLOCKS, shaped(2 * TOKENS + BLOCKS * PAIR, CHUNK),
+        packed = copy_kernel("pack_blocks", pack_blocks_kernel, 2 + BLOCKS, shaped(PACKED, CHUNK),
                              ANYWHERE, scalars, x_in, cotangent, ab_in)
-        block_pieces = [packed] + [send(packed, along_b(k)) for k in range(1, SIDE)]
+        below, above = send(packed, along_b(1)), send(packed, along_b(3))
+        first = send(below[:PACKED // 2], along_b(1))
+        second = send(above[PACKED // 2:], along_b(3))
+        block_pieces = [packed, below, first, second, above]
     with jax.named_scope("weight_blocks"):
         w_pieces[0], _ = lax.optimization_barrier((w_pieces[0], packed))
         w_own = settle_weights(place, w_pieces)

time: 451 us -> 440 us (0.976)
  Pallas kernels: 84.6 us -> 75.8 us
  waiting for transfers between devices: 170 us -> 165 us
    pallas_call x16, Pallas kernels: 30.9 us -> 25.7 us  [forward_tick(): pl.pallas_call(functools.partial(forward_kernel, tick), grid_spec=grid_sp...]
    ppermute x127 -> x128, waiting for transfers between devices: 162 us -> 158 us  [send(): return lax.ppermute(value, ('section', 'tp'), pairs)]
    ppermute x127 -> x128, starting transfers between devices: 175 us -> 178 us  [send(): return lax.ppermute(value, ('section', 'tp'), pairs)]
  transfers between devices with their start and end apart: 128 -> 129, of which waited for: 55 -> 58; matrix products, arithmetic and copies ran while one was open for 0% -> 0% of each run, Pallas kernels for 10% -> 10%
where the time goes in v3:
time: 440 us; the launch traced here: 431 us
  starting transfers between devices  183 us (42%)
  waiting for transfers between devices  165 us (38%)
  Pallas kernels  75.8 us (17%)
  local copies, waits for them, and re-layouts  5.35 us (1%)
    ppermute x128, starting transfers between devices, send(): return lax.ppermute(value, ('section', 'tp'), pairs)  178 us
    ppermute x128, waiting for transfers between devices, send(): return lax.ppermute(value, ('section', 'tp'), pairs)  158 us
    pallas_call x16, Pallas kernels, backward_tick(): pl.pallas_call(functools.partial(backward_kernel, tick), grid_spec=grid_s...  31.6 us
    pallas_call x16, Pallas kernels, forward_tick(): pl.pallas_call(functools.partial(forward_kernel, tick), grid_spec=grid_sp...  25.7 us
  transfers between devices with their start and end apart: 129, of which 58 were waited for; matrix products, arithmetic and copies ran while one was open for 0% of the time, Pallas kernels for 10%

profile of v3, /device:TPU:15, one launch (start us, length us, event | category | flops | bytes accessed | tf_op | source)
XLA Modules:
  0.0 431.5 jit_solution(5997165332474519910)
XLA Ops:
  4.2 5.1 %all-to-all-start = ((bf16[8,256,384]{2,1,0:T(8,128)(2,1)}), bf16[8,256,384]{2,1,0:T(8,128)(2,1)S(1)}, u32[]{:S(2)}, u32[]{:S(2)}) async-start(bf16[8,256,384]{2,1,0:T(8,128)(2,1)} %pack_layers.1), calls=%async_computation | async-start | bytes 3145728 | tf_op jit(solution)/shard_map/adapters/all_to_all | solution.py:424
  16.2 3.3 collective-permute-start.1
  20.6 7.7 %all-to-all-done.ab = bf16[8,256,384]{2,1,0:T(8,128)(2,1)S(1)} async-done(((bf16[8,256,384]{2,1,0:T(8,128)(2,1)}), bf16[8,256,384]{2,1,0:T(8,128)(2,1)S(1)}, u32[]{:S(2)}, u32[]{:S(2)}) %all-to-all-start) | async-done | bytes 1572896 | tf_op jit(solution)/shard_map/adapters/all_to_all | solution.py:424
  28.3 3.2 pack_blocks.1.own
  32.4 13.7 %collective-permute-done.1.w2 = bf16[1536,384]{1,0:T(8,128)(2,1)} collective-permute-done((bf16[1536,384]{1,0:T(8,128)(2,1)}, bf16[1536,384]{1,0:T(8,128)(2,1)}, u32[]{:S(2)}, u32[]{:S(2)}) %collective-permute-start.1) | collective-permute-done | bytes 1179680 | tf_op jit(solution)/shard_map/weight_blocks/ppermute | solution.py:57
  51.7 22.3 %collective-permute-done.4.p1 = bf16[2560,384]{1,0:T(8,128)(2,1)S(1)} collective-permute-done((bf16[2560,384]{1,0:T(8,128)(2,1)S(1)}, bf16[2560,384]{1,0:T(8,128)(2,1)S(1)}, u32[]{:S(2)}, u32[]{:S(2)}) %collective-permute-start.4) | collective-permute-done | bytes 1966112 | tf_op jit(solution)/shard_map/blocks/ppermute | solution.py:57
  75.9 11.6 %collective-permute-done.5.p2_first = bf16[1280,384]{1,0:T(8,128)(2,1)S(1)} collective-permute-done((bf16[1280,384]{1,0:T(8,128)(2,1)S(1)}, bf16[1280,384]{1,0:T(8,128)(2,1)S(1)}, u32[]{:S(2)}, u32[]{:S(2)}) %collective-permute-start.5) | collective-permute-done | bytes 983072 | tf_op jit(solution)/shard_map/blocks/ppermute | solution.py:57
  88.9 3.0 settle_blocks.1
  93.7 5.6 %collective-permute-start.10 = (bf16[32,2048]{1,0:T(8,128)(2,1)S(1)}, bf16[32,2048]{1,0:T(8,128)(2,1)S(1)}, u32[]{:S(2)}, u32[]{:S(2)}) collective-permute-start(bf16[32,2048]{1,0:T(8,128)(2,1)S(1)} %get-tuple-element.166), channel_id=1, source_target_pairs={{0,18},{1,19},{2,16},{3,17},{4,22},{5,23},{6,20},{7,21},{8,26},{9,... | collective-permute-start | bytes 393224 | tf_op jit(solution)/shard_map/forward/ppermute | solution.py:57
  99.3 3.1 collective-permute-start.11
  108.7 7.1 %collective-permute-start.12 = (bf16[32,2048]{1,0:T(8,128)(2,1)S(1)}, bf16[32,2048]{1,0:T(8,128)(2,1)S(1)}, u32[]{:S(2)}, u32[]{:S(2)}) collective-permute-start(bf16[32,2048]{1,0:T(8,128)(2,1)S(1)} %get-tuple-element.170), channel_id=1, source_target_pairs={{0,16},{1,17},{2,18},{3,19},{4,20},{5,21},{6,22},{7,23},{8,24},{9,... | collective-permute-start | bytes 393224 | tf_op jit(solution)/shard_map/forward/ppermute | solution.py:57
  117.1 2.8 collective-permute-start.15
  144.3 3.1 collective-permute-done.22.p2
  162.1 3.0 collective-permute-start.28
  169.8 2.9 collective-permute-done.30.p2
  187.5 2.9 collective-permute-start.36
  194.8 3.3 collective-permute-done.38.p2
  200.7 2.8 collective-permute-start.40
  226.9 3.5 collective-permute-start.74
  243.0 3.5 collective-permute-start.78
  257.9 3.3 collective-permute-start.82
  264.5 3.0 collective-permute-start.56
  280.1 4.1 collective-permute-start.60
  290.9 3.3 collective-permute-start.90
  296.8 2.8 collective-permute-start.64
  304.0 5.6 %collective-permute-start.67 = (bf16[32,2048]{1,0:T(8,128)(2,1)S(1)}, bf16[32,2048]{1,0:T(8,128)(2,1)S(1)}, u32[]{:S(2)}, u32[]{:S(2)}) collective-permute-start(bf16[32,2048]{1,0:T(8,128)(2,1)S(1)} %get-tuple-element.223), channel_id=1, source_target_pairs={{0,19},{1,16},{2,17},{3,18},{4,23},{5,20},{6,21},{7,22},{8,27},{9,... | collective-permute-start | bytes 393224 | tf_op jit(solution)/shard_map/forward/ppermute | solution.py:57
  313.3 2.9 collective-permute-done.93.q1
  324.0 5.4 %collective-permute-done.97.q1 = bf16[32,2048]{1,0:T(8,128)(2,1)S(1)} collective-permute-done((bf16[32,2048]{1,0:T(8,128)(2,1)S(1)}, bf16[32,2048]{1,0:T(8,128)(2,1)S(1)}, u32[]{:S(2)}, u32[]{:S(2)}) %collective-permute-start.97) | collective-permute-done | bytes 131104 | tf_op jit(solution)/shard_map/backward/ppermute | solution.py:57
  329.3 3.6 collective-permute-done.98.q2
  335.4 3.5 collective-permute-start.103
  338.9 3.5 collective-permute-done.101.q1
  342.4 4.2 collective-permute-done.102.q2
  348.9 3.0 collective-permute-start.107
  351.9 3.9 collective-permute-done.105.q1
  355.8 3.7 collective-permute-done.106.q2
  362.2 3.1 collective-permute-start.111
  365.4 4.0 collective-permute-done.109.q1
  369.4 4.1 collective-permute-done.110.q2
  378.5 4.0 collective-permute-done.113.q1
  382.5 3.7 collective-permute-done.114.q2
  389.0 3.0 collective-permute-start.119
  392.0 4.3 collective-permute-done.117.q1
  396.3 4.0 collective-permute-done.118.q2
  405.3 4.0 collective-permute-done.121.q1
  409.3 3.7 collective-permute-done.122.q2
  415.8 3.0 collective-permute-start.127
  418.8 4.3 collective-permute-done.125.q1
  423.1 4.0 collective-permute-done.126.q2
  (279 shorter events, 211.4 us)
Async XLA Ops:
  4.2 24.1 %all-to-all-start = ((bf16[8,256,384]{2,1,0:T(8,128)(2,1)}), bf16[8,256,384]{2,1,0:T(8,128)(2,1)S(1)}, u32[]{:S(2)}, u32[]{:S(2)}) async-start(bf16[8,256,384]{2,1,0:T(8,128)(2,1)} %pack_layers.1), calls=%async_computation | async-start | bytes 3145728 | tf_op jit(solution)/shard_map/adapters/all_to_all | solution.py:424
  14.5 17.9 %collective-permute-start = (bf16[1536,384]{1,0:T(8,128)(2,1)}, bf16[1536,384]{1,0:T(8,128)(2,1)}, u32[]{:S(2)}, u32[]{:S(2)}) collective-permute-start(bf16[1536,384]{1,0:T(8,128)(2,1)} %bitcast.6), channel_id=1, source_target_pairs={{0,1},{1,2},{2,3},{3,0},{4,5},{5,6},{6,7},{7,4},{8,9},{9,10},{10,1... | collective-permute-start | bytes 3538952 | tf_op jit(solution)/shard_map/weight_blocks/ppermute | solution.py:57
  16.2 29.8 %collective-permute-start.1 = (bf16[1536,384]{1,0:T(8,128)(2,1)}, bf16[1536,384]{1,0:T(8,128)(2,1)}, u32[]{:S(2)}, u32[]{:S(2)}) collective-permute-start(bf16[1536,384]{1,0:T(8,128)(2,1)} %bitcast.7), channel_id=1, source_target_pairs={{0,2},{1,3},{2,0},{3,1},{4,6},{5,7},{6,4},{7,5},{8,10},{9,11},{10,... | collective-permute-start | bytes 3538952 | tf_op jit(solution)/shard_map/weight_blocks/ppermute | solution.py:57
  19.5 26.5 %collective-permute-start.2 = (bf16[1536,384]{1,0:T(8,128)(2,1)}, bf16[1536,384]{1,0:T(8,128)(2,1)}, u32[]{:S(2)}, u32[]{:S(2)}) collective-permute-start(bf16[1536,384]{1,0:T(8,128)(2,1)} %bitcast.8), channel_id=1, source_target_pairs={{0,3},{1,0},{2,1},{3,2},{4,7},{5,4},{6,5},{7,6},{8,11},{9,8},{10,9... | collective-permute-start | bytes 3538952 | tf_op jit(solution)/shard_map/weight_blocks/ppermute | solution.py:57
  50.1 94.2 %collective-permute-start.3 = (bf16[4,384,1536]{2,1,0:T(8,128)(2,1)S(1)}, bf16[4,384,1536]{2,1,0:T(8,128)(2,1)S(1)}, u32[]{:S(2)}, u32[]{:S(2)}) collective-permute-start(bf16[4,384,1536]{2,1,0:T(8,128)(2,1)S(1)} %transpose_weights.1), channel_id=1, source_target_pairs={{0,16},{1,17},{2,18},{3,19},{4,20},{5,21},{6,22},{7,23},{8,24},{9,... | collective-permute-start | bytes 14155784 | tf_op jit(solution)/shard_map/previous_weights/ppermute | solution.py:57
  50.3 23.8 %collective-permute-start.4 = (bf16[2560,384]{1,0:T(8,128)(2,1)S(1)}, bf16[2560,384]{1,0:T(8,128)(2,1)S(1)}, u32[]{:S(2)}, u32[]{:S(2)}) collective-permute-start(bf16[2560,384]{1,0:T(8,128)(2,1)S(1)} %pack_blocks.1.own), channel_id=1, source_target_pairs={{0,4},{1,5},{2,6},{3,7},{4,8},{5,9},{6,10},{7,11},{8,12},{9,13},{1... | collective-permute-start | bytes 5898248 | tf_op jit(solution)/shard_map/blocks/ppermute | solution.py:57
  51.5 23.9 %collective-permute-start.6 = (bf16[2560,384]{1,0:T(8,128)(2,1)S(1)}, bf16[2560,384]{1,0:T(8,128)(2,1)S(1)}, u32[]{:S(2)}, u32[]{:S(2)}) collective-permute-start(bf16[2560,384]{1,0:T(8,128)(2,1)S(1)} %pack_blocks.1.own), channel_id=1, source_target_pairs={{0,12},{1,13},{2,14},{3,15},{4,0},{5,1},{6,2},{7,3},{8,4},{9,5},{1... | collective-permute-start | bytes 5898248 | tf_op jit(solution)/shard_map/blocks/ppermute | solution.py:57
  74.2 13.3 %collective-permute-start.5 = (bf16[1280,384]{1,0:T(8,128)(2,1)S(1)}, bf16[1280,384]{1,0:T(8,128)(2,1)S(1)}, u32[]{:S(2)}, u32[]{:S(2)}) collective-permute-start(bf16[1280,384]{1,0:T(8,128)(2,1)S(1)} %slice.8), channel_id=1, source_target_pairs={{0,4},{1,5},{2,6},{3,7},{4,8},{5,9},{6,10},{7,11},{8,12},{9,13},{1... | collective-permute-start | bytes 2949128 | tf_op jit(solution)/shard_map/blocks/ppermute | solution.py:57
  75.5 13.3 %collective-permute-start.7 = (bf16[1280,384]{1,0:T(8,128)(2,1)S(1)}, bf16[1280,384]{1,0:T(8,128)(2,1)S(1)}, u32[]{:S(2)}, u32[]{:S(2)}) collective-permute-start(bf16[1280,384]{1,0:T(8,128)(2,1)S(1)} %slice.9), channel_id=1, source_target_pairs={{0,12},{1,13},{2,14},{3,15},{4,0},{5,1},{6,2},{7,3},{8,4},{9,5},{1... | collective-permute-start | bytes 2949128 | tf_op jit(solution)/shard_map/blocks/ppermute | solution.py:57
  108.7 11.3 %collective-permute-start.12 = (bf16[32,2048]{1,0:T(8,128)(2,1)S(1)}, bf16[32,2048]{1,0:T(8,128)(2,1)S(1)}, u32[]{:S(2)}, u32[]{:S(2)}) collective-permute-start(bf16[32,2048]{1,0:T(8,128)(2,1)S(1)} %get-tuple-element.170), channel_id=1, source_target_pairs={{0,16},{1,17},{2,18},{3,19},{4,20},{5,21},{6,22},{7,23},{8,24},{9,... | collective-permute-start | bytes 393224 | tf_op jit(solution)/shard_map/forward/ppermute | solution.py:57
  200.7 11.3 %collective-permute-start.40 = (bf16[32,2048]{1,0:T(8,128)(2,1)S(1)}, bf16[32,2048]{1,0:T(8,128)(2,1)S(1)}, u32[]{:S(2)}, u32[]{:S(2)}) collective-permute-start(bf16[32,2048]{1,0:T(8,128)(2,1)S(1)} %get-tuple-element.199), channel_id=1, source_target_pairs={{0,16},{1,17},{2,18},{3,19},{4,20},{5,21},{6,22},{7,23},{8,24},{9,... | collective-permute-start | bytes 393224 | tf_op jit(solution)/shard_map/forward/ppermute | solution.py:57
  203.5 10.6 %collective-permute-start.41 = (bf16[32,2048]{1,0:T(8,128)(2,1)S(1)}, bf16[32,2048]{1,0:T(8,128)(2,1)S(1)}, u32[]{:S(2)}, u32[]{:S(2)}) collective-permute-start(bf16[32,2048]{1,0:T(8,128)(2,1)S(1)} %get-tuple-element.199), channel_id=1, source_target_pairs={{0,17},{1,18},{2,19},{3,16},{4,21},{5,22},{6,23},{7,20},{8,25},{9,... | collective-permute-start | bytes 393224 | tf_op jit(solution)/shard_map/forward/ppermute | solution.py:57
  204.7 10.7 %collective-permute-start.42 = (bf16[32,2048]{1,0:T(8,128)(2,1)S(1)}, bf16[32,2048]{1,0:T(8,128)(2,1)S(1)}, u32[]{:S(2)}, u32[]{:S(2)}) collective-permute-start(bf16[32,2048]{1,0:T(8,128)(2,1)S(1)} %get-tuple-element.199), channel_id=1, source_target_pairs={{0,18},{1,19},{2,16},{3,17},{4,22},{5,23},{6,20},{7,21},{8,26},{9,... | collective-permute-start | bytes 393224 | tf_op jit(solution)/shard_map/forward/ppermute | solution.py:57
  214.2 10.6 %collective-permute-start.68 = (bf16[32,2560]{1,0:T(8,128)(2,1)S(1)}, bf16[32,2560]{1,0:T(8,128)(2,1)S(1)}, u32[]{:S(2)}, u32[]{:S(2)}) collective-permute-start(bf16[32,2560]{1,0:T(8,128)(2,1)S(1)} %get-tuple-element.230), channel_id=1, source_target_pairs={{0,112},{1,113},{2,114},{3,115},{4,116},{5,117},{6,118},{7,119},{8... | collective-permute-start | bytes 491528 | tf_op jit(solution)/shard_map/backward/ppermute | solution.py:57
  230.4 10.5 %collective-permute-start.72 = (bf16[32,2560]{1,0:T(8,128)(2,1)S(1)}, bf16[32,2560]{1,0:T(8,128)(2,1)S(1)}, u32[]{:S(2)}, u32[]{:S(2)}) collective-permute-start(bf16[32,2560]{1,0:T(8,128)(2,1)S(1)} %get-tuple-element.235), channel_id=1, source_target_pairs={{0,112},{1,113},{2,114},{3,115},{4,116},{5,117},{6,118},{7,119},{8... | collective-permute-start | bytes 491528 | tf_op jit(solution)/shard_map/backward/ppermute | solution.py:57
  235.7 10.8 %collective-permute-start.49 = (bf16[32,2048]{1,0:T(8,128)(2,1)S(1)}, bf16[32,2048]{1,0:T(8,128)(2,1)S(1)}, u32[]{:S(2)}, u32[]{:S(2)}) collective-permute-start(bf16[32,2048]{1,0:T(8,128)(2,1)S(1)} %get-tuple-element.207), channel_id=1, source_target_pairs={{0,17},{1,18},{2,19},{3,16},{4,21},{5,22},{6,23},{7,20},{8,25},{9,... | collective-permute-start | bytes 393224 | tf_op jit(solution)/shard_map/forward/ppermute | solution.py:57
  257.9 10.6 %collective-permute-start.82 = (bf16[32,2048]{1,0:T(8,128)(2,1)S(1)}, bf16[32,2048]{1,0:T(8,128)(2,1)S(1)}, u32[]{:S(2)}, u32[]{:S(2)}) collective-permute-start(bf16[32,2048]{1,0:T(8,128)(2,1)S(1)} %get-tuple-element.246), channel_id=1, source_target_pairs={{0,114},{1,115},{2,112},{3,113},{4,118},{5,119},{6,116},{7,117},{8... | collective-permute-start | bytes 393224 | tf_op jit(solution)/shard_map/backward/ppermute | solution.py:57
  273.7 13.1 %collective-permute-start.84 = (bf16[32,2560]{1,0:T(8,128)(2,1)S(1)}, bf16[32,2560]{1,0:T(8,128)(2,1)S(1)}, u32[]{:S(2)}, u32[]{:S(2)}) collective-permute-start(bf16[32,2560]{1,0:T(8,128)(2,1)S(1)} %get-tuple-element.250), channel_id=1, source_target_pairs={{0,112},{1,113},{2,114},{3,115},{4,116},{5,117},{6,118},{7,119},{8... | collective-permute-start | bytes 491528 | tf_op jit(solution)/shard_map/backward/ppermute | solution.py:57
  275.6 10.7 %collective-permute-start.86 = (bf16[32,2048]{1,0:T(8,128)(2,1)S(1)}, bf16[32,2048]{1,0:T(8,128)(2,1)S(1)}, u32[]{:S(2)}, u32[]{:S(2)}) collective-permute-start(bf16[32,2048]{1,0:T(8,128)(2,1)S(1)} %get-tuple-element.251), channel_id=1, source_target_pairs={{0,114},{1,115},{2,112},{3,113},{4,118},{5,119},{6,116},{7,117},{8... | collective-permute-start | bytes 393224 | tf_op jit(solution)/shard_map/backward/ppermute | solution.py:57
  280.1 10.8 %collective-permute-start.60 = (bf16[32,2048]{1,0:T(8,128)(2,1)S(1)}, bf16[32,2048]{1,0:T(8,128)(2,1)S(1)}, u32[]{:S(2)}, u32[]{:S(2)}) collective-permute-start(bf16[32,2048]{1,0:T(8,128)(2,1)S(1)} %get-tuple-element.219), channel_id=1, source_target_pairs={{0,16},{1,17},{2,18},{3,19},{4,20},{5,21},{6,22},{7,23},{8,24},{9,... | collective-permute-start | bytes 393224 | tf_op jit(solution)/shard_map/forward/ppermute | solution.py:57
  288.9 10.8 %collective-permute-start.89 = (bf16[32,2048]{1,0:T(8,128)(2,1)S(1)}, bf16[32,2048]{1,0:T(8,128)(2,1)S(1)}, u32[]{:S(2)}, u32[]{:S(2)}) collective-permute-start(bf16[32,2048]{1,0:T(8,128)(2,1)S(1)} %get-tuple-element.256), channel_id=1, source_target_pairs={{0,113},{1,114},{2,115},{3,112},{4,117},{5,118},{6,119},{7,116},{8... | collective-permute-start | bytes 393224 | tf_op jit(solution)/shard_map/backward/ppermute | solution.py:57
  296.8 12.8 %collective-permute-start.64 = (bf16[32,2048]{1,0:T(8,128)(2,1)S(1)}, bf16[32,2048]{1,0:T(8,128)(2,1)S(1)}, u32[]{:S(2)}, u32[]{:S(2)}) collective-permute-start(bf16[32,2048]{1,0:T(8,128)(2,1)S(1)} %get-tuple-element.223), channel_id=1, source_target_pairs={{0,16},{1,17},{2,18},{3,19},{4,20},{5,21},{6,22},{7,23},{8,24},{9,... | collective-permute-start | bytes 393224 | tf_op jit(solution)/shard_map/forward/ppermute | solution.py:57
  300.4 11.4 %collective-permute-start.66 = (bf16[32,2048]{1,0:T(8,128)(2,1)S(1)}, bf16[32,2048]{1,0:T(8,128)(2,1)S(1)}, u32[]{:S(2)}, u32[]{:S(2)}) collective-permute-start(bf16[32,2048]{1,0:T(8,128)(2,1)S(1)} %get-tuple-element.223), channel_id=1, source_target_pairs={{0,18},{1,19},{2,16},{3,17},{4,22},{5,23},{6,20},{7,21},{8,26},{9,... | collective-permute-start | bytes 393224 | tf_op jit(solution)/shard_map/forward/ppermute | solution.py:57
  304.0 15.9 %collective-permute-start.92 = (bf16[32,2560]{1,0:T(8,128)(2,1)S(1)}, bf16[32,2560]{1,0:T(8,128)(2,1)S(1)}, u32[]{:S(2)}, u32[]{:S(2)}) collective-permute-start(bf16[32,2560]{1,0:T(8,128)(2,1)S(1)} %get-tuple-element.260), channel_id=1, source_target_pairs={{0,112},{1,113},{2,114},{3,115},{4,116},{5,117},{6,118},{7,119},{8... | collective-permute-start | bytes 491528 | tf_op jit(solution)/shard_map/backward/ppermute | solution.py:57
  321.9 11.3 %collective-permute-start.96 = (bf16[32,2560]{1,0:T(8,128)(2,1)S(1)}, bf16[32,2560]{1,0:T(8,128)(2,1)S(1)}, u32[]{:S(2)}, u32[]{:S(2)}) collective-permute-start(bf16[32,2560]{1,0:T(8,128)(2,1)S(1)} %get-tuple-element.267), channel_id=1, source_target_pairs={{0,112},{1,113},{2,114},{3,115},{4,116},{5,117},{6,118},{7,119},{8... | collective-permute-start | bytes 491528 | tf_op jit(solution)/shard_map/backward/ppermute | solution.py:57
  322.0 10.9 %collective-permute-start.98 = (bf16[32,2048]{1,0:T(8,128)(2,1)S(1)}, bf16[32,2048]{1,0:T(8,128)(2,1)S(1)}, u32[]{:S(2)}, u32[]{:S(2)}) collective-permute-start(bf16[32,2048]{1,0:T(8,128)(2,1)S(1)} %get-tuple-element.268), channel_id=1, source_target_pairs={{0,114},{1,115},{2,112},{3,113},{4,118},{5,119},{6,116},{7,117},{8... | collective-permute-start | bytes 393224 | tf_op jit(solution)/shard_map/backward/ppermute | solution.py:57
  322.1 11.1 %collective-permute-start.99 = (bf16[32,2048]{1,0:T(8,128)(2,1)S(1)}, bf16[32,2048]{1,0:T(8,128)(2,1)S(1)}, u32[]{:S(2)}, u32[]{:S(2)}) collective-permute-start(bf16[32,2048]{1,0:T(8,128)(2,1)S(1)} %get-tuple-element.268), channel_id=1, source_target_pairs={{0,115},{1,112},{2,113},{3,114},{4,119},{5,116},{6,117},{7,118},{8... | collective-permute-start | bytes 393224 | tf_op jit(solution)/shard_map/backward/ppermute | solution.py:57
  335.2 11.5 %collective-permute-start.100 = (bf16[32,2560]{1,0:T(8,128)(2,1)S(1)}, bf16[32,2560]{1,0:T(8,128)(2,1)S(1)}, u32[]{:S(2)}, u32[]{:S(2)}) collective-permute-start(bf16[32,2560]{1,0:T(8,128)(2,1)S(1)} %get-tuple-element.272), channel_id=1, source_target_pairs={{0,112},{1,113},{2,114},{3,115},{4,116},{5,117},{6,118},{7,119},{8... | collective-permute-start | bytes 491528 | tf_op jit(solution)/shard_map/backward/ppermute | solution.py:57
  335.3 11.3 %collective-permute-start.102 = (bf16[32,2048]{1,0:T(8,128)(2,1)S(1)}, bf16[32,2048]{1,0:T(8,128)(2,1)S(1)}, u32[]{:S(2)}, u32[]{:S(2)}) collective-permute-start(bf16[32,2048]{1,0:T(8,128)(2,1)S(1)} %get-tuple-element.273), channel_id=1, source_target_pairs={{0,114},{1,115},{2,112},{3,113},{4,118},{5,119},{6,116},{7,117},{8... | collective-permute-start | bytes 393224 | tf_op jit(solution)/shard_map/backward/ppermute | solution.py:57
  335.4 11.3 %collective-permute-start.103 = (bf16[32,2048]{1,0:T(8,128)(2,1)S(1)}, bf16[32,2048]{1,0:T(8,128)(2,1)S(1)}, u32[]{:S(2)}, u32[]{:S(2)}) collective-permute-start(bf16[32,2048]{1,0:T(8,128)(2,1)S(1)} %get-tuple-element.273), channel_id=1, source_target_pairs={{0,115},{1,112},{2,113},{3,114},{4,119},{5,116},{6,117},{7,118},{8... | collective-permute-start | bytes 393224 | tf_op jit(solution)/shard_map/backward/ppermute | solution.py:57
  348.7 11.3 %collective-permute-start.104 = (bf16[32,2560]{1,0:T(8,128)(2,1)S(1)}, bf16[32,2560]{1,0:T(8,128)(2,1)S(1)}, u32[]{:S(2)}, u32[]{:S(2)}) collective-permute-start(bf16[32,2560]{1,0:T(8,128)(2,1)S(1)} %get-tuple-element.277), channel_id=1, source_target_pairs={{0,112},{1,113},{2,114},{3,115},{4,116},{5,117},{6,118},{7,119},{8... | collective-permute-start | bytes 491528 | tf_op jit(solution)/shard_map/backward/ppermute | solution.py:57
  348.8 10.7 %collective-permute-start.106 = (bf16[32,2048]{1,0:T(8,128)(2,1)S(1)}, bf16[32,2048]{1,0:T(8,128)(2,1)S(1)}, u32[]{:S(2)}, u32[]{:S(2)}) collective-permute-start(bf16[32,2048]{1,0:T(8,128)(2,1)S(1)} %get-tuple-element.278), channel_id=1, source_target_pairs={{0,114},{1,115},{2,112},{3,113},{4,118},{5,119},{6,116},{7,117},{8... | collective-permute-start | bytes 393224 | tf_op jit(solution)/shard_map/backward/ppermute | solution.py:57
  348.9 11.1 %collective-permute-start.107 = (bf16[32,2048]{1,0:T(8,128)(2,1)S(1)}, bf16[32,2048]{1,0:T(8,128)(2,1)S(1)}, u32[]{:S(2)}, u32[]{:S(2)}) collective-permute-start(bf16[32,2048]{1,0:T(8,128)(2,1)S(1)} %get-tuple-element.278), channel_id=1, source_target_pairs={{0,115},{1,112},{2,113},{3,114},{4,119},{5,116},{6,117},{7,118},{8... | collective-permute-start | bytes 393224 | tf_op jit(solution)/shard_map/backward/ppermute | solution.py:57
  362.0 11.5 %collective-permute-start.108 = (bf16[32,2560]{1,0:T(8,128)(2,1)S(1)}, bf16[32,2560]{1,0:T(8,128)(2,1)S(1)}, u32[]{:S(2)}, u32[]{:S(2)}) collective-permute-start(bf16[32,2560]{1,0:T(8,128)(2,1)S(1)} %get-tuple-element.282), channel_id=1, source_target_pairs={{0,112},{1,113},{2,114},{3,115},{4,116},{5,117},{6,118},{7,119},{8... | collective-permute-start | bytes 491528 | tf_op jit(solution)/shard_map/backward/ppermute | solution.py:57
  362.1 11.4 %collective-permute-start.110 = (bf16[32,2048]{1,0:T(8,128)(2,1)S(1)}, bf16[32,2048]{1,0:T(8,128)(2,1)S(1)}, u32[]{:S(2)}, u32[]{:S(2)}) collective-permute-start(bf16[32,2048]{1,0:T(8,128)(2,1)S(1)} %get-tuple-element.283), channel_id=1, source_target_pairs={{0,114},{1,115},{2,112},{3,113},{4,118},{5,119},{6,116},{7,117},{8... | collective-permute-start | bytes 393224 | tf_op jit(solution)/shard_map/backward/ppermute | solution.py:57
  362.2 11.3 %collective-permute-start.111 = (bf16[32,2048]{1,0:T(8,128)(2,1)S(1)}, bf16[32,2048]{1,0:T(8,128)(2,1)S(1)}, u32[]{:S(2)}, u32[]{:S(2)}) collective-permute-start(bf16[32,2048]{1,0:T(8,128)(2,1)S(1)} %get-tuple-element.283), channel_id=1, source_target_pairs={{0,115},{1,112},{2,113},{3,114},{4,119},{5,116},{6,117},{7,118},{8... | collective-permute-start | bytes 393224 | tf_op jit(solution)/shard_map/backward/ppermute | solution.py:57
  375.5 11.3 %collective-permute-start.112 = (bf16[32,2560]{1,0:T(8,128)(2,1)S(1)}, bf16[32,2560]{1,0:T(8,128)(2,1)S(1)}, u32[]{:S(2)}, u32[]{:S(2)}) collective-permute-start(bf16[32,2560]{1,0:T(8,128)(2,1)S(1)} %get-tuple-element.287), channel_id=1, source_target_pairs={{0,112},{1,113},{2,114},{3,115},{4,116},{5,117},{6,118},{7,119},{8... | collective-permute-start | bytes 491528 | tf_op jit(solution)/shard_map/backward/ppermute | solution.py:57
  375.6 10.6 %collective-permute-start.114 = (bf16[32,2048]{1,0:T(8,128)(2,1)S(1)}, bf16[32,2048]{1,0:T(8,128)(2,1)S(1)}, u32[]{:S(2)}, u32[]{:S(2)}) collective-permute-start(bf16[32,2048]{1,0:T(8,128)(2,1)S(1)} %get-tuple-element.288), channel_id=1, source_target_pairs={{0,114},{1,115},{2,112},{3,113},{4,118},{5,119},{6,116},{7,117},{8... | collective-permute-start | bytes 393224 | tf_op jit(solution)/shard_map/backward/ppermute | solution.py:57
  375.7 11.1 %collective-permute-start.115 = (bf16[32,2048]{1,0:T(8,128)(2,1)S(1)}, bf16[32,2048]{1,0:T(8,128)(2,1)S(1)}, u32[]{:S(2)}, u32[]{:S(2)}) collective-permute-start(bf16[32,2048]{1,0:T(8,128)(2,1)S(1)} %get-tuple-element.288), channel_id=1, source_target_pairs={{0,115},{1,112},{2,113},{3,114},{4,119},{5,116},{6,117},{7,118},{8... | collective-permute-start | bytes 393224 | tf_op jit(solution)/shard_map/backward/ppermute | solution.py:57
  388.9 11.5 %collective-permute-start.116 = (bf16[32,2560]{1,0:T(8,128)(2,1)S(1)}, bf16[32,2560]{1,0:T(8,128)(2,1)S(1)}, u32[]{:S(2)}, u32[]{:S(2)}) collective-permute-start(bf16[32,2560]{1,0:T(8,128)(2,1)S(1)} %get-tuple-element.292), channel_id=1, source_target_pairs={{0,112},{1,113},{2,114},{3,115},{4,116},{5,117},{6,118},{7,119},{8... | collective-permute-start | bytes 491528 | tf_op jit(solution)/shard_map/backward/ppermute | solution.py:57
  389.0 11.4 %collective-permute-start.118 = (bf16[32,2048]{1,0:T(8,128)(2,1)S(1)}, bf16[32,2048]{1,0:T(8,128)(2,1)S(1)}, u32[]{:S(2)}, u32[]{:S(2)}) collective-permute-start(bf16[32,2048]{1,0:T(8,128)(2,1)S(1)} %get-tuple-element.293), channel_id=1, source_target_pairs={{0,114},{1,115},{2,112},{3,113},{4,118},{5,119},{6,116},{7,117},{8... | collective-permute-start | bytes 393224 | tf_op jit(solution)/shard_map/backward/ppermute | solution.py:57
  389.0 11.3 %collective-permute-start.119 = (bf16[32,2048]{1,0:T(8,128)(2,1)S(1)}, bf16[32,2048]{1,0:T(8,128)(2,1)S(1)}, u32[]{:S(2)}, u32[]{:S(2)}) collective-permute-start(bf16[32,2048]{1,0:T(8,128)(2,1)S(1)} %get-tuple-element.293), channel_id=1, source_target_pairs={{0,115},{1,112},{2,113},{3,114},{4,119},{5,116},{6,117},{7,118},{8... | collective-permute-start | bytes 393224 | tf_op jit(solution)/shard_map/backward/ppermute | solution.py:57
  402.4 11.3 %collective-permute-start.120 = (bf16[32,2560]{1,0:T(8,128)(2,1)S(1)}, bf16[32,2560]{1,0:T(8,128)(2,1)S(1)}, u32[]{:S(2)}, u32[]{:S(2)}) collective-permute-start(bf16[32,2560]{1,0:T(8,128)(2,1)S(1)} %get-tuple-element.297), channel_id=1, source_target_pairs={{0,112},{1,113},{2,114},{3,115},{4,116},{5,117},{6,118},{7,119},{8... | collective-permute-start | bytes 491528 | tf_op jit(solution)/shard_map/backward/ppermute | solution.py:57
  402.5 10.6 %collective-permute-start.122 = (bf16[32,2048]{1,0:T(8,128)(2,1)S(1)}, bf16[32,2048]{1,0:T(8,128)(2,1)S(1)}, u32[]{:S(2)}, u32[]{:S(2)}) collective-permute-start(bf16[32,2048]{1,0:T(8,128)(2,1)S(1)} %get-tuple-element.298), channel_id=1, source_target_pairs={{0,114},{1,115},{2,112},{3,113},{4,118},{5,119},{6,116},{7,117},{8... | collective-permute-start | bytes 393224 | tf_op jit(solution)/shard_map/backward/ppermute | solution.py:57
  402.6 11.1 %collective-permute-start.123 = (bf16[32,2048]{1,0:T(8,128)(2,1)S(1)}, bf16[32,2048]{1,0:T(8,128)(2,1)S(1)}, u32[]{:S(2)}, u32[]{:S(2)}) collective-permute-start(bf16[32,2048]{1,0:T(8,128)(2,1)S(1)} %get-tuple-element.298), channel_id=1, source_target_pairs={{0,115},{1,112},{2,113},{3,114},{4,119},{5,116},{6,117},{7,118},{8... | collective-permute-start | bytes 393224 | tf_op jit(solution)/shard_map/backward/ppermute | solution.py:57
  415.7 11.5 %collective-permute-start.124 = (bf16[32,2560]{1,0:T(8,128)(2,1)S(1)}, bf16[32,2560]{1,0:T(8,128)(2,1)S(1)}, u32[]{:S(2)}, u32[]{:S(2)}) collective-permute-start(bf16[32,2560]{1,0:T(8,128)(2,1)S(1)} %get-tuple-element.302), channel_id=1, source_target_pairs={{0,112},{1,113},{2,114},{3,115},{4,116},{5,117},{6,118},{7,119},{8... | collective-permute-start | bytes 491528 | tf_op jit(solution)/shard_map/backward/ppermute | solution.py:57
  415.8 11.4 %collective-permute-start.126 = (bf16[32,2048]{1,0:T(8,128)(2,1)S(1)}, bf16[32,2048]{1,0:T(8,128)(2,1)S(1)}, u32[]{:S(2)}, u32[]{:S(2)}) collective-permute-start(bf16[32,2048]{1,0:T(8,128)(2,1)S(1)} %get-tuple-element.303), channel_id=1, source_target_pairs={{0,114},{1,115},{2,112},{3,113},{4,118},{5,119},{6,116},{7,117},{8... | collective-permute-start | bytes 393224 | tf_op jit(solution)/shard_map/backward/ppermute | solution.py:57
  415.8 11.3 %collective-permute-start.127 = (bf16[32,2048]{1,0:T(8,128)(2,1)S(1)}, bf16[32,2048]{1,0:T(8,128)(2,1)S(1)}, u32[]{:S(2)}, u32[]{:S(2)}) collective-permute-start(bf16[32,2048]{1,0:T(8,128)(2,1)S(1)} %get-tuple-element.303), channel_id=1, source_target_pairs={{0,115},{1,112},{2,113},{3,114},{4,119},{5,116},{6,117},{7,118},{8... | collective-permute-start | bytes 393224 | tf_op jit(solution)/shard_map/backward/ppermute | solution.py:57
  (88 other events, 669.1 us)
